TPU v7x, 128 devices: a whole 4x4x4 slice. The times are simulated.
128 devices in a mesh: section: 8 (over y, core), dp: 16 (over z, x).
Axes of the slice: x: 4, y: 4, z: 4, core: 2. Of those that a mesh axis runs over, the one named last changes fastest.
Arguments:
- layer_input: bfloat16 [8, 6144, 8192], P('section', 'dp'), may hold values from -6 to 6
- value_grad: bfloat16 [8, 6144, 1024], P('section', 'dp'), may hold values from -6 to 6
- frozen_weight: bfloat16 [8, 8192, 1024], P('section', 'dp'), may hold values from -0.0625 to 0.0625
- adapter_down: bfloat16 [8, 32, 8192, 64], P('section', None, 'dp'), may hold values from -0.0625 to 0.0625
- adapter_up: bfloat16 [8, 32, 64, 1024], P('section'), may hold values from -0.75 to 0.75
- group_tenant: int32 [8, 48], P('section'), may hold values from 0 to 31
- slot_tenant: int32 [32], replicated, may hold values from 0 to 31, each once
Outputs:
- upstream: bfloat16 [8, 6144, 8192], P('section', 'dp')
- down_matrix_gradient: float32 [8, 32, 8192, 64], P('section', None, 'dp')
- up_grad: float32 [8, 32, 64, 1024], P('section', 'dp')
All inputs are finite; a program needn't handle non-finite values.
Results may differ from a plain program's by a relative error of at most 0.024.
Values may be sent and summed in bfloat16 or wider, within the bound.
No kernel may reach another device: no remote copies, remote signals or barrier semaphores. Data moves between devices by JAX's collectives and lax.ppermute only.
A program may use at most 128 MiB of HBM per device.

v0:
```python
import jax
import jax.numpy as jnp
from jax import lax
from jax.sharding import PartitionSpec as P

GROUP_ROWS = 128


adapter_scale = 2.0


def passed_along(block, axis, distance):
    devices = range(lax.axis_size(axis))
    route = [(i - distance, i) for i in devices if i - distance in devices]
    return lax.ppermute(block, axis, route)


def local(
    layer_input, value_grad, frozen_weight, adapter_down, adapter_up, group_tenant, slot_tenant
):
    single_float = jnp.float32
    brain_half_float = jnp.bfloat16
    rows_in = layer_input[0]
    cot_mine = value_grad[0]
    weight_slice = frozen_weight[0]
    down_slice = adapter_down[0]
    up_table = adapter_up[0]
    tenants = group_tenant[0]
    n_dp = lax.axis_size("dp")
    me_dp = lax.axis_index("dp")
    n_groups = tenants.shape[0]
    groups_dev = n_groups // n_dp
    n_tenants = down_slice.shape[0]
    width_slice = down_slice.shape[1]
    rank = down_slice.shape[2]
    kv_width = up_table.shape[2]
    cot_all = lax.all_gather(cot_mine, "dp", axis=0, tiled=True)
    rows_slice = lax.all_to_all(rows_in, "dp", split_axis=1, concat_axis=0, tiled=True)
    all_rows = cot_all.shape[0]
    cot_groups = cot_all.reshape(n_groups, GROUP_ROWS, kv_width)
    up_sel = up_table[tenants]
    selected_down = down_slice[tenants]
    low_rank_state = jnp.einsum(
        "gnk,grk->gnr", cot_groups, up_sel, preferred_element_type=single_float
    ).astype(brain_half_float)
    frozen_input_gradient = jnp.einsum(
        "nk,dk->nd", cot_all, weight_slice, preferred_element_type=single_float
    )
    adapter_input_gradient = jnp.einsum(
        "lfk,lok->lfo", low_rank_state, selected_down, preferred_element_type=single_float
    ).reshape(all_rows, width_slice)
    gradient_rows_piece = (frozen_input_gradient + adapter_scale * adapter_input_gradient).astype(
        brain_half_float
    )
    grad_rows = lax.all_to_all(gradient_rows_piece, "dp", split_axis=0, concat_axis=1, tiled=True)
    handed = passed_along(grad_rows, "section", -1)
    in_groups = rows_slice.reshape(n_groups, GROUP_ROWS, width_slice)
    tenant_ids = jnp.arange(n_tenants, dtype=jnp.int32)
    tenant_one_hot = (tenants[None, :] == tenant_ids[:, None]).astype(single_float)
    group_wise = jnp.einsum(
        "gnd,gnr->gdr", in_groups, low_rank_state, preferred_element_type=single_float
    )
    down_matrix_gradient = jnp.einsum(
        "pc,cxf->pxf", tenant_one_hot, group_wise, precision=lax.Precision.HIGHEST
    ) * (adapter_scale / GROUP_ROWS)
    proj_part = jnp.einsum(
        "gnd,gdr->gnr", in_groups, selected_down, preferred_element_type=single_float
    )
    proj_mine = (
        lax.psum_scatter(
            proj_part.reshape(all_rows, rank).astype(jnp.bfloat16),
            "dp",
            scatter_dimension=0,
            tiled=True,
        )
        .astype(jnp.float32)
        .astype(brain_half_float)
    )
    mine_tenants = lax.dynamic_slice_in_dim(tenants, me_dp * groups_dev, groups_dev)
    local_group_list = adapter_scale * jnp.einsum(
        "lma,lmb->lab",
        proj_mine.reshape(groups_dev, GROUP_ROWS, rank),
        cot_mine.reshape(groups_dev, GROUP_ROWS, kv_width),
        preferred_element_type=single_float,
    )
    mine_hot = (mine_tenants[None, :] == tenant_ids[:, None]).astype(single_float)
    terms = jnp.einsum(
        "tc,crk->trk", mine_hot, local_group_list, precision=lax.Precision.HIGHEST
    ).astype(brain_half_float)
    terms = lax.optimization_barrier(terms).astype(single_float)[slot_tenant]
    up_grad = (
        lax.psum_scatter(terms.astype(jnp.bfloat16), "dp", scatter_dimension=0, tiled=True).astype(
            jnp.float32
        )
        / GROUP_ROWS
    )
    return (handed[None], down_matrix_gradient[None], up_grad[None])


def solution(mesh):
    placed = (
        P("section", "dp", None),
        P("section", "dp", None),
        P("section", "dp", None),
        P("section", None, "dp", None),
        P("section", None, None, None),
        P("section", None),
        P(),
    )
    return jax.shard_map(
        local,
        mesh=mesh,
        in_specs=placed,
        out_specs=(
            P("section", "dp", None),
            P("section", None, "dp", None),
            P("section", "dp", None, None),
        ),
        check_vma=False,
    )
```

profile of v0, /device:TPU:24, one launch (start us, length us, event | category | flops | bytes accessed | tf_op | source)
XLA Modules:
  0.0 479.6 jit_solution(2396006301370551718)
XLA Ops:
  7.2 0.0 all-gather.3.cloned.1.call-start
  7.2 0.7 all-gather.3.cloned.1.call-update
  7.9 5.7 %copy.42 = bf16[48,8,16,512]{3,2,1,0:T(8,128)(2,1)S(1)} copy(bf16[48,8,16,512]{3,1,2,0:T(8,128)(2,1)} %bitcast.65) | data formatting | bytes 12582912
  13.6 6.4 %copy.28 = bf16[384,16,512]{2,0,1:T(8,128)(2,1)} copy(bf16[384,16,512]{2,1,0:T(8,128)(2,1)S(1)} %bitcast.62) | data formatting | bytes 12582912 | tf_op jit(solution)/shard_map/all_to_all | solution.py:38
  20.0 8.1 %all-to-all-start.1 = ((bf16[384,16,512]{2,0,1:T(8,128)(2,1)}), bf16[384,16,512]{2,0,1:T(8,128)(2,1)}, u32[]{:S(2)}, u32[]{:S(2)}) async-start(bf16[384,16,512]{2,0,1:T(8,128)(2,1)} %copy.28), calls=%async_computation.1 | async-start | bytes 12582912 | tf_op jit(solution)/shard_map/all_to_all | solution.py:38
  28.1 7.3 %gather_fusion = bf16[48,64,1024]{2,1,0:T(8,128)(2,1)} fusion(bf16[32,64,1024]{2,1,0:T(8,128)(2,1)} %bitcast.64, s32[1024]{0:T(1024)S(1)} %pad_clamp_fusion.1), kind=kCustom, calls=%fused_computation | custom fusion | bytes 12583104 | tf_op jit(solution)/shard_map/gather | solution.py:41
  35.4 2.5 gather_fusion.1
  37.9 139.5 %all-gather.3.cloned.1.call-done = bf16[1,6144,1024]{2,1,0:T(8,128)(2,1)} async-done(((bf16[1,384,1024]{2,1,0:T(8,128)(2,1)}), bf16[1,6144,1024]{2,1,0:T(8,128)(2,1)}) %all-gather.3.cloned.1.call-update) | async-done | bytes 12582928 | tf_op jit(solution)/shard_map/all_gather | solution.py:37
  177.4 11.8 %convolution_convert_fusion.2 = bf16[48,64,128]{2,1,0:T(8,128)(2,1)} fusion(bf16[48,64,1024]{2,1,0:T(8,128)(2,1)} %gather_fusion, bf16[48,128,1024]{2,1,0:T(8,128)(2,1)} %bitcast.63), kind=kOutput, calls=%fused_computation.14 | convolution fusion | flops 805699584 | bytes 19660800 | tf_op jit(solution)/shard_map/gnk,grk->gnr/dot_general | solution.py:43
  189.2 7.5 %broadcast_multiply_fusion = f32[48,128,512]{2,1,0:T(8,128)} fusion(bf16[48,64,128]{2,1,0:T(8,128)(2,1)} %convolution_convert_fusion.2, bf16[48,512,64]{1,2,0:T(8,128)(2,1)S(1)} %copy-done.2), kind=kOutput, calls=%fused_computation.9 | convolution fusion | flops 405798912 | bytes 16515072 | tf_op jit(solution)/shard_map/lfk,lok->lfo/dot_general | solution.py:49
  196.8 15.0 %fusion = bf16[6144,512]{1,0:T(8,128)(2,1)} fusion(f32[48,128,512]{2,1,0:T(8,128)} %broadcast_multiply_fusion, bf16[1,6144,1024]{2,1,0:T(8,128)(2,1)} %all-gather.3.cloned.1.call-done, bf16[1,512,1024]{2,1,0:T(8,128)(2,1)S(1)} %copy-done.5), kind=kOutput, calls=%fused_computation.4 | convolution fusion | flops 6448742400 | bytes 32505856 | tf_op jit(solution)/shard_map/nk,dk->nd/dot_general | solution.py:46
  211.8 7.9 %all-to-all-start = ((bf16[16,384,512]{2,1,0:T(8,128)(2,1)}), bf16[16,384,512]{2,1,0:T(8,128)(2,1)}, u32[]{:S(2)}, u32[]{:S(2)}) async-start(bf16[16,384,512]{2,1,0:T(8,128)(2,1)} %bitcast.66), calls=%async_computation | async-start | bytes 12582912 | tf_op jit(solution)/shard_map/all_to_all | solution.py:55
  219.7 0.0 reduce-scatter.7.cloned.1.call-start
  219.8 5.9 %fusion.9 = bf16[48,128,64]{1,2,0:T(8,128)(2,1)} fusion(bf16[48,512,64]{1,2,0:T(8,128)(2,1)S(1)} %copy-done.2, bf16[48,128,512]{2,1,0:T(8,128)(2,1)} %bitcast.14), kind=kOutput, calls=%fused_computation.15 | convolution fusion | flops 403046400 | bytes 10223616 | tf_op jit(solution)/shard_map/gnd,gdr->gnr/dot_general | solution.py:66
  225.7 2.4 copy.37
  228.1 0.0 reduce-scatter.7.cloned.1.call-update
  228.2 0.3 reduce-scatter.5.cloned.1.call-start
  228.4 0.1 dynamic-slice_bitcast_fusion
  228.5 129.7 %reduce-scatter.7.cloned.1.call-done = bf16[384,64]{1,0:T(8,128)(2,1)} async-done(((bf16[6144,64]{1,0:T(8,128)(2,1)}), bf16[384,64]{1,0:T(8,128)(2,1)}) %reduce-scatter.7.cloned.1.call-update) | async-done | bytes 49168
  358.2 1.5 convolution_multiply_fusion
  359.7 4.0 convolution_convert_fusion
  363.7 4.3 copy.33
  368.1 5.0 %gather_fusion.2 = bf16[32,64,1024]{2,1,0:T(8,128)(2,1)} fusion(bf16[32,64,1024]{2,1,0:T(8,128)(2,1)} %copy.33, s32[1024]{0:T(1024)S(1)} %pad_clamp_fusion), kind=kCustom, calls=%fused_computation.2 | custom fusion | bytes 8388736 | tf_op jit(solution)/shard_map/gather | solution.py:90
  373.1 0.0 reduce-scatter.5.cloned.1.call-update
  373.1 6.5 %copy.41 = bf16[16,48,8,512]{3,2,0,1:T(8,128)(2,1)} copy(bf16[16,48,8,512]{3,2,1,0:T(8,128)(2,1)} %bitcast.26) | data formatting | bytes 12582912 | tf_op jit(solution)/shard_map/all_to_all | solution.py:55
  379.6 1.9 collective-permute-start
  381.5 68.7 %reduce-scatter.5.cloned.1.call-done = bf16[2,64,1024]{2,1,0:T(8,128)(2,1)} async-done(((bf16[32,64,1024]{2,1,0:T(8,128)(2,1)}), bf16[2,64,1024]{2,1,0:T(8,128)(2,1)}) %reduce-scatter.5.cloned.1.call-update) | async-done | bytes 262160 | tf_op jit(solution)/shard_map/reduce_scatter | solution.py:92
  450.2 1.8 multiply_bitcast_fusion.1
  452.0 3.8 convolution_bitcast_fusion
  455.8 6.5 %multiply_bitcast_fusion = f32[1,32,512,64]{2,1,3,0:T(8,128)S(1)} fusion(f32[48,512,64]{1,2,0:T(8,128)S(1)} %convolution_bitcast_fusion, s32[48]{0:T(128)S(1)} %bitcast.70), kind=kOutput, calls=%fused_computation.10 | convolution fusion | flops 605029888 | bytes 10485952 | tf_op jit(solution)/shard_map/pc,cxf->pxf/dot_general | solution.py:63
  462.3 4.4 copy.34
  466.7 6.3 %copy.50 = bf16[1,384,8192]{2,1,0:T(8,128)(2,1)} copy(bf16[1,384,8192]{2,1,0:T(8,128)(2,1)} %bitcast.10) | data formatting | bytes 12582912
  (21 shorter events, 0.1 us)
Async XLA Ops:
  7.2 28.2 %copy-start = (bf16[1,32,512,64]{2,3,1,0:T(8,128)(2,1)S(1)}, bf16[1,32,512,64]{2,3,1,0:T(8,128)(2,1)}, u32[]{:S(2)}) copy-start(bf16[1,32,512,64]{2,3,1,0:T(8,128)(2,1)} %param.10) | copy-start | bytes 6291460
  7.2 170.2 %all-gather.3.cloned.1.call-start = ((), (), s32[]{:S(2)}) async-start(), calls=%async_computation.5 | async-start | bytes 13369344 | tf_op jit(solution)/shard_map/all_gather | solution.py:37
  20.0 8.1 %copy-start.4 = (s32[1,48]{1,0:T(1,128)S(1)}, s32[1,48]{1,0:T(1,128)}, u32[]{:S(2)}) copy-start(s32[1,48]{1,0:T(1,128)} %param.12) | copy-start | bytes 580
  20.0 191.8 %all-to-all-start.1 = ((bf16[384,16,512]{2,0,1:T(8,128)(2,1)}), bf16[384,16,512]{2,0,1:T(8,128)(2,1)}, u32[]{:S(2)}, u32[]{:S(2)}) async-start(bf16[384,16,512]{2,0,1:T(8,128)(2,1)} %copy.28), calls=%async_computation.1 | async-start | bytes 12582912 | tf_op jit(solution)/shard_map/all_to_all | solution.py:38
  177.4 11.8 %copy-start.2 = (bf16[48,512,64]{1,2,0:T(8,128)(2,1)S(1)}, bf16[48,512,64]{1,2,0:T(8,128)(2,1)}, u32[]{:S(2)}) copy-start(bf16[48,512,64]{1,2,0:T(8,128)(2,1)} %gather_fusion.1) | copy-start | bytes 9437188
  189.2 7.5 %copy-start.5 = (bf16[1,512,1024]{2,1,0:T(8,128)(2,1)S(1)}, bf16[1,512,1024]{2,1,0:T(8,128)(2,1)}, u32[]{:S(2)}) copy-start(bf16[1,512,1024]{2,1,0:T(8,128)(2,1)} %param.9) | copy-start | bytes 3145732
  211.8 161.3 %all-to-all-start = ((bf16[16,384,512]{2,1,0:T(8,128)(2,1)}), bf16[16,384,512]{2,1,0:T(8,128)(2,1)}, u32[]{:S(2)}, u32[]{:S(2)}) async-start(bf16[16,384,512]{2,1,0:T(8,128)(2,1)} %bitcast.66), calls=%async_computation | async-start | bytes 12582912 | tf_op jit(solution)/shard_map/all_to_all | solution.py:55
  219.7 138.5 %reduce-scatter.7.cloned.1.call-start = ((), (), s32[]{:S(2)}) async-start(), calls=%async_computation.6 | async-start | bytes 1671168
  219.8 8.8 %copy-start.6 = (s32[32]{0:T(128)S(1)}, s32[32]{0:T(128)}, u32[]{:S(2)}) copy-start(s32[32]{0:T(128)} %param.13) | copy-start | bytes 388
  228.2 222.1 %reduce-scatter.5.cloned.1.call-start = ((), (), s32[]{:S(2)}) async-start(), calls=%async_computation.4 | async-start | bytes 4456448 | tf_op jit(solution)/shard_map/reduce_scatter | solution.py:92
  373.1 78.9 %copy-start.3 = (bf16[48,64,128]{2,1,0:T(8,128)(2,1)S(1)}, bf16[48,64,128]{2,1,0:T(8,128)(2,1)}, u32[]{:S(2)}) copy-start(bf16[48,64,128]{2,1,0:T(8,128)(2,1)} %convolution_convert_fusion.2) | copy-start | bytes 2359300
  379.6 87.1 %collective-permute-start = (bf16[384,8192]{1,0:T(8,128)(2,1)}, bf16[384,8192]{1,0:T(8,128)(2,1)}, u32[]{:S(2)}, u32[]{:S(2)}) collective-permute-start(bf16[384,8192]{1,0:T(8,128)(2,1)} %bitcast.27), channel_id=1, source_target_pairs={{16,0},{32,16},{48,32},{64,48},{80,64},{96,80},{112,96},{17,1},{33... | collective-permute-start | bytes 18874376 | tf_op jit(solution)/shard_map/ppermute | solution.py:15
  466.7 6.3 %copy-start.1 = (bf16[1,32,512,64]{2,3,1,0:T(8,128)(2,1)S(1)}, bf16[1,32,512,64]{2,3,1,0:T(8,128)(2,1)}, u32[]{:S(2)}) copy-start(bf16[1,32,512,64]{2,3,1,0:T(8,128)(2,1)} %param.10) | copy-start | bytes 6291460
Sparse Core Ops, SparseCore 0:
  10.2 167.1 all-gather.2
  228.3 129.9 reduce-scatter.6
  373.2 76.9 reduce-scatter.4
where the time goes:
time: 480 us
  waiting for transfers between devices  339 us (71%)
  matrix products  56 us (12%)
  local copies, waits for them, and re-layouts  51.1 us (11%)
  starting transfers between devices  18.2 us (4%)
  between operations  13.9 us (3%)
    all_gather x1, waiting for transfers between devices, local(): cot_all = lax.all_gather(cot_mine, 'dp', axis=0, tiled=True)  139 us
    unnamed x4, waiting for transfers between devices  130 us
    reduce_scatter x1, waiting for transfers between devices, local(): lax.psum_scatter(terms.astype(jnp.bfloat16), 'dp', scatter_dimension=0, t...  68.7 us
    unnamed x18, local copies, waits for them, and re-layouts  19 us
    dot_general x1, matrix products, local(): jnp.einsum('nk,dk->nd', cot_all, weight_slice, preferred_element_type=sin...  15 us
    dot_general x1, matrix products, local(): jnp.einsum('gnk,grk->gnr', cot_groups, up_sel, preferred_element_type=sin...  11.8 us
  transfers between devices with their start and end apart: 6, of which 3 were waited for; matrix products, arithmetic and copies ran while one was open for 21% of the time, Pallas kernels for 0%

commit v1 on v0

v1 whole, which is shorter than its diff:
```python
import jax
import jax.numpy as jnp
from jax import lax
from jax.experimental import pallas as pl
from jax.experimental.pallas import tpu as pltpu
from jax.sharding import PartitionSpec as P

GROUP_ROWS = 128
ADAPTER_SCALE = 2.0
RING = 4

F32 = jnp.float32
BF16 = jnp.bfloat16
NT = (((1,), (1,)), ((), ()))
TN = (((0,), (0,)), ((), ()))


def dot(a, b, dims):
    return lax.dot_general(a, b, dims, preferred_element_type=F32)


def cost(flops, nbytes):
    return pl.CostEstimate(flops=int(flops), bytes_accessed=int(nbytes), transcendentals=0)


def to_previous_section(block):
    n = lax.axis_size("section")
    return lax.ppermute(block, "section", [(i, i - 1) for i in range(1, n)])


def along_x(distance):
    return [
        (RING * z + x, RING * z + (x + distance) % RING) for z in range(RING) for x in range(RING)
    ]


def along_z(distance):
    return [
        (RING * z + x, RING * ((z + distance) % RING) + x) for z in range(RING) for x in range(RING)
    ]


def exchange(blocks):
    return lax.all_to_all(blocks, "dp", split_axis=0, concat_axis=0, tiled=True)


def gather_ring(part, first, second):
    n = part.shape[0]
    up = lax.ppermute(part, "dp", first(1))
    down = lax.ppermute(part, "dp", first(-1))
    far_a = lax.ppermute(up[: n // 2], "dp", first(1))
    far_b = lax.ppermute(down[n // 2 :], "dp", first(-1))
    line = jnp.concatenate([part, up, down, far_a, far_b], axis=0)
    m = line.shape[0]
    plane_up = lax.ppermute(line, "dp", second(1))
    plane_down = lax.ppermute(line, "dp", second(-1))
    plane_far_a = lax.ppermute(plane_up[: m // 2], "dp", second(1))
    plane_far_b = lax.ppermute(plane_down[m // 2 :], "dp", second(-1))
    return line, plane_up, plane_down, plane_far_a, plane_far_b


def group_terms(x, low_t):
    rows, width = x.shape
    groups, rank, _ = low_t.shape
    n = lax.axis_size("dp")
    cols = width // n

    def body(x_ref, low_ref, o_ref):
        for g in range(groups):
            o_ref[0, g] = jnp.dot(
                low_ref[g],
                x_ref[g * GROUP_ROWS : (g + 1) * GROUP_ROWS, :],
                preferred_element_type=F32,
            ).astype(BF16)

    return pl.pallas_call(
        body,
        grid=(n,),
        in_specs=[
            pl.BlockSpec((rows, cols), lambda d: (0, d)),
            pl.BlockSpec((groups, rank, GROUP_ROWS), lambda d: (0, 0, 0)),
        ],
        out_specs=pl.BlockSpec((1, groups, rank, cols), lambda d: (d, 0, 0, 0)),
        out_shape=jax.ShapeDtypeStruct((n, groups, rank, cols), BF16),
        cost_estimate=cost(2 * rows * width * rank, 2 * (rows * width + groups * rank * width)),
    )(x, low_t)


def project(x, down):
    rows, width = x.shape
    n, groups, rank, cols = down.shape

    def body(x_ref, a_ref, o_ref, acc):
        d = pl.program_id(0)

        @pl.when(d == 0)
        def _():
            acc[...] = jnp.zeros_like(acc)

        for g in range(groups):
            span = slice(g * GROUP_ROWS, (g + 1) * GROUP_ROWS)
            acc[:, span] += dot(a_ref[0, g], x_ref[span, :], NT)

        @pl.when(d == n - 1)
        def _():
            o_ref[...] = acc[...].astype(BF16)

    return pl.pallas_call(
        body,
        grid=(n,),
        in_specs=[
            pl.BlockSpec((rows, cols), lambda d: (0, d)),
            pl.BlockSpec((1, groups, rank, cols), lambda d: (d, 0, 0, 0)),
        ],
        out_specs=pl.BlockSpec((rank, rows), lambda d: (0, 0)),
        out_shape=jax.ShapeDtypeStruct((rank, rows), BF16),
        scratch_shapes=[pltpu.VMEM((rank, rows), F32)],
        cost_estimate=cost(2 * rows * width * rank, 2 * (rows * width + groups * rank * width)),
    )(x, down)


def sum_by_tenant(parts, tenants, n_tenants):
    n_groups, rank, cols = parts.shape
    steps = 4
    r = rank // steps
    scale = ADAPTER_SCALE / GROUP_ROWS

    def body(t_ref, p_ref, o_ref):
        o_ref[...] = jnp.zeros_like(o_ref)

        @pl.loop(0, n_groups)
        def _(g):
            t = t_ref[g]
            o_ref[t] += p_ref[g].astype(F32) * scale

    return pl.pallas_call(
        body,
        grid_spec=pltpu.PrefetchScalarGridSpec(
            num_scalar_prefetch=1,
            grid=(steps,),
            in_specs=[pl.BlockSpec((n_groups, r, cols), lambda i, t: (0, i, 0))],
            out_specs=pl.BlockSpec((n_tenants, r, cols), lambda i, t: (0, i, 0)),
        ),
        out_shape=jax.ShapeDtypeStruct((n_tenants, rank, cols), F32),
        cost_estimate=cost(
            n_groups * rank * cols, 2 * n_groups * rank * cols + 4 * n_tenants * rank * cols
        ),
    )(tenants, parts)


def up_terms(v_t, proj_t, tenants, slots):
    n, kv, rows = v_t.shape
    rank = proj_t.shape[1]
    groups = rows // GROUP_ROWS
    n_tenants = slots.shape[0]
    per = n_tenants // n

    def body(t_ref, s_ref, v_ref, p_ref, o_ref, acc):
        acc[...] = jnp.zeros_like(acc)

        @pl.loop(0, n)
        def _(d):
            for g in range(groups):
                span = slice(g * GROUP_ROWS, (g + 1) * GROUP_ROWS)
                t = t_ref[d * groups + g]
                acc[t] += dot(v_ref[d, :, span], p_ref[d, :, span], NT)

        for o in range(n):
            for k in range(per):
                o_ref[o, :, k * rank : (k + 1) * rank] = acc[s_ref[o * per + k]].astype(BF16)

    return pl.pallas_call(
        body,
        in_specs=[
            pl.BlockSpec(memory_space=pltpu.SMEM),
            pl.BlockSpec(memory_space=pltpu.SMEM),
            pl.BlockSpec(memory_space=pltpu.VMEM),
            pl.BlockSpec(memory_space=pltpu.VMEM),
        ],
        out_specs=pl.BlockSpec(memory_space=pltpu.VMEM),
        out_shape=jax.ShapeDtypeStruct((n, kv, per * rank), BF16),
        scratch_shapes=[pltpu.VMEM((n_tenants, kv, rank), F32)],
        cost_estimate=cost(2 * n * rows * kv * rank, 4 * n * rows * kv),
    )(tenants, slots, v_t, proj_t)


def gradient_columns(out, blocks, v, weight, low_t, down):
    rows, kv = v.shape
    n, groups, rank, cols = down.shape
    half = cols // 2
    count = weight.shape[0] // half

    def body(b_ref, v_ref, w_ref, low_ref, a_ref, *rest):
        o_ref = rest[-1]
        frozen = dot(v_ref[...], w_ref[...], NT)
        for g in range(groups):
            span = slice(g * GROUP_ROWS, (g + 1) * GROUP_ROWS)
            adapter = dot(low_ref[g], a_ref[0, g], TN)
            o_ref[span, :] = (frozen[span] + ADAPTER_SCALE * adapter).astype(BF16)

    in_specs = [
        pl.BlockSpec((rows, kv), lambda i, b: (0, 0)),
        pl.BlockSpec((half, kv), lambda i, b: (i, 0)),
        pl.BlockSpec((groups, rank, GROUP_ROWS), lambda i, b: (0, 0, 0)),
        pl.BlockSpec((1, groups, rank, half), lambda i, b: (b[i] // 2, 0, 0, b[i] % 2)),
    ]
    args = [blocks, v, weight, low_t, down]
    aliases = {}
    if out is not None:
        in_specs.append(pl.BlockSpec(memory_space=pl.ANY))
        aliases = {len(args): 0}
        args.append(out)
    width = n * cols
    return pl.pallas_call(
        body,
        grid_spec=pltpu.PrefetchScalarGridSpec(
            num_scalar_prefetch=1,
            grid=(count,),
            in_specs=in_specs,
            out_specs=pl.BlockSpec((rows, half), lambda i, b: (0, b[i])),
        ),
        out_shape=jax.ShapeDtypeStruct((rows, width), BF16),
        input_output_aliases=aliases,
        cost_estimate=cost(
            2 * rows * (kv + rank) * half * count, 2 * (rows * kv + count * half * (kv + rows))
        ),
    )(*args)


def local(
    layer_input, value_grad, frozen_weight, adapter_down, adapter_up, group_tenant, slot_tenant
):
    x = layer_input[0]
    v = value_grad[0]
    w = frozen_weight[0]
    down = jnp.swapaxes(adapter_down[0], 1, 2)
    up = adapter_up[0]
    tenants = group_tenant[0]
    n = lax.axis_size("dp")
    me = lax.axis_index("dp")
    rows, kv = v.shape
    n_tenants, rank, cols = down.shape
    groups = rows // GROUP_ROWS
    my_tenants = lax.dynamic_slice_in_dim(tenants, me * groups, groups)

    w_next = to_previous_section(w)
    v_next = to_previous_section(v)

    down_mine = exchange(down[tenants].reshape(n, groups, rank, cols))
    v_t_all = exchange(v.T.reshape(n, kv // n, rows))

    low_t = jnp.einsum(
        "grk,gnk->grn",
        up[my_tenants],
        v.reshape(groups, GROUP_ROWS, kv),
        preferred_element_type=F32,
    ).astype(BF16)
    low_next = to_previous_section(low_t)
    terms = exchange(group_terms(x, low_t))

    half = cols // 2
    ring_a = gather_ring(w_next[:half], along_x, along_z)
    ring_b = gather_ring(w_next[half:], along_z, along_x)

    proj_t = project(x, down_mine)
    down_next = to_previous_section(down_mine)
    proj_all = lax.all_gather(proj_t, "dp", axis=0)
    up_sent = exchange(up_terms(v_t_all, proj_all, tenants, slot_tenant))
    up_grad = (
        up_sent.reshape(kv, -1).T.reshape(-1, rank, kv).astype(F32) * (ADAPTER_SCALE / GROUP_ROWS)
    )

    mz, mx = me // RING, me % RING
    order = (0, -1, 1, 2)

    def ids(first, second, part):
        out = []
        for s in second:
            for f in first:
                dz, dx = (s, f) if part == 0 else (f, s)
                d = RING * ((mz + dz) % RING) + (mx + dx) % RING
                out.append(2 * d + part)
        return jnp.stack(out).astype(jnp.int32)

    out = None
    for piece, (first, second) in enumerate(
        ((order, (0,)), (order, (-1,)), (order, (1,)), (order[:2], (2,)), (order[2:], (2,)))
    ):
        for part, ring in enumerate((ring_a, ring_b)):
            out = gradient_columns(
                out, ids(first, second, part), v_next, ring[piece], low_next, down_next
            )

    down_grad = sum_by_tenant(terms.reshape(n * groups, rank, cols), tenants, n_tenants)
    return (out[None], jnp.swapaxes(down_grad, 1, 2)[None], up_grad[None])


def solution(mesh):
    placed = (
        P("section", "dp", None),
        P("section", "dp", None),
        P("section", "dp", None),
        P("section", None, "dp", None),
        P("section", None, None, None),
        P("section", None),
        P(),
    )
    return jax.shard_map(
        local,
        mesh=mesh,
        in_specs=placed,
        out_specs=(
            P("section", "dp", None),
            P("section", None, "dp", None),
            P("section", "dp", None, None),
        ),
        check_vma=False,
    )
```

time: 480 us -> 331 us (0.69)
  waiting for transfers between devices: 339 us -> 111 us
  Pallas kernels: 0 us -> 81.6 us
  matrix products: 56 us -> 2.14 us
  starting transfers between devices: 18.2 us -> 56.2 us
  blocking collectives: 0 us -> 25.8 us
  between operations: 13.9 us -> 0.83 us
  local copies, waits for them, and re-layouts: 51.1 us -> 44.5 us
  other arithmetic: 1.82 us -> 6.99 us
    all_gather x1 -> x0, waiting for transfers between devices: 139 us -> none  [local(): cot_all = lax.all_gather(cot_mine, 'dp', axis=0, tiled=True)]
    unnamed x4 -> x0, waiting for transfers between devices: 130 us -> none
    ppermute x1 -> x20, waiting for transfers between devices: 0.01 us -> 98.6 us  [the longest x2 61.3 us: gather_ring(): plane_up = lax.ppermute(line, 'dp', second(1))]
    pallas_call x0 -> x14, Pallas kernels: none -> 81.6 us  [the longest x10 47.4 us: gradient_columns(): pl.pallas_call(body, grid_spec=pltpu.PrefetchScalarGridSpec(num_scalar_pr...]
    reduce_scatter x1 -> x0, waiting for transfers between devices: 68.7 us -> none  [local(): lax.psum_scatter(terms.astype(jnp.bfloat16), 'dp', scatter_dimension=0, t...]
    dot_general x8 -> x1, matrix products: 56 us -> 2.14 us  [local(): jnp.einsum('grk,gnk->grn', up[my_tenants], v.reshape(groups, GROUP_ROWS,...]
    ppermute x1 -> x20, starting transfers between devices: 1.91 us -> 34.8 us  [the longest x4 8.45 us: to_previous_section(): return lax.ppermute(block, 'section', [(i, i - 1) for i in range(1, n)])]
    all_gather x0 -> x1, blocking collectives: none -> 25.8 us  [local(): proj_all = lax.all_gather(proj_t, 'dp', axis=0)]
  transfers between devices with their start and end apart: 6 -> 24, of which waited for: 3 -> 4; matrix products, arithmetic and copies ran while one was open for 21% -> 14% of each run, Pallas kernels for 0% -> 24%
where the time goes in v1:
time: 331 us; the launch traced here: 329 us
  waiting for transfers between devices  111 us (34%)
  Pallas kernels  81.6 us (25%)
  starting transfers between devices  56.2 us (17%)
  local copies, waits for them, and re-layouts  44.5 us (13%)
  blocking collectives  25.8 us (8%)
  other arithmetic  6.99 us (2%)
    ppermute x2, waiting for transfers between devices, gather_ring(): plane_up = lax.ppermute(line, 'dp', second(1))  61.3 us
    pallas_call x10, Pallas kernels, gradient_columns(): pl.pallas_call(body, grid_spec=pltpu.PrefetchScalarGridSpec(num_scalar_pr...  47.4 us
    all_gather x1, blocking collectives, local(): proj_all = lax.all_gather(proj_t, 'dp', axis=0)  25.8 us
    ppermute x2, waiting for transfers between devices, gather_ring(): up = lax.ppermute(part, 'dp', first(1))  24.6 us
    all_to_all x4, starting transfers between devices, exchange(): return lax.all_to_all(blocks, 'dp', split_axis=0, concat_axis=0, tiled=True)  21.4 us
    unnamed x22, local copies, waits for them, and re-layouts  14.1 us
    ppermute x4, waiting for transfers between devices, to_previous_section(): return lax.ppermute(block, 'section', [(i, i - 1) for i in range(1, n)])  12.6 us
    all_to_all x4, waiting for transfers between devices, exchange(): return lax.all_to_all(blocks, 'dp', split_axis=0, concat_axis=0, tiled=True)  11.9 us
  transfers between devices with their start and end apart: 24, of which 4 were waited for; matrix products, arithmetic and copies ran while one was open for 14% of the time, Pallas kernels for 24%

profile of v1, /device:TPU:24, one launch (start us, length us, event | category | flops | bytes accessed | tf_op | source)
XLA Modules:
  0.0 328.6 jit_solution(4280041738995542392)
XLA Ops:
  0.7 2.4 copy.19
  3.1 7.9 %all-to-all-start.2 = ((bf16[16,64,384]{2,1,0:T(8,128)(2,1)}), bf16[16,64,384]{2,1,0:T(8,128)(2,1)S(1)}, u32[]{:S(2)}, u32[]{:S(2)}) async-start(bf16[16,64,384]{2,1,0:T(8,128)(2,1)} %bitcast.74), calls=%async_computation.2 | async-start | bytes 1572864 | tf_op jit(solution)/shard_map/all_to_all | solution.py:44
  11.0 2.5 gather_fusion.1
  13.6 11.9 %all-to-all-done.2.v_ref = bf16[16,64,384]{2,1,0:T(8,128)(2,1)S(1)} async-done(((bf16[16,64,384]{2,1,0:T(8,128)(2,1)}), bf16[16,64,384]{2,1,0:T(8,128)(2,1)S(1)}, u32[]{:S(2)}, u32[]{:S(2)}) %all-to-all-start.2) | async-done | bytes 786464 | tf_op jit(solution)/shard_map/all_to_all | solution.py:44
  26.4 3.7 %all-to-all-start = ((bf16[16,3,64,512]{3,2,1,0:T(8,128)(2,1)}), bf16[16,3,64,512]{3,2,1,0:T(8,128)(2,1)S(1)}, u32[]{:S(2)}, u32[]{:S(2)}) async-start(bf16[16,3,64,512]{3,2,1,0:T(8,128)(2,1)} %bitcast.69), calls=%async_computation | async-start | bytes 6291456 | tf_op jit(solution)/shard_map/all_to_all | solution.py:44
  32.1 12.6 %collective-permute-done.1 = bf16[512,1024]{1,0:T(8,128)(2,1)S(1)} collective-permute-done((bf16[512,1024]{1,0:T(8,128)(2,1)}, bf16[512,1024]{1,0:T(8,128)(2,1)S(1)}, u32[]{:S(2)}, u32[]{:S(2)}) %collective-permute-start.1) | collective-permute-done | bytes 1048608 | tf_op jit(solution)/shard_map/ppermute | solution.py:28
  52.7 2.8 gather_fusion
  57.6 24.6 %collective-permute-done.10 = bf16[256,1024]{1,0:T(8,128)(2,1)} collective-permute-done((bf16[256,1024]{1,0:T(8,128)(2,1)}, bf16[256,1024]{1,0:T(8,128)(2,1)}, u32[]{:S(2)}, u32[]{:S(2)}) %collective-permute-start.10) | collective-permute-done | bytes 524320 | tf_op jit(solution)/shard_map/ppermute | solution.py:49
  83.9 11.6 %shard_map.104 = bf16[16,3,64,512]{3,2,1,0:T(8,128)(2,1)} custom-call(bf16[384,8192]{1,0:T(8,128)(2,1)} %bitcast.67, bf16[3,64,128]{2,1,0:T(8,128)(2,1)} %convolution_convert_fusion.low_ref), custom_call_target="tpu_custom_call" | custom-call | flops 402653184 | bytes 9437184 | tf_op jit(solution)/shard_map/pallas_call | solution.py:76
  97.2 3.2 collective-permute-start.13
  103.8 3.2 collective-permute-start.5
  112.5 4.5 %all-to-all-start.1 = ((bf16[16,3,64,512]{3,2,1,0:T(8,128)(2,1)}), bf16[16,3,64,512]{3,2,1,0:T(8,128)(2,1)}, u32[]{:S(2)}, u32[]{:S(2)}) async-start(bf16[16,3,64,512]{3,2,1,0:T(8,128)(2,1)} %shard_map.104), calls=%async_computation.1 | async-start | bytes 6291456 | tf_op jit(solution)/shard_map/all_to_all | solution.py:44
  136.8 61.3 %collective-permute-done.18.w_ref = bf16[1024,1024]{1,0:T(8,128)(2,1)} collective-permute-done((bf16[1024,1024]{1,0:T(8,128)(2,1)}, bf16[1024,1024]{1,0:T(8,128)(2,1)}, u32[]{:S(2)}, u32[]{:S(2)}) %collective-permute-start.18) | collective-permute-done | bytes 2097184 | tf_op jit(solution)/shard_map/ppermute | solution.py:55
  202.4 11.7 %shard_map.106 = bf16[64,384]{1,0:T(8,128)(2,1)} custom-call(bf16[384,8192]{1,0:T(8,128)(2,1)} %bitcast.68, bf16[16,3,64,512]{3,2,1,0:T(8,128)(2,1)} %copy-done.3), custom_call_target="tpu_custom_call" | custom-call | flops 402653184 | bytes 9437184 | tf_op jit(solution)/shard_map/pallas_call | solution.py:108
  214.0 2.7 collective-permute-start.8
  216.7 25.8 %all-gather = bf16[1024,384]{1,0:T(8,128)(2,1)} all-gather(bf16[64,384]{1,0:T(8,128)(2,1)} %shard_map.106), channel_id=2, replica_groups=mesh['section'=8,'dp'=16] {'dp'}, dimensions={0}, use_global_device_ids=true | all-gather | bytes 835584 | tf_op jit(solution)/shard_map/all_gather | solution.py:267
  242.5 4.9 %shard_map.107 = bf16[16,64,128]{2,1,0:T(8,128)(2,1)} custom-call(s32[48]{0:T(128)} %bitcast.79, s32[32]{0:T(128)} %s_ref.1, bf16[16,64,384]{2,1,0:T(8,128)(2,1)} %copy-done.5, bf16[16,64,384]{2,1,0:T(8,128)(2,1)} %bitcast.75), custom_call_target="tpu_custom_call" | custom-call | flops 50331648 | bytes 1572864 | tf_op jit(solution)/shard_map/pallas_call | solution.py:172
  247.4 2.3 slice.53
  252.6 2.3 slice.51
  254.9 5.3 %all-to-all-start.3 = ((bf16[16,64,128]{2,1,0:T(8,128)(2,1)}), bf16[16,64,128]{2,1,0:T(8,128)(2,1)S(1)}, u32[]{:S(2)}, u32[]{:S(2)}) async-start(bf16[16,64,128]{2,1,0:T(8,128)(2,1)} %shard_map.107), calls=%async_computation.3 | async-start | bytes 524288 | tf_op jit(solution)/shard_map/all_to_all | solution.py:44
  262.1 2.7 collective-permute-start.15
  270.6 6.0 %shard_map.105 = f32[32,64,512]{2,1,0:T(8,128)} custom-call(s32[48]{0:T(128)} %bitcast.80, bf16[48,64,512]{2,1,0:T(8,128)(2,1)} %bitcast.46.p_ref), custom_call_target="tpu_custom_call" | custom-call | flops 1572864 | bytes 7340032 | tf_op jit(solution)/shard_map/pallas_call | solution.py:136
  281.2 5.4 %shard_map.94.rest_0_ = bf16[384,8192]{1,0:T(8,128)(2,1)} custom-call(s32[4]{0:T(128)} %pad_add_fusion.9.b_ref, bf16[384,1024]{1,0:T(8,128)(2,1)} %collective-permute-done.v_ref, bf16[1024,1024]{1,0:T(8,128)(2,1)} %constant_dynamic-update-slice_fusion.5.w_ref, bf16[3,64,128]{2,1,0:T(8,128)(2,1)} %copy-done.4, bf16[16,3,64,512]{3,2,1,0:T(8,128)(2,1)} %copy-done.2), custom_call_target="tpu_custom_call" | custom-call | flops 855638016 | bytes 3670016 | tf_op jit(solution)/shard_map/pallas_call | solution.py:214
  286.6 5.4 %shard_map.95.rest_0_ = bf16[384,8192]{1,0:T(8,128)(2,1)} custom-call(s32[4]{0:T(128)} %pad_add_fusion.8.b_ref, bf16[384,1024]{1,0:T(8,128)(2,1)} %collective-permute-done.v_ref, bf16[1024,1024]{1,0:T(8,128)(2,1)} %constant_dynamic-update-slice_fusion.w_ref, bf16[3,64,128]{2,1,0:T(8,128)(2,1)} %copy-done.4, ...), custom_call_target="tpu_custom_call", output_to_operand_aliasing={{}: (5, {})} | custom-call | flops 855638016 | bytes 3670016 | tf_op jit(solution)/shard_map/pallas_call | solution.py:214
  292.0 5.4 %shard_map.96.rest_0_ = bf16[384,8192]{1,0:T(8,128)(2,1)} custom-call(s32[4]{0:T(128)} %pad_add_fusion.7.b_ref, bf16[384,1024]{1,0:T(8,128)(2,1)} %collective-permute-done.v_ref, bf16[1024,1024]{1,0:T(8,128)(2,1)} %collective-permute-done.18.w_ref, bf16[3,64,128]{2,1,0:T(8,128)(2,1)} %copy-done.4, ...), custom_call_target="tpu_custom_call", output_to_operand_aliasing={{}: (5, {})} | custom-call | flops 855638016 | bytes 3670016 | tf_op jit(solution)/shard_map/pallas_call | solution.py:214
  297.4 5.4 %shard_map.97.rest_0_ = bf16[384,8192]{1,0:T(8,128)(2,1)} custom-call(s32[4]{0:T(128)} %pad_add_fusion.6.b_ref, bf16[384,1024]{1,0:T(8,128)(2,1)} %collective-permute-done.v_ref, bf16[1024,1024]{1,0:T(8,128)(2,1)} %collective-permute-done.16.w_ref, bf16[3,64,128]{2,1,0:T(8,128)(2,1)} %copy-done.4, ...), custom_call_target="tpu_custom_call", output_to_operand_aliasing={{}: (5, {})} | custom-call | flops 855638016 | bytes 3670016 | tf_op jit(solution)/shard_map/pallas_call | solution.py:214
  302.8 5.4 %shard_map.98.rest_0_ = bf16[384,8192]{1,0:T(8,128)(2,1)} custom-call(s32[4]{0:T(128)} %pad_add_fusion.5.b_ref, bf16[384,1024]{1,0:T(8,128)(2,1)} %collective-permute-done.v_ref, bf16[1024,1024]{1,0:T(8,128)(2,1)} %collective-permute-done.14.w_ref, bf16[3,64,128]{2,1,0:T(8,128)(2,1)} %copy-done.4, ...), custom_call_target="tpu_custom_call", output_to_operand_aliasing={{}: (5, {})} | custom-call | flops 855638016 | bytes 3670016 | tf_op jit(solution)/shard_map/pallas_call | solution.py:214
  308.2 5.4 %shard_map.99.rest_0_ = bf16[384,8192]{1,0:T(8,128)(2,1)} custom-call(s32[4]{0:T(128)} %pad_add_fusion.4.b_ref, bf16[384,1024]{1,0:T(8,128)(2,1)} %collective-permute-done.v_ref, bf16[1024,1024]{1,0:T(8,128)(2,1)} %collective-permute-done.6.w_ref, bf16[3,64,128]{2,1,0:T(8,128)(2,1)} %copy-done.4, ...), custom_call_target="tpu_custom_call", output_to_operand_aliasing={{}: (5, {})} | custom-call | flops 855638016 | bytes 3670016 | tf_op jit(solution)/shard_map/pallas_call | solution.py:214
  313.6 3.7 %shard_map.100.rest_0_ = bf16[384,8192]{1,0:T(8,128)(2,1)} custom-call(s32[2]{0:T(128)} %pad_add_fusion.3.b_ref, bf16[384,1024]{1,0:T(8,128)(2,1)} %collective-permute-done.v_ref, bf16[512,1024]{1,0:T(8,128)(2,1)} %collective-permute-done.19.w_ref, bf16[3,64,128]{2,1,0:T(8,128)(2,1)} %copy-done.4, ...), custom_call_target="tpu_custom_call", output_to_operand_aliasing={{}: (5, {})} | custom-call | flops 427819008 | bytes 2228224 | tf_op jit(solution)/shard_map/pallas_call | solution.py:214
  317.3 3.7 %shard_map.101.rest_0_ = bf16[384,8192]{1,0:T(8,128)(2,1)} custom-call(s32[2]{0:T(128)} %pad_add_fusion.2.b_ref, bf16[384,1024]{1,0:T(8,128)(2,1)} %collective-permute-done.v_ref, bf16[512,1024]{1,0:T(8,128)(2,1)} %collective-permute-done.17.w_ref, bf16[3,64,128]{2,1,0:T(8,128)(2,1)} %copy-done.4, ...), custom_call_target="tpu_custom_call", output_to_operand_aliasing={{}: (5, {})} | custom-call | flops 427819008 | bytes 2228224 | tf_op jit(solution)/shard_map/pallas_call | solution.py:214
  321.1 3.7 %shard_map.102.rest_0_ = bf16[384,8192]{1,0:T(8,128)(2,1)} custom-call(s32[2]{0:T(128)} %pad_add_fusion.1.b_ref, bf16[384,1024]{1,0:T(8,128)(2,1)} %collective-permute-done.v_ref, bf16[512,1024]{1,0:T(8,128)(2,1)} %collective-permute-done.15.w_ref, bf16[3,64,128]{2,1,0:T(8,128)(2,1)} %copy-done.4, ...), custom_call_target="tpu_custom_call", output_to_operand_aliasing={{}: (5, {})} | custom-call | flops 427819008 | bytes 2228224 | tf_op jit(solution)/shard_map/pallas_call | solution.py:214
  324.8 3.8 %shard_map.103 = bf16[384,8192]{1,0:T(8,128)(2,1)} custom-call(s32[2]{0:T(128)} %pad_add_fusion.b_ref, bf16[384,1024]{1,0:T(8,128)(2,1)} %collective-permute-done.v_ref, bf16[512,1024]{1,0:T(8,128)(2,1)} %collective-permute-done.7.w_ref, bf16[3,64,128]{2,1,0:T(8,128)(2,1)} %copy-done.4, ...), custom_call_target="tpu_custom_call", output_to_operand_aliasing={{}: (5, {})} | custom-call | flops 427819008 | bytes 2228224 | tf_op jit(solution)/shard_map/pallas_call | solution.py:214
  (84 shorter events, 64.4 us)
Async XLA Ops:
  0.6 10.4 %copy-start = (bf16[1,32,512,64]{2,3,1,0:T(8,128)(2,1)S(1)}, bf16[1,32,512,64]{2,3,1,0:T(8,128)(2,1)}, u32[]{:S(2)}) copy-start(bf16[1,32,512,64]{2,3,1,0:T(8,128)(2,1)} %param.10) | copy-start | bytes 6291460
  0.6 10.3 %copy-start.7 = (s32[1,48]{1,0:T(1,128)S(1)}, s32[1,48]{1,0:T(1,128)}, u32[]{:S(2)}) copy-start(s32[1,48]{1,0:T(1,128)} %param.12) | copy-start | bytes 580
  3.1 22.4 %all-to-all-start.2 = ((bf16[16,64,384]{2,1,0:T(8,128)(2,1)}), bf16[16,64,384]{2,1,0:T(8,128)(2,1)S(1)}, u32[]{:S(2)}, u32[]{:S(2)}) async-start(bf16[16,64,384]{2,1,0:T(8,128)(2,1)} %bitcast.74), calls=%async_computation.2 | async-start | bytes 1572864 | tf_op jit(solution)/shard_map/all_to_all | solution.py:44
  25.5 0.9 copy-start.5
  26.4 84.4 %all-to-all-start = ((bf16[16,3,64,512]{3,2,1,0:T(8,128)(2,1)}), bf16[16,3,64,512]{3,2,1,0:T(8,128)(2,1)S(1)}, u32[]{:S(2)}, u32[]{:S(2)}) async-start(bf16[16,3,64,512]{3,2,1,0:T(8,128)(2,1)} %bitcast.69), calls=%async_computation | async-start | bytes 6291456 | tf_op jit(solution)/shard_map/all_to_all | solution.py:44
  30.1 14.5 %collective-permute-start.1 = (bf16[512,1024]{1,0:T(8,128)(2,1)}, bf16[512,1024]{1,0:T(8,128)(2,1)S(1)}, u32[]{:S(2)}, u32[]{:S(2)}) collective-permute-start(bf16[512,1024]{1,0:T(8,128)(2,1)} %bitcast.81), channel_id=1, source_target_pairs={{16,0},{32,16},{48,32},{64,48},{80,64},{96,80},{112,96},{17,1},{33... | collective-permute-start | bytes 3145736 | tf_op jit(solution)/shard_map/ppermute | solution.py:28
  46.1 36.1 %collective-permute-start.10 = (bf16[256,1024]{1,0:T(8,128)(2,1)}, bf16[256,1024]{1,0:T(8,128)(2,1)}, u32[]{:S(2)}, u32[]{:S(2)}) collective-permute-start(bf16[256,1024]{1,0:T(8,128)(2,1)} %get-tuple-element.3), channel_id=1, source_target_pairs={{0,1},{1,2},{2,3},{3,0},{4,5},{5,6},{6,7},{7,4},{8,9},{9,10},{10,1... | collective-permute-start | bytes 1572872 | tf_op jit(solution)/shard_map/ppermute | solution.py:49
  47.9 47.6 %collective-permute-start.11 = (bf16[256,1024]{1,0:T(8,128)(2,1)}, bf16[256,1024]{1,0:T(8,128)(2,1)}, u32[]{:S(2)}, u32[]{:S(2)}) collective-permute-start(bf16[256,1024]{1,0:T(8,128)(2,1)} %get-tuple-element.3), channel_id=1, source_target_pairs={{0,3},{1,0},{2,1},{3,2},{4,7},{5,4},{6,5},{7,6},{8,11},{9,8},{10,9... | collective-permute-start | bytes 1572872 | tf_op jit(solution)/shard_map/ppermute | solution.py:50
  49.4 51.1 %collective-permute-start.2 = (bf16[256,1024]{1,0:T(8,128)(2,1)}, bf16[256,1024]{1,0:T(8,128)(2,1)}, u32[]{:S(2)}, u32[]{:S(2)}) collective-permute-start(bf16[256,1024]{1,0:T(8,128)(2,1)} %get-tuple-element.6), channel_id=1, source_target_pairs={{0,4},{1,5},{2,6},{3,7},{4,8},{5,9},{6,10},{7,11},{8,12},{9,13},{1... | collective-permute-start | bytes 1572872 | tf_op jit(solution)/shard_map/ppermute | solution.py:49
  51.2 51.0 %collective-permute-start.3 = (bf16[256,1024]{1,0:T(8,128)(2,1)}, bf16[256,1024]{1,0:T(8,128)(2,1)}, u32[]{:S(2)}, u32[]{:S(2)}) collective-permute-start(bf16[256,1024]{1,0:T(8,128)(2,1)} %get-tuple-element.6), channel_id=1, source_target_pairs={{0,12},{1,13},{2,14},{3,15},{4,0},{5,1},{6,2},{7,3},{8,4},{9,5},{1... | collective-permute-start | bytes 1572872 | tf_op jit(solution)/shard_map/ppermute | solution.py:50
  83.9 33.1 %collective-permute-start.12 = (bf16[128,1024]{1,0:T(8,128)(2,1)}, bf16[128,1024]{1,0:T(8,128)(2,1)}, u32[]{:S(2)}, u32[]{:S(2)}) collective-permute-start(bf16[128,1024]{1,0:T(8,128)(2,1)} %slice.49), channel_id=1, source_target_pairs={{0,1},{1,2},{2,3},{3,0},{4,5},{5,6},{6,7},{7,4},{8,9},{9,10},{10,1... | collective-permute-start | bytes 786440 | tf_op jit(solution)/shard_map/ppermute | solution.py:51
  97.2 21.4 %collective-permute-start.13 = (bf16[128,1024]{1,0:T(8,128)(2,1)}, bf16[128,1024]{1,0:T(8,128)(2,1)}, u32[]{:S(2)}, u32[]{:S(2)}) collective-permute-start(bf16[128,1024]{1,0:T(8,128)(2,1)} %slice.50), channel_id=1, source_target_pairs={{0,3},{1,0},{2,1},{3,2},{4,7},{5,4},{6,5},{7,6},{8,11},{9,8},{10,9... | collective-permute-start | bytes 786440 | tf_op jit(solution)/shard_map/ppermute | solution.py:52
  102.1 25.6 %collective-permute-start.4 = (bf16[128,1024]{1,0:T(8,128)(2,1)}, bf16[128,1024]{1,0:T(8,128)(2,1)S(1)}, u32[]{:S(2)}, u32[]{:S(2)}) collective-permute-start(bf16[128,1024]{1,0:T(8,128)(2,1)} %slice.45), channel_id=1, source_target_pairs={{0,4},{1,5},{2,6},{3,7},{4,8},{5,9},{6,10},{7,11},{8,12},{9,13},{1... | collective-permute-start | bytes 786440 | tf_op jit(solution)/shard_map/ppermute | solution.py:51
  103.8 24.6 %collective-permute-start.5 = (bf16[128,1024]{1,0:T(8,128)(2,1)}, bf16[128,1024]{1,0:T(8,128)(2,1)}, u32[]{:S(2)}, u32[]{:S(2)}) collective-permute-start(bf16[128,1024]{1,0:T(8,128)(2,1)} %slice.46), channel_id=1, source_target_pairs={{0,12},{1,13},{2,14},{3,15},{4,0},{5,1},{6,2},{7,3},{8,4},{9,5},{1... | collective-permute-start | bytes 786440 | tf_op jit(solution)/shard_map/ppermute | solution.py:52
  110.8 1.7 copy-start.3
  112.5 142.4 %all-to-all-start.1 = ((bf16[16,3,64,512]{3,2,1,0:T(8,128)(2,1)}), bf16[16,3,64,512]{3,2,1,0:T(8,128)(2,1)}, u32[]{:S(2)}, u32[]{:S(2)}) async-start(bf16[16,3,64,512]{3,2,1,0:T(8,128)(2,1)} %shard_map.104), calls=%async_computation.1 | async-start | bytes 6291456 | tf_op jit(solution)/shard_map/all_to_all | solution.py:44
  120.3 77.8 %collective-permute-start.18 = (bf16[1024,1024]{1,0:T(8,128)(2,1)}, bf16[1024,1024]{1,0:T(8,128)(2,1)}, u32[]{:S(2)}, u32[]{:S(2)}) collective-permute-start(bf16[1024,1024]{1,0:T(8,128)(2,1)} %constant_dynamic-update-slice_fusion.5.w_ref), channel_id=1, source_target_pairs={{0,4},{1,5},{2,6},{3,7},{4,8},{5,9},{6,10},{7,11},{8,12},{9,13},{1... | collective-permute-start | bytes 6291464 | tf_op jit(solution)/shard_map/ppermute | solution.py:55
  124.0 155.6 %collective-permute-start.9 = (bf16[16,3,64,512]{3,2,1,0:T(8,128)(2,1)}, bf16[16,3,64,512]{3,2,1,0:T(8,128)(2,1)S(1)}, u32[]{:S(2)}, u32[]{:S(2)}) collective-permute-start(bf16[16,3,64,512]{3,2,1,0:T(8,128)(2,1)} %copy-done.3), channel_id=1, source_target_pairs={{16,0},{32,16},{48,32},{64,48},{80,64},{96,80},{112,96},{17,1},{33... | collective-permute-start | bytes 9437192 | tf_op jit(solution)/shard_map/ppermute | solution.py:28
  130.1 83.9 %collective-permute-start.16 = (bf16[1024,1024]{1,0:T(8,128)(2,1)}, bf16[1024,1024]{1,0:T(8,128)(2,1)}, u32[]{:S(2)}, u32[]{:S(2)}) collective-permute-start(bf16[1024,1024]{1,0:T(8,128)(2,1)} %constant_dynamic-update-slice_fusion.w_ref), channel_id=1, source_target_pairs={{0,1},{1,2},{2,3},{3,0},{4,5},{5,6},{6,7},{7,4},{8,9},{9,10},{10,1... | collective-permute-start | bytes 6291464 | tf_op jit(solution)/shard_map/ppermute | solution.py:55
  131.6 120.4 %collective-permute-start.14 = (bf16[1024,1024]{1,0:T(8,128)(2,1)}, bf16[1024,1024]{1,0:T(8,128)(2,1)}, u32[]{:S(2)}, u32[]{:S(2)}) collective-permute-start(bf16[1024,1024]{1,0:T(8,128)(2,1)} %constant_dynamic-update-slice_fusion.5.w_ref), channel_id=1, source_target_pairs={{0,12},{1,13},{2,14},{3,15},{4,0},{5,1},{6,2},{7,3},{8,4},{9,5},{1... | collective-permute-start | bytes 6291464 | tf_op jit(solution)/shard_map/ppermute | solution.py:56
  133.4 128.8 %collective-permute-start.6 = (bf16[1024,1024]{1,0:T(8,128)(2,1)}, bf16[1024,1024]{1,0:T(8,128)(2,1)}, u32[]{:S(2)}, u32[]{:S(2)}) collective-permute-start(bf16[1024,1024]{1,0:T(8,128)(2,1)} %constant_dynamic-update-slice_fusion.w_ref), channel_id=1, source_target_pairs={{0,3},{1,0},{2,1},{3,2},{4,7},{5,4},{6,5},{7,6},{8,11},{9,8},{10,9... | collective-permute-start | bytes 6291464 | tf_op jit(solution)/shard_map/ppermute | solution.py:56
  198.1 69.5 %collective-permute-start = (bf16[384,1024]{1,0:T(8,128)(2,1)}, bf16[384,1024]{1,0:T(8,128)(2,1)}, u32[]{:S(2)}, u32[]{:S(2)}) collective-permute-start(bf16[384,1024]{1,0:T(8,128)(2,1)} %bitcast.73), channel_id=1, source_target_pairs={{16,0},{32,16},{48,32},{64,48},{80,64},{96,80},{112,96},{17,1},{33... | collective-permute-start | bytes 2359304 | tf_op jit(solution)/shard_map/ppermute | solution.py:28
  202.4 11.7 %copy-start.6 = (bf16[3,64,128]{2,1,0:T(8,128)(2,1)S(1)}, bf16[3,64,128]{2,1,0:T(8,128)(2,1)}, u32[]{:S(2)}) copy-start(bf16[3,64,128]{2,1,0:T(8,128)(2,1)} %convolution_convert_fusion.low_ref) | copy-start | bytes 147460
  214.0 46.1 %collective-permute-start.8 = (bf16[3,64,128]{2,1,0:T(8,128)(2,1)S(1)}, bf16[3,64,128]{2,1,0:T(8,128)(2,1)S(1)}, u32[]{:S(2)}, u32[]{:S(2)}) collective-permute-start(bf16[3,64,128]{2,1,0:T(8,128)(2,1)S(1)} %copy-done.6), channel_id=1, source_target_pairs={{16,0},{32,16},{48,32},{64,48},{80,64},{96,80},{112,96},{17,1},{33... | collective-permute-start | bytes 147464 | tf_op jit(solution)/shard_map/ppermute | solution.py:28
  252.0 61.6 %collective-permute-start.19 = (bf16[512,1024]{1,0:T(8,128)(2,1)}, bf16[512,1024]{1,0:T(8,128)(2,1)}, u32[]{:S(2)}, u32[]{:S(2)}) collective-permute-start(bf16[512,1024]{1,0:T(8,128)(2,1)} %slice.53), channel_id=1, source_target_pairs={{0,4},{1,5},{2,6},{3,7},{4,8},{5,9},{6,10},{7,11},{8,12},{9,13},{1... | collective-permute-start | bytes 3145736 | tf_op jit(solution)/shard_map/ppermute | solution.py:57
  254.9 21.8 %all-to-all-start.3 = ((bf16[16,64,128]{2,1,0:T(8,128)(2,1)}), bf16[16,64,128]{2,1,0:T(8,128)(2,1)S(1)}, u32[]{:S(2)}, u32[]{:S(2)}) async-start(bf16[16,64,128]{2,1,0:T(8,128)(2,1)} %shard_map.107), calls=%async_computation.3 | async-start | bytes 524288 | tf_op jit(solution)/shard_map/all_to_all | solution.py:44
  260.1 16.5 %copy-start.4 = (bf16[3,64,128]{2,1,0:T(8,128)(2,1)}, bf16[3,64,128]{2,1,0:T(8,128)(2,1)S(1)}, u32[]{:S(2)}) copy-start(bf16[3,64,128]{2,1,0:T(8,128)(2,1)S(1)} %collective-permute-done.8.low_ref) | copy-start | bytes 147460
  260.1 57.2 %collective-permute-start.17 = (bf16[512,1024]{1,0:T(8,128)(2,1)}, bf16[512,1024]{1,0:T(8,128)(2,1)}, u32[]{:S(2)}, u32[]{:S(2)}) collective-permute-start(bf16[512,1024]{1,0:T(8,128)(2,1)} %slice.52), channel_id=1, source_target_pairs={{0,1},{1,2},{2,3},{3,0},{4,5},{5,6},{6,7},{7,4},{8,9},{9,10},{10,1... | collective-permute-start | bytes 3145736 | tf_op jit(solution)/shard_map/ppermute | solution.py:57
  262.1 58.9 %collective-permute-start.15 = (bf16[512,1024]{1,0:T(8,128)(2,1)}, bf16[512,1024]{1,0:T(8,128)(2,1)}, u32[]{:S(2)}, u32[]{:S(2)}) collective-permute-start(bf16[512,1024]{1,0:T(8,128)(2,1)} %slice.51), channel_id=1, source_target_pairs={{0,12},{1,13},{2,14},{3,15},{4,0},{5,1},{6,2},{7,3},{8,4},{9,5},{1... | collective-permute-start | bytes 3145736 | tf_op jit(solution)/shard_map/ppermute | solution.py:58
  267.6 57.1 %collective-permute-start.7 = (bf16[512,1024]{1,0:T(8,128)(2,1)}, bf16[512,1024]{1,0:T(8,128)(2,1)}, u32[]{:S(2)}, u32[]{:S(2)}) collective-permute-start(bf16[512,1024]{1,0:T(8,128)(2,1)} %slice.47), channel_id=1, source_target_pairs={{0,3},{1,0},{2,1},{3,2},{4,7},{5,4},{6,5},{7,6},{8,11},{9,8},{10,9... | collective-permute-start | bytes 3145736 | tf_op jit(solution)/shard_map/ppermute | solution.py:58
  279.5 1.6 copy-start.2
  324.8 3.8 %copy-start.1 = (bf16[1,32,512,64]{2,3,1,0:T(8,128)(2,1)S(1)}, bf16[1,32,512,64]{2,3,1,0:T(8,128)(2,1)}, u32[]{:S(2)}) copy-start(bf16[1,32,512,64]{2,3,1,0:T(8,128)(2,1)} %param.10) | copy-start | bytes 6291460

commit v2 on v1

v2 whole, which is shorter than its diff:
```python
import jax
import jax.numpy as jnp
from jax import lax
from jax.experimental import pallas as pl
from jax.experimental.pallas import tpu as pltpu
from jax.sharding import PartitionSpec as P

GROUP_ROWS = 128
ADAPTER_SCALE = 2.0
WIDE = 4
PARAMS = pltpu.CompilerParams(vmem_limit_bytes=48 * 2**20)
RING = 4

F32 = jnp.float32
BF16 = jnp.bfloat16
NT = (((1,), (1,)), ((), ()))


def dot(a, b, dims):
    return lax.dot_general(a, b, dims, preferred_element_type=F32)


def cost(flops, nbytes):
    return pl.CostEstimate(flops=int(flops), bytes_accessed=int(nbytes), transcendentals=0)


def to_previous_section(block):
    n = lax.axis_size("section")
    return lax.ppermute(block, "section", [(i, i - 1) for i in range(1, n)])


def along(axis, distance, down):
    route = []
    for section in range(lax.axis_size("section") - down):
        for z in range(RING):
            for x in range(RING):
                if (axis == "row") == (section % 2 == 0):
                    to = (z, (x + distance) % RING)
                else:
                    to = ((z + distance) % RING, x)
                base = RING * RING * section
                start = base + RING * RING * down + RING * z + x
                route.append((start, base + RING * to[0] + to[1]))
    return route


def move(block, axis, distance, down=0):
    return lax.ppermute(block, ("section", "dp"), along(axis, distance, down))


def exchange(blocks):
    return lax.all_to_all(blocks, "dp", split_axis=0, concat_axis=0, tiled=True)


def together(*values):
    return lax.optimization_barrier(values)


def group_terms(x, low_t):
    rows, width = x.shape
    groups, rank, _ = low_t.shape
    n = lax.axis_size("dp")
    cols = width // n

    def body(x_ref, low_ref, o_ref):
        for q in range(WIDE):
            for g in range(groups):
                o_ref[q, g] = jnp.dot(
                    low_ref[g],
                    x_ref[g * GROUP_ROWS : (g + 1) * GROUP_ROWS, q * cols : (q + 1) * cols],
                    preferred_element_type=F32,
                ).astype(BF16)

    return pl.pallas_call(
        body,
        grid=(n // WIDE,),
        in_specs=[
            pl.BlockSpec((rows, WIDE * cols), lambda d: (0, d)),
            pl.BlockSpec((groups, rank, GROUP_ROWS), lambda d: (0, 0, 0)),
        ],
        out_specs=pl.BlockSpec((WIDE, groups, rank, cols), lambda d: (d, 0, 0, 0)),
        out_shape=jax.ShapeDtypeStruct((n, groups, rank, cols), BF16),
        compiler_params=PARAMS,
        cost_estimate=cost(2 * rows * width * rank, 2 * (rows * width + groups * rank * width)),
    )(x, low_t)


def segments(groups, rank):
    half = groups * rank // 2
    out = []
    for g in range(groups):
        start, stop = g * rank, (g + 1) * rank
        for side in range(2):
            lo, hi = max(start, side * half), min(stop, (side + 1) * half)
            if lo < hi:
                out.append((g, slice(lo - start, hi - start), side, slice(lo - side * half, hi - side * half)))
    return out


def up_parts(x, down, v):
    rows, width = x.shape
    n, groups, rank, cols = down.shape
    kv = v.shape[1]

    def body(x_ref, a_ref, v_ref, o_ref, acc):
        d = pl.program_id(0)

        @pl.when(d == 0)
        def _():
            acc[...] = jnp.zeros_like(acc)

        for g in range(groups):
            span = slice(g * GROUP_ROWS, (g + 1) * GROUP_ROWS)
            for q in range(WIDE):
                acc[:, span] += dot(a_ref[q, g], x_ref[span, q * cols : (q + 1) * cols], NT)

        @pl.when(d == n // WIDE - 1)
        def _():
            for g, term, side, place in segments(groups, rank):
                span = slice(g * GROUP_ROWS, (g + 1) * GROUP_ROWS)
                o_ref[place, side * kv : (side + 1) * kv] = jnp.dot(
                    acc[term, span].astype(BF16), v_ref[span, :], preferred_element_type=F32
                ).astype(BF16)

    return pl.pallas_call(
        body,
        grid=(n // WIDE,),
        in_specs=[
            pl.BlockSpec((rows, WIDE * cols), lambda d: (0, d)),
            pl.BlockSpec((WIDE, groups, rank, cols), lambda d: (d, 0, 0, 0)),
            pl.BlockSpec((rows, kv), lambda d: (0, 0)),
        ],
        out_specs=pl.BlockSpec((groups * rank // 2, 2 * kv), lambda d: (0, 0)),
        out_shape=jax.ShapeDtypeStruct((groups * rank // 2, 2 * kv), BF16),
        scratch_shapes=[pltpu.VMEM((rank, rows), F32)],
        compiler_params=PARAMS,
        cost_estimate=cost(2 * rows * width * rank, 2 * (rows * width + groups * rank * width)),
    )(x, down, v)


def frozen_terms(stacks, weights, tail=None, with_tail=0):
    rows, kv = stacks[0].shape
    width = sum(w.shape[0] for w in weights)
    extra = tail.shape[0] if with_tail else 0
    heights = [rows + (extra if i < with_tail else 0) for i in range(len(stacks))]
    tails = [tail] if with_tail else []

    def body(*refs):
        w_refs, refs = refs[: len(weights)], refs[len(weights) :]
        v_refs, refs = refs[: len(stacks)], refs[len(stacks) :]
        o_refs = refs[len(tails) :]
        for i, (v_ref, o_ref) in enumerate(zip(v_refs, o_refs)):
            left = 0
            for w_ref in w_refs:
                span = slice(left, left + w_ref.shape[0])
                o_ref[:rows, span] = dot(v_ref[...], w_ref[...], NT).astype(BF16)
                left += w_ref.shape[0]
            if i < with_tail:
                o_ref[rows:, :] = refs[0][...]

    def whole(shape):
        return pl.BlockSpec(shape, lambda i: (0, 0))

    return pl.pallas_call(
        body,
        grid=(1,),
        in_specs=[whole(a.shape) for a in (*weights, *stacks, *tails)],
        out_specs=[whole((h, width)) for h in heights],
        out_shape=[jax.ShapeDtypeStruct((h, width), BF16) for h in heights],
        compiler_params=PARAMS,
        cost_estimate=cost(
            2 * sum(heights) * kv * width, 2 * (sum(heights) * (kv + width) + kv * width)
        ),
    )(*weights, *stacks, *tails)


def up_by_slot(pieces, places, slots, rank):
    groups = places.shape[0] // len(pieces)
    height, kv = groups * rank // 2, pieces[0].shape[1] // 2

    def body(place_ref, *refs):
        parts, o_ref, acc = refs[:-2], refs[-2], refs[-1]
        acc[...] = jnp.zeros_like(acc)
        for p, part in enumerate(parts):
            for g, term, side, rows in segments(groups, rank):
                place = place_ref[p * groups + g]

                @pl.when(place < slots)
                def _():
                    acc[place, term] += part[rows, side * kv : (side + 1) * kv].astype(F32)

        o_ref[...] = acc[...].astype(BF16)

    in_specs = [pl.BlockSpec(memory_space=pltpu.SMEM)]
    for piece in pieces:
        last = piece.shape[0] // height - 1
        in_specs.append(pl.BlockSpec((height, 2 * kv), lambda i, last=last: (last, 0)))
    return pl.pallas_call(
        body,
        grid=(1,),
        in_specs=in_specs,
        out_specs=pl.BlockSpec((slots, rank, kv), lambda i: (0, 0, 0)),
        out_shape=jax.ShapeDtypeStruct((slots, rank, kv), BF16),
        scratch_shapes=[pltpu.VMEM((slots, rank, kv), F32)],
        compiler_params=PARAMS,
        cost_estimate=cost(
            len(pieces) * height * kv, 2 * (2 * len(pieces) * height + slots * rank) * kv
        ),
    )(places, *pieces)


def sum_by_tenant(parts, tenants, n_tenants):
    n, groups, rank, cols = parts.shape
    steps = 4
    r = rank // steps
    scale = ADAPTER_SCALE / GROUP_ROWS

    def body(t_ref, p_ref, o_ref):
        o_ref[...] = jnp.zeros_like(o_ref)

        @pl.loop(0, n)
        def _(d):
            for g in range(groups):
                o_ref[t_ref[d * groups + g]] += p_ref[d, g].astype(F32) * scale

    return pl.pallas_call(
        body,
        grid_spec=pltpu.PrefetchScalarGridSpec(
            num_scalar_prefetch=1,
            grid=(steps,),
            in_specs=[pl.BlockSpec((n, groups, r, cols), lambda i, t: (0, 0, i, 0))],
            out_specs=pl.BlockSpec((n_tenants, r, cols), lambda i, t: (0, i, 0)),
        ),
        out_shape=jax.ShapeDtypeStruct((n_tenants, rank, cols), F32),
        cost_estimate=cost(
            n * groups * rank * cols, 2 * n * groups * rank * cols + 4 * n_tenants * rank * cols
        ),
    )(tenants, parts)


def gradient_columns(out, blocks, frozen, low, down):
    n, groups, rank, cols = down.shape
    rows = groups * GROUP_ROWS
    count = frozen.shape[1] // cols

    def body(b_ref, f_ref, low_ref, a_ref, *rest):
        o_ref = rest[-1]
        for g in range(groups):
            span = slice(g * GROUP_ROWS, (g + 1) * GROUP_ROWS)
            adapter = jnp.dot(low_ref[g], a_ref[0, g], preferred_element_type=F32)
            o_ref[span, :] = (f_ref[span, :].astype(F32) + ADAPTER_SCALE * adapter).astype(BF16)

    in_specs = [
        pl.BlockSpec((rows, cols), lambda i, b: (0, i)),
        pl.BlockSpec((groups, GROUP_ROWS, rank), lambda i, b: (0, 0, 0)),
        pl.BlockSpec((1, groups, rank, cols), lambda i, b: (b[i], 0, 0, 0)),
    ]
    args = [blocks, frozen, low, down]
    aliases = {}
    if out is not None:
        in_specs.append(pl.BlockSpec(memory_space=pl.ANY))
        aliases = {len(args): 0}
        args.append(out)
    return pl.pallas_call(
        body,
        grid_spec=pltpu.PrefetchScalarGridSpec(
            num_scalar_prefetch=1,
            grid=(count,),
            in_specs=in_specs,
            out_specs=pl.BlockSpec((rows, cols), lambda i, b: (0, b[i])),
        ),
        out_shape=jax.ShapeDtypeStruct((rows, n * cols), BF16),
        input_output_aliases=aliases,
        cost_estimate=cost(2 * rows * rank * cols * count, 4 * count * rows * cols),
    )(*args)


def local(
    layer_input, value_grad, frozen_weight, adapter_down, adapter_up, group_tenant, slot_tenant
):
    x = layer_input[0]
    v = value_grad[0]
    w = frozen_weight[0]
    down = jnp.swapaxes(adapter_down[0], 1, 2)
    up = adapter_up[0]
    tenants = group_tenant[0]
    n = lax.axis_size("dp")
    me = lax.axis_index("dp")
    rows, kv = v.shape
    n_tenants, rank, cols = down.shape
    groups = rows // GROUP_ROWS
    my_tenants = lax.dynamic_slice_in_dim(tenants, me * groups, groups)

    weights = tuple(move(w, "col", step, 1) for step in (0, 1, -1, 2))
    v_next = to_previous_section(v)

    down_mine = exchange(down[tenants].reshape(n, groups, rank, cols))

    low = jnp.einsum(
        "gnk,grk->gnr",
        v.reshape(groups, GROUP_ROWS, kv),
        up[my_tenants],
        preferred_element_type=F32,
    ).astype(BF16)
    low_next = to_previous_section(low)
    sent = group_terms(x, jnp.swapaxes(low, 1, 2))
    v_below, v_above, v_far = (move(v_next, "row", step) for step in (1, -1, 2))
    x, sent = together(x, sent)

    parts = up_parts(x, down_mine, v)
    parts, low_next = together(parts, low_next)
    down_next = to_previous_section(down_mine)
    for_above, for_below = frozen_terms((v_above, v_below), weights, parts, 2)
    from_below, from_above = move(for_above, "row", 1), move(for_below, "row", -1)
    (for_far,) = frozen_terms((v_far,), weights, parts, 1)
    from_far = move(for_far, "row", 2)
    sent, from_below, from_above, from_far, v_next = together(
        sent, from_below, from_above, from_far, v_next
    )
    terms = exchange(sent)
    (own,) = frozen_terms((v_next,), weights)

    odd = lax.axis_index("section") % 2 == 1
    mz, mx = me // RING, me % RING
    row, col = jnp.where(odd, mz, mx), jnp.where(odd, mx, mz)

    def device_at(r, c):
        return jnp.where(odd, RING * r + c, RING * c + r).astype(jnp.int32)

    steps = jnp.array([0, -1, 1, 2])
    per = n_tenants // n
    holders = device_at((row + steps) % RING, col)
    held = tenants.reshape(n, groups)[holders].reshape(-1)
    owners = device_at(row, (col + steps) % RING)
    wanted = slot_tenant.reshape(n, per)[owners].reshape(-1)
    matches = held[:, None] == wanted[None, :]
    places = jnp.where(jnp.any(matches, 1), jnp.argmax(matches, 1), wanted.shape[0])
    by_slot = up_by_slot(
        (parts, from_below, from_above, from_far),
        places.astype(jnp.int32),
        RING * per,
        rank,
    )
    mine, to_below, to_above, to_far = by_slot.reshape(RING, per, rank, kv)
    from_up = (move(to_below, "col", -1), move(to_above, "col", 1), move(to_far, "col", 2))

    out = None
    for piece, step in ((own, 0), (from_below, -1), (from_above, 1), (from_far, 2)):
        blocks = device_at((row + step) % RING, (col + steps) % RING)
        out = gradient_columns(out, blocks, piece, low_next, down_next)

    out, *from_up = together(out, *from_up)
    up_grad = sum((block.astype(F32) for block in from_up), mine.astype(F32))
    up_grad = up_grad * (ADAPTER_SCALE / GROUP_ROWS)
    out, up_grad, terms = together(out, up_grad, terms)
    down_grad = sum_by_tenant(terms, tenants, n_tenants)
    return (out[None], jnp.swapaxes(down_grad, 1, 2)[None], up_grad[None])


def solution(mesh):
    placed = (
        P("section", "dp", None),
        P("section", "dp", None),
        P("section", "dp", None),
        P("section", None, "dp", None),
        P("section", None, None, None),
        P("section", None),
        P(),
    )
    return jax.shard_map(
        local,
        mesh=mesh,
        in_specs=placed,
        out_specs=(
            P("section", "dp", None),
            P("section", None, "dp", None),
            P("section", "dp", None, None),
        ),
        check_vma=False,
    )
```

time: 331 us -> 209 us (0.63)
  waiting for transfers between devices: 111 us -> 80.3 us
  local copies, waits for them, and re-layouts: 44.5 us -> 17.1 us
  Pallas kernels: 81.6 us -> 55.3 us
  blocking collectives: 25.8 us -> 0 us
  starting transfers between devices: 56.2 us -> 47.8 us
    pallas_call x10 -> x4, Pallas kernels: 47.4 us -> 19.5 us  [gradient_columns(): pl.pallas_call(body, grid_spec=pltpu.PrefetchScalarGridSpec(num_scalar_pr...]
    all_gather x1 -> x0, blocking collectives: 25.8 us -> none  [local(): proj_all = lax.all_gather(proj_t, 'dp', axis=0)]
    slice x9 -> x0, local copies, waits for them, and re-layouts: 17.3 us -> none  [the longest x2 4.58 us: gather_ring(): plane_far_a = lax.ppermute(plane_up[:m // 2], 'dp', second(1))]
    all_to_all x4 -> x2, waiting for transfers between devices: 11.9 us -> 0.01 us  [exchange(): return lax.all_to_all(blocks, 'dp', split_axis=0, concat_axis=0, tiled=True)]
    ppermute x16 -> x13, waiting for transfers between devices: 86 us -> 76.1 us  [move(): return lax.ppermute(block, ('section', 'dp'), along(axis, distance, down))]
    ppermute x4 -> x3, waiting for transfers between devices: 12.6 us -> 4.17 us  [to_previous_section(): return lax.ppermute(block, 'section', [(i, i - 1) for i in range(1, n)])]
    all_to_all x4 -> x2, starting transfers between devices: 21.4 us -> 13.4 us  [exchange(): return lax.all_to_all(blocks, 'dp', split_axis=0, concat_axis=0, tiled=True)]
    unnamed x22 -> x23, local copies, waits for them, and re-layouts: 14.1 us -> 8.61 us
  transfers between devices with their start and end apart: 24 -> 18, of which waited for: 4 -> 4; matrix products, arithmetic and copies ran while one was open for 14% -> 6% of each run, Pallas kernels for 24% -> 24%
where the time goes in v2:
time: 209 us; the launch traced here: 208 us
  waiting for transfers between devices  80.3 us (38%)
  Pallas kernels  55.3 us (26%)
  starting transfers between devices  47.8 us (23%)
  local copies, waits for them, and re-layouts  17.1 us (8%)
  other arithmetic  4.86 us (2%)
    ppermute x13, waiting for transfers between devices, move(): return lax.ppermute(block, ('section', 'dp'), along(axis, distance, down))  76.1 us
    ppermute x13, starting transfers between devices, move(): return lax.ppermute(block, ('section', 'dp'), along(axis, distance, down))  27.9 us
    pallas_call x4, Pallas kernels, gradient_columns(): pl.pallas_call(body, grid_spec=pltpu.PrefetchScalarGridSpec(num_scalar_pr...  19.5 us
    pallas_call x3, Pallas kernels, frozen_terms(): pl.pallas_call(body, grid=(1,), in_specs=[whole(a.shape) for a in (*weigh...  18.8 us
    all_to_all x2, starting transfers between devices, exchange(): return lax.all_to_all(blocks, 'dp', split_axis=0, concat_axis=0, tiled=True)  13.4 us
    unnamed x23, local copies, waits for them, and re-layouts  8.61 us
    ppermute x3, starting transfers between devices, to_previous_section(): return lax.ppermute(block, 'section', [(i, i - 1) for i in range(1, n)])  6.44 us
    pallas_call x1, Pallas kernels, up_parts(): pl.pallas_call(body, grid=(n // WIDE,), in_specs=[pl.BlockSpec((rows, WID...  5.74 us
  transfers between devices with their start and end apart: 18, of which 4 were waited for; matrix products, arithmetic and copies ran while one was open for 6% of the time, Pallas kernels for 24%

profile of v2, /device:TPU:24, one launch (start us, length us, event | category | flops | bytes accessed | tf_op | source)
XLA Modules:
  0.0 207.7 jit_solution(6202809650036528697)
XLA Ops:
  2.2 2.5 %gather_fusion.1 = bf16[48,64,512]{2,1,0:T(8,128)(2,1)} fusion(bf16[32,64,512]{2,1,0:T(8,128)(2,1)S(1)} %bitcast.26, s32[1024]{0:T(1024)S(1)} %pad_clamp_fusion.2), kind=kCustom, calls=%fused_computation.1 | custom fusion | bytes 6291648 | tf_op jit(solution)/shard_map/gather | solution.py:297
  4.8 8.1 %all-to-all-start = ((bf16[16,3,64,512]{3,2,1,0:T(8,128)(2,1)}), bf16[16,3,64,512]{3,2,1,0:T(8,128)(2,1)}, u32[]{:S(2)}, u32[]{:S(2)}) async-start(bf16[16,3,64,512]{3,2,1,0:T(8,128)(2,1)} %bitcast.33), calls=%async_computation | async-start | bytes 6291456 | tf_op jit(solution)/shard_map/all_to_all | solution.py:52
  12.8 1.9 collective-permute-start
  14.8 4.1 %collective-permute-start.1 = (bf16[512,1024]{1,0:T(8,128)(2,1)}, bf16[512,1024]{1,0:T(8,128)(2,1)}, u32[]{:S(2)}, u32[]{:S(2)}) collective-permute-start(bf16[512,1024]{1,0:T(8,128)(2,1)} %bitcast.40), channel_id=1, source_target_pairs={{16,4},{17,5},{18,6},{19,7},{20,8},{21,9},{22,10},{23,11},{24,12},... | collective-permute-start | bytes 3145736 | tf_op jit(solution)/shard_map/ppermute | solution.py:48
  18.8 2.1 %collective-permute-start.4 = (bf16[384,1024]{1,0:T(8,128)(2,1)S(1)}, bf16[384,1024]{1,0:T(8,128)(2,1)}, u32[]{:S(2)}, u32[]{:S(2)}) collective-permute-start(bf16[384,1024]{1,0:T(8,128)(2,1)S(1)} %bitcast.27), channel_id=1, source_target_pairs={{16,0},{32,16},{48,32},{64,48},{80,64},{96,80},{112,96},{17,1},{33... | collective-permute-start | bytes 2359304 | tf_op jit(solution)/shard_map/ppermute | solution.py:29
  21.0 3.5 %gather_fusion = bf16[3,64,1024]{2,1,0:T(8,128)(2,1)} fusion(bf16[32,64,1024]{2,1,0:T(8,128)(2,1)} %bitcast.37, s32[1024]{0:T(1024)S(1)} %pad_clamp_fusion.3), kind=kCustom, calls=%fused_computation | custom fusion | bytes 786444 | tf_op jit(solution)/shard_map/gather | solution.py:302
  26.1 2.3 %collective-permute-start.7 = (bf16[3,128,64]{2,1,0:T(8,128)(2,1)S(1)}, bf16[3,128,64]{2,1,0:T(8,128)(2,1)S(1)}, u32[]{:S(2)}, u32[]{:S(2)}) collective-permute-start(bf16[3,128,64]{2,1,0:T(8,128)(2,1)S(1)} %bitcast.36), channel_id=1, source_target_pairs={{16,0},{32,16},{48,32},{64,48},{80,64},{96,80},{112,96},{17,1},{33... | collective-permute-start | bytes 147464 | tf_op jit(solution)/shard_map/ppermute | solution.py:29
  28.4 4.2 %collective-permute-start.2 = (bf16[512,1024]{1,0:T(8,128)(2,1)}, bf16[512,1024]{1,0:T(8,128)(2,1)}, u32[]{:S(2)}, u32[]{:S(2)}) collective-permute-start(bf16[512,1024]{1,0:T(8,128)(2,1)} %bitcast.41), channel_id=1, source_target_pairs={{16,12},{17,13},{18,14},{19,15},{20,0},{21,1},{22,2},{23,3},{24,4}... | collective-permute-start | bytes 3145736 | tf_op jit(solution)/shard_map/ppermute | solution.py:48
  32.6 4.2 %collective-permute-done.7.low_ref = bf16[3,128,64]{2,1,0:T(8,128)(2,1)S(1)} collective-permute-done((bf16[3,128,64]{2,1,0:T(8,128)(2,1)S(1)}, bf16[3,128,64]{2,1,0:T(8,128)(2,1)S(1)}, u32[]{:S(2)}, u32[]{:S(2)}) %collective-permute-start.7) | collective-permute-done | bytes 49184 | tf_op jit(solution)/shard_map/ppermute | solution.py:29
  36.7 7.0 %collective-permute-start.3 = (bf16[512,1024]{1,0:T(8,128)(2,1)}, bf16[512,1024]{1,0:T(8,128)(2,1)}, u32[]{:S(2)}, u32[]{:S(2)}) collective-permute-start(bf16[512,1024]{1,0:T(8,128)(2,1)} %bitcast.42), channel_id=1, source_target_pairs={{16,8},{17,9},{18,10},{19,11},{20,12},{21,13},{22,14},{23,15},{24,... | collective-permute-start | bytes 3145736 | tf_op jit(solution)/shard_map/ppermute | solution.py:48
  45.9 30.1 %collective-permute-done.1.refs_1_ = bf16[512,1024]{1,0:T(8,128)(2,1)} collective-permute-done((bf16[512,1024]{1,0:T(8,128)(2,1)}, bf16[512,1024]{1,0:T(8,128)(2,1)}, u32[]{:S(2)}, u32[]{:S(2)}) %collective-permute-start.1) | collective-permute-done | bytes 1048608 | tf_op jit(solution)/shard_map/ppermute | solution.py:48
  76.0 4.2 %shard_map.103 = bf16[16,3,64,512]{3,2,1,0:T(8,128)(2,1)S(1)} custom-call(bf16[384,8192]{1,0:T(8,128)(2,1)} %bitcast.31, bf16[3,64,128]{2,1,0:T(8,128)(2,1)S(1)} %convolution_convert_fusion.low_ref), custom_call_target="tpu_custom_call" | custom-call | flops 402653184 | bytes 9437184 | tf_op jit(solution)/shard_map/pallas_call | solution.py:74
  80.2 1.6 copy-done.1
  81.8 5.7 %shard_map.104.refs_6_.refs_5_.refs_0_ = bf16[96,2048]{1,0:T(8,128)(2,1)S(1)} custom-call(bf16[384,8192]{1,0:T(8,128)(2,1)} %bitcast.32, bf16[16,3,64,512]{3,2,1,0:T(8,128)(2,1)} %all-to-all-done.a_ref, bf16[384,1024]{1,0:T(8,128)(2,1)S(1)} %bitcast.29), custom_call_target="tpu_custom_call" | custom-call | flops 402653184 | bytes 9437184 | tf_op jit(solution)/shard_map/pallas_call | solution.py:125
  87.6 9.7 %collective-permute-done.5.refs_4_ = bf16[384,1024]{1,0:T(8,128)(2,1)} collective-permute-done((bf16[384,1024]{1,0:T(8,128)(2,1)}, bf16[384,1024]{1,0:T(8,128)(2,1)}, u32[]{:S(2)}, u32[]{:S(2)}) %collective-permute-start.5) | collective-permute-done | bytes 786464 | tf_op jit(solution)/shard_map/ppermute | solution.py:48
  97.3 8.0 %shard_map.105 = (bf16[480,2048]{1,0:T(8,128)(2,1)}, bf16[480,2048]{1,0:T(8,128)(2,1)}) custom-call(bf16[512,1024]{1,0:T(8,128)(2,1)} %collective-permute-done.refs_0_, bf16[512,1024]{1,0:T(8,128)(2,1)} %collective-permute-done.1.refs_1_, bf16[512,1024]{1,0:T(8,128)(2,1)} %collective-permute-done.2.refs_2_, ...), custom_call_target="tpu_custom_call" | custom-call | flops 4026531840 | bytes 10092544 | tf_op jit(solution)/shard_map/pallas_call | solution.py:164
  106.1 2.3 %collective-permute-start.9 = (bf16[480,2048]{1,0:T(8,128)(2,1)}, bf16[480,2048]{1,0:T(8,128)(2,1)S(1)}, u32[]{:S(2)}, u32[]{:S(2)}) collective-permute-start(bf16[480,2048]{1,0:T(8,128)(2,1)} %get-tuple-element.26), channel_id=1, source_target_pairs={{0,3},{1,0},{2,1},{3,2},{4,7},{5,4},{6,5},{7,6},{8,11},{9,8},{10,9... | collective-permute-start | bytes 5898248 | tf_op jit(solution)/shard_map/ppermute | solution.py:48
  108.5 5.5 %shard_map.106 = bf16[480,2048]{1,0:T(8,128)(2,1)} custom-call(bf16[512,1024]{1,0:T(8,128)(2,1)} %collective-permute-done.refs_0_, bf16[512,1024]{1,0:T(8,128)(2,1)} %collective-permute-done.1.refs_1_, bf16[512,1024]{1,0:T(8,128)(2,1)} %collective-permute-done.2.refs_2_, bf16[512,1024]{1,0:T(8,128)(2,1)} %collective-permute-done.3.refs_3_, ...), custom_call_target="tpu_custom_call" | custom-call | flops 2013265920 | bytes 7143424 | tf_op jit(solution)/shard_map/pallas_call | solution.py:164
  114.0 2.1 collective-permute-start.12
  116.0 36.3 %collective-permute-done.8.f_ref.refs_1_ = bf16[480,2048]{1,0:T(8,128)(2,1)S(1)} collective-permute-done((bf16[480,2048]{1,0:T(8,128)(2,1)}, bf16[480,2048]{1,0:T(8,128)(2,1)S(1)}, u32[]{:S(2)}, u32[]{:S(2)}) %collective-permute-start.8) | collective-permute-done | bytes 1966112 | tf_op jit(solution)/shard_map/ppermute | solution.py:48
  154.9 5.4 %all-to-all-start.1 = ((bf16[16,3,64,512]{3,2,1,0:T(8,128)(2,1)}), bf16[16,3,64,512]{3,2,1,0:T(8,128)(2,1)}, u32[]{:S(2)}, u32[]{:S(2)}) async-start(bf16[16,3,64,512]{3,2,1,0:T(8,128)(2,1)} %copy-done.1), calls=%async_computation.1 | async-start | bytes 6291456 | tf_op jit(solution)/shard_map/all_to_all | solution.py:52
  163.8 1.5 copy-done.3
  165.4 1.5 copy-done.5
  169.2 3.0 %collective-permute-start.13 = (bf16[2,64,1024]{2,1,0:T(8,128)(2,1)}, bf16[2,64,1024]{2,1,0:T(8,128)(2,1)S(1)}, u32[]{:S(2)}, u32[]{:S(2)}) collective-permute-start(bf16[2,64,1024]{2,1,0:T(8,128)(2,1)} %get-tuple-element.45), channel_id=1, source_target_pairs={{0,12},{1,13},{2,14},{3,15},{4,0},{5,1},{6,2},{7,3},{8,4},{9,5},{1... | collective-permute-start | bytes 786440 | tf_op jit(solution)/shard_map/ppermute | solution.py:48
  172.2 2.3 %collective-permute-start.15 = (bf16[2,64,1024]{2,1,0:T(8,128)(2,1)}, bf16[2,64,1024]{2,1,0:T(8,128)(2,1)}, u32[]{:S(2)}, u32[]{:S(2)}) collective-permute-start(bf16[2,64,1024]{2,1,0:T(8,128)(2,1)} %get-tuple-element.43), channel_id=1, source_target_pairs={{0,8},{1,9},{2,10},{3,11},{4,12},{5,13},{6,14},{7,15},{8,0},{9,1},... | collective-permute-start | bytes 786440 | tf_op jit(solution)/shard_map/ppermute | solution.py:48
  175.1 5.4 %shard_map.107.f_ref = bf16[384,2048]{1,0:T(8,128)(2,1)} custom-call(bf16[512,1024]{1,0:T(8,128)(2,1)} %collective-permute-done.refs_0_, bf16[512,1024]{1,0:T(8,128)(2,1)} %collective-permute-done.1.refs_1_, bf16[512,1024]{1,0:T(8,128)(2,1)} %collective-permute-done.2.refs_2_, bf16[512,1024]{1,0:T(8,128)(2,1)} %collective-permute-done.3.refs_3_, ...), custom_call_target="tpu_custom_call" | custom-call | flops 1610612736 | bytes 6553600 | tf_op jit(solution)/shard_map/pallas_call | solution.py:164
  180.5 4.9 %shard_map.108.rest_0_ = bf16[384,8192]{1,0:T(8,128)(2,1)} custom-call(s32[4]{0:T(128)} %get-tuple-element.47.b_ref, bf16[384,2048]{1,0:T(8,128)(2,1)} %shard_map.107.f_ref, bf16[3,128,64]{2,1,0:T(8,128)(2,1)} %copy-done.7, bf16[16,3,64,512]{3,2,1,0:T(8,128)(2,1)} %collective-permute-done.12.a_ref), custom_call_target="tpu_custom_call" | custom-call | flops 100663296 | bytes 3145728 | tf_op jit(solution)/shard_map/pallas_call | solution.py:264
  185.4 4.9 %shard_map.109.rest_0_ = bf16[384,8192]{1,0:T(8,128)(2,1)} custom-call(s32[4]{0:T(128)} %get-tuple-element.49.b_ref, bf16[480,2048]{1,0:T(8,128)(2,1)} %copy-done.2, bf16[3,128,64]{2,1,0:T(8,128)(2,1)} %copy-done.7, bf16[16,3,64,512]{3,2,1,0:T(8,128)(2,1)} %collective-permute-done.12.a_ref, ...), custom_call_target="tpu_custom_call", output_to_operand_aliasing={{}: (4, {})} | custom-call | flops 100663296 | bytes 3145728 | tf_op jit(solution)/shard_map/pallas_call | solution.py:264
  190.2 4.9 %shard_map.110.rest_0_ = bf16[384,8192]{1,0:T(8,128)(2,1)} custom-call(s32[4]{0:T(128)} %get-tuple-element.48.b_ref, bf16[480,2048]{1,0:T(8,128)(2,1)} %copy-done.4, bf16[3,128,64]{2,1,0:T(8,128)(2,1)} %copy-done.7, bf16[16,3,64,512]{3,2,1,0:T(8,128)(2,1)} %collective-permute-done.12.a_ref, ...), custom_call_target="tpu_custom_call", output_to_operand_aliasing={{}: (4, {})} | custom-call | flops 100663296 | bytes 3145728 | tf_op jit(solution)/shard_map/pallas_call | solution.py:264
  195.1 4.9 %shard_map.111 = bf16[384,8192]{1,0:T(8,128)(2,1)} custom-call(s32[4]{0:T(128)} %get-tuple-element.50.b_ref, bf16[480,2048]{1,0:T(8,128)(2,1)} %collective-permute-done.11.f_ref.refs_3_, bf16[3,128,64]{2,1,0:T(8,128)(2,1)} %copy-done.7, bf16[16,3,64,512]{3,2,1,0:T(8,128)(2,1)} %collective-permute-done.12.a_ref, ...), custom_call_target="tpu_custom_call", output_to_operand_aliasing={{}: (4, {})} | custom-call | flops 100663296 | bytes 3145728 | tf_op jit(solution)/shard_map/pallas_call | solution.py:264
  200.0 2.0 add_multiply_fusion
  202.0 5.7 %shard_map.113 = f32[32,64,512]{2,1,0:T(8,128)} custom-call(s32[48]{0:T(128)} %bitcast.38, bf16[16,3,64,512]{3,2,1,0:T(8,128)(2,1)} %all-to-all-done.1.p_ref), custom_call_target="tpu_custom_call" | custom-call | flops 1572864 | bytes 7340032 | tf_op jit(solution)/shard_map/pallas_call | solution.py:226
  (61 shorter events, 15.0 us)
Async XLA Ops:
  0.6 1.6 copy-start
  4.8 14.1 %copy-start.6 = (bf16[1,384,1024]{2,1,0:T(8,128)(2,1)S(1)}, bf16[1,384,1024]{2,1,0:T(8,128)(2,1)}, u32[]{:S(2)}) copy-start(bf16[1,384,1024]{2,1,0:T(8,128)(2,1)} %param.9) | copy-start | bytes 2359300
  4.8 16.2 %copy-start.10 = (s32[1,48]{1,0:T(1,128)S(1)}, s32[1,48]{1,0:T(1,128)}, u32[]{:S(2)}) copy-start(s32[1,48]{1,0:T(1,128)} %param.13) | copy-start | bytes 580
  4.8 77.0 %all-to-all-start = ((bf16[16,3,64,512]{3,2,1,0:T(8,128)(2,1)}), bf16[16,3,64,512]{3,2,1,0:T(8,128)(2,1)}, u32[]{:S(2)}, u32[]{:S(2)}) async-start(bf16[16,3,64,512]{3,2,1,0:T(8,128)(2,1)} %bitcast.33), calls=%async_computation | async-start | bytes 6291456 | tf_op jit(solution)/shard_map/all_to_all | solution.py:52
  12.8 32.2 %collective-permute-start = (bf16[512,1024]{1,0:T(8,128)(2,1)}, bf16[512,1024]{1,0:T(8,128)(2,1)}, u32[]{:S(2)}, u32[]{:S(2)}) collective-permute-start(bf16[512,1024]{1,0:T(8,128)(2,1)} %bitcast.39), channel_id=1, source_target_pairs={{16,0},{17,1},{18,2},{19,3},{20,4},{21,5},{22,6},{23,7},{24,8},{25... | collective-permute-start | bytes 3145736 | tf_op jit(solution)/shard_map/ppermute | solution.py:48
  14.8 61.2 %collective-permute-start.1 = (bf16[512,1024]{1,0:T(8,128)(2,1)}, bf16[512,1024]{1,0:T(8,128)(2,1)}, u32[]{:S(2)}, u32[]{:S(2)}) collective-permute-start(bf16[512,1024]{1,0:T(8,128)(2,1)} %bitcast.40), channel_id=1, source_target_pairs={{16,4},{17,5},{18,6},{19,7},{20,8},{21,9},{22,10},{23,11},{24,12},... | collective-permute-start | bytes 3145736 | tf_op jit(solution)/shard_map/ppermute | solution.py:48
  18.8 24.9 %collective-permute-start.4 = (bf16[384,1024]{1,0:T(8,128)(2,1)S(1)}, bf16[384,1024]{1,0:T(8,128)(2,1)}, u32[]{:S(2)}, u32[]{:S(2)}) collective-permute-start(bf16[384,1024]{1,0:T(8,128)(2,1)S(1)} %bitcast.27), channel_id=1, source_target_pairs={{16,0},{32,16},{48,32},{64,48},{80,64},{96,80},{112,96},{17,1},{33... | collective-permute-start | bytes 2359304 | tf_op jit(solution)/shard_map/ppermute | solution.py:29
  26.1 10.7 %collective-permute-start.7 = (bf16[3,128,64]{2,1,0:T(8,128)(2,1)S(1)}, bf16[3,128,64]{2,1,0:T(8,128)(2,1)S(1)}, u32[]{:S(2)}, u32[]{:S(2)}) collective-permute-start(bf16[3,128,64]{2,1,0:T(8,128)(2,1)S(1)} %bitcast.36), channel_id=1, source_target_pairs={{16,0},{32,16},{48,32},{64,48},{80,64},{96,80},{112,96},{17,1},{33... | collective-permute-start | bytes 147464 | tf_op jit(solution)/shard_map/ppermute | solution.py:29
  28.4 59.2 %collective-permute-start.2 = (bf16[512,1024]{1,0:T(8,128)(2,1)}, bf16[512,1024]{1,0:T(8,128)(2,1)}, u32[]{:S(2)}, u32[]{:S(2)}) collective-permute-start(bf16[512,1024]{1,0:T(8,128)(2,1)} %bitcast.41), channel_id=1, source_target_pairs={{16,12},{17,13},{18,14},{19,15},{20,0},{21,1},{22,2},{23,3},{24,4}... | collective-permute-start | bytes 3145736 | tf_op jit(solution)/shard_map/ppermute | solution.py:48
  36.7 43.4 %copy-start.7 = (bf16[3,128,64]{2,1,0:T(8,128)(2,1)}, bf16[3,128,64]{2,1,0:T(8,128)(2,1)S(1)}, u32[]{:S(2)}) copy-start(bf16[3,128,64]{2,1,0:T(8,128)(2,1)S(1)} %collective-permute-done.7.low_ref) | copy-start | bytes 147460
  36.7 50.8 %collective-permute-start.3 = (bf16[512,1024]{1,0:T(8,128)(2,1)}, bf16[512,1024]{1,0:T(8,128)(2,1)}, u32[]{:S(2)}, u32[]{:S(2)}) collective-permute-start(bf16[512,1024]{1,0:T(8,128)(2,1)} %bitcast.42), channel_id=1, source_target_pairs={{16,8},{17,9},{18,10},{19,11},{20,12},{21,13},{22,14},{23,15},{24,... | collective-permute-start | bytes 3145736 | tf_op jit(solution)/shard_map/ppermute | solution.py:48
  43.8 53.5 %collective-permute-start.5 = (bf16[384,1024]{1,0:T(8,128)(2,1)}, bf16[384,1024]{1,0:T(8,128)(2,1)}, u32[]{:S(2)}, u32[]{:S(2)}) collective-permute-start(bf16[384,1024]{1,0:T(8,128)(2,1)} %collective-permute-done.4.refs_4_), channel_id=1, source_target_pairs={{0,3},{1,0},{2,1},{3,2},{4,7},{5,4},{6,5},{7,6},{8,11},{9,8},{10,9... | collective-permute-start | bytes 2359304 | tf_op jit(solution)/shard_map/ppermute | solution.py:48
  45.0 52.2 %collective-permute-start.6 = (bf16[384,1024]{1,0:T(8,128)(2,1)}, bf16[384,1024]{1,0:T(8,128)(2,1)}, u32[]{:S(2)}, u32[]{:S(2)}) collective-permute-start(bf16[384,1024]{1,0:T(8,128)(2,1)} %collective-permute-done.4.refs_4_), channel_id=1, source_target_pairs={{0,1},{1,2},{2,3},{3,0},{4,5},{5,6},{6,7},{7,4},{8,9},{9,10},{10,1... | collective-permute-start | bytes 2359304 | tf_op jit(solution)/shard_map/ppermute | solution.py:48
  76.0 32.5 %collective-permute-start.10 = (bf16[384,1024]{1,0:T(8,128)(2,1)}, bf16[384,1024]{1,0:T(8,128)(2,1)}, u32[]{:S(2)}, u32[]{:S(2)}) collective-permute-start(bf16[384,1024]{1,0:T(8,128)(2,1)} %collective-permute-done.4.refs_4_), channel_id=1, source_target_pairs={{0,2},{1,3},{2,0},{3,1},{4,6},{5,7},{6,4},{7,5},{8,10},{9,11},{10,... | collective-permute-start | bytes 2359304 | tf_op jit(solution)/shard_map/ppermute | solution.py:48
  80.2 1.6 copy-start.1
  105.2 47.1 %collective-permute-start.8 = (bf16[480,2048]{1,0:T(8,128)(2,1)}, bf16[480,2048]{1,0:T(8,128)(2,1)S(1)}, u32[]{:S(2)}, u32[]{:S(2)}) collective-permute-start(bf16[480,2048]{1,0:T(8,128)(2,1)} %get-tuple-element.25), channel_id=1, source_target_pairs={{0,1},{1,2},{2,3},{3,0},{4,5},{5,6},{6,7},{7,4},{8,9},{9,10},{10,1... | collective-permute-start | bytes 5898248 | tf_op jit(solution)/shard_map/ppermute | solution.py:48
  106.1 47.5 %collective-permute-start.9 = (bf16[480,2048]{1,0:T(8,128)(2,1)}, bf16[480,2048]{1,0:T(8,128)(2,1)S(1)}, u32[]{:S(2)}, u32[]{:S(2)}) collective-permute-start(bf16[480,2048]{1,0:T(8,128)(2,1)} %get-tuple-element.26), channel_id=1, source_target_pairs={{0,3},{1,0},{2,1},{3,2},{4,7},{5,4},{6,5},{7,6},{8,11},{9,8},{10,9... | collective-permute-start | bytes 5898248 | tf_op jit(solution)/shard_map/ppermute | solution.py:48
  114.0 47.7 %copy-start.9 = (s32[4]{0:T(128)S(1)}, s32[4]{0:T(128)}, u32[]{:S(2)}) copy-start(s32[4]{0:T(128)} %constant.112.clone) | copy-start | bytes 52
  114.0 48.4 %copy-start.8 = (s32[32]{0:T(128)S(1)}, s32[32]{0:T(128)}, u32[]{:S(2)}) copy-start(s32[32]{0:T(128)} %param.14) | copy-start | bytes 388
  114.0 41.0 %collective-permute-start.11 = (bf16[480,2048]{1,0:T(8,128)(2,1)}, bf16[480,2048]{1,0:T(8,128)(2,1)}, u32[]{:S(2)}, u32[]{:S(2)}) collective-permute-start(bf16[480,2048]{1,0:T(8,128)(2,1)} %shard_map.106), channel_id=1, source_target_pairs={{0,2},{1,3},{2,0},{3,1},{4,6},{5,7},{6,4},{7,5},{8,10},{9,11},{10,... | collective-permute-start | bytes 5898248 | tf_op jit(solution)/shard_map/ppermute | solution.py:48
  114.0 66.5 %collective-permute-start.12 = (bf16[16,3,64,512]{3,2,1,0:T(8,128)(2,1)}, bf16[16,3,64,512]{3,2,1,0:T(8,128)(2,1)}, u32[]{:S(2)}, u32[]{:S(2)}) collective-permute-start(bf16[16,3,64,512]{3,2,1,0:T(8,128)(2,1)} %all-to-all-done.a_ref), channel_id=1, source_target_pairs={{16,0},{32,16},{48,32},{64,48},{80,64},{96,80},{112,96},{17,1},{33... | collective-permute-start | bytes 9437192 | tf_op jit(solution)/shard_map/ppermute | solution.py:29
  152.4 1.3 copy-start.2
  153.7 1.3 copy-start.4
  154.9 47.1 %all-to-all-start.1 = ((bf16[16,3,64,512]{3,2,1,0:T(8,128)(2,1)}), bf16[16,3,64,512]{3,2,1,0:T(8,128)(2,1)}, u32[]{:S(2)}, u32[]{:S(2)}) async-start(bf16[16,3,64,512]{3,2,1,0:T(8,128)(2,1)} %copy-done.1), calls=%async_computation.1 | async-start | bytes 6291456 | tf_op jit(solution)/shard_map/all_to_all | solution.py:52
  163.8 1.5 copy-start.3
  165.3 1.5 copy-start.5
  169.2 30.8 %collective-permute-start.13 = (bf16[2,64,1024]{2,1,0:T(8,128)(2,1)}, bf16[2,64,1024]{2,1,0:T(8,128)(2,1)S(1)}, u32[]{:S(2)}, u32[]{:S(2)}) collective-permute-start(bf16[2,64,1024]{2,1,0:T(8,128)(2,1)} %get-tuple-element.45), channel_id=1, source_target_pairs={{0,12},{1,13},{2,14},{3,15},{4,0},{5,1},{6,2},{7,3},{8,4},{9,5},{1... | collective-permute-start | bytes 786440 | tf_op jit(solution)/shard_map/ppermute | solution.py:48
  172.2 27.8 %collective-permute-start.14 = (bf16[2,64,1024]{2,1,0:T(8,128)(2,1)}, bf16[2,64,1024]{2,1,0:T(8,128)(2,1)}, u32[]{:S(2)}, u32[]{:S(2)}) collective-permute-start(bf16[2,64,1024]{2,1,0:T(8,128)(2,1)} %get-tuple-element.44), channel_id=1, source_target_pairs={{0,4},{1,5},{2,6},{3,7},{4,8},{5,9},{6,10},{7,11},{8,12},{9,13},{1... | collective-permute-start | bytes 786440 | tf_op jit(solution)/shard_map/ppermute | solution.py:48
  172.2 27.8 %collective-permute-start.15 = (bf16[2,64,1024]{2,1,0:T(8,128)(2,1)}, bf16[2,64,1024]{2,1,0:T(8,128)(2,1)}, u32[]{:S(2)}, u32[]{:S(2)}) collective-permute-start(bf16[2,64,1024]{2,1,0:T(8,128)(2,1)} %get-tuple-element.43), channel_id=1, source_target_pairs={{0,8},{1,9},{2,10},{3,11},{4,12},{5,13},{6,14},{7,15},{8,0},{9,1},... | collective-permute-start | bytes 786440 | tf_op jit(solution)/shard_map/ppermute | solution.py:48

commit v3 on v2

--- a/solution.py
+++ b/solution.py
@@ -8,7 +8,7 @@
 GROUP_ROWS = 128
 ADAPTER_SCALE = 2.0
 WIDE = 4
-PARAMS = pltpu.CompilerParams(vmem_limit_bytes=48 * 2**20)
+PARAMS = pltpu.CompilerParams(vmem_limit_bytes=58 * 2**20)
 RING = 4
 
 F32 = jnp.float32
@@ -138,38 +138,67 @@
     )(x, down, v)
 
 
-def frozen_terms(stacks, weights, tail=None, with_tail=0):
-    rows, kv = stacks[0].shape
-    width = sum(w.shape[0] for w in weights)
-    extra = tail.shape[0] if with_tail else 0
-    heights = [rows + (extra if i < with_tail else 0) for i in range(len(stacks))]
-    tails = [tail] if with_tail else []
+def frozen_terms(stacks, weights, tail=None):
+    kv = weights[0].shape[1]
+    rows = stacks[0].shape[0]
+    n_w, n_out = len(weights), len(stacks)
+    cols = weights[0].shape[0]
+    extra = 0 if tail is None else tail.shape[0]
+    height, width = rows + extra, n_w * cols
+    tails = [] if tail is None else [tail]
 
     def body(*refs):
-        w_refs, refs = refs[: len(weights)], refs[len(weights) :]
-        v_refs, refs = refs[: len(stacks)], refs[len(stacks) :]
-        o_refs = refs[len(tails) :]
-        for i, (v_ref, o_ref) in enumerate(zip(v_refs, o_refs)):
-            left = 0
-            for w_ref in w_refs:
-                span = slice(left, left + w_ref.shape[0])
-                o_ref[:rows, span] = dot(v_ref[...], w_ref[...], NT).astype(BF16)
-                left += w_ref.shape[0]
-            if i < with_tail:
-                o_ref[rows:, :] = refs[0][...]
-
-    def whole(shape):
-        return pl.BlockSpec(shape, lambda i: (0, 0))
-
-    return pl.pallas_call(
-        body,
-        grid=(1,),
-        in_specs=[whole(a.shape) for a in (*weights, *stacks, *tails)],
-        out_specs=[whole((h, width)) for h in heights],
-        out_shape=[jax.ShapeDtypeStruct((h, width), BF16) for h in heights],
+        w_hbm, refs = refs[:n_w], refs[n_w:]
+        v_hbm, refs = refs[:n_out], refs[n_out:]
+        tail_refs, refs = refs[: len(tails)], refs[len(tails) :]
+        out_hbm, refs = refs[:n_out], refs[n_out:]
+        w_vmem, v_vmem, out_vmem, w_sem, v_sem, out_sem = refs
+        w_loads = [
+            pltpu.make_async_copy(w_hbm[q], w_vmem.at[q], w_sem.at[q]) for q in range(n_w)
+        ]
+        v_loads = [
+            pltpu.make_async_copy(v_hbm[i], v_vmem.at[i], v_sem.at[i]) for i in range(n_out)
+        ]
+        w_loads[0].start()
+        for load in v_loads + w_loads[1:2]:
+            load.start()
+        stores = []
+        for q in range(n_w):
+            w_loads[q].wait()
+            if q + 2 < n_w:
+                w_loads[q + 2].start()
+            span = slice(q * cols, (q + 1) * cols)
+            for i in range(n_out):
+                if q == 0:
+                    v_loads[i].wait()
+                out_vmem[i, q, :rows, :] = dot(v_vmem[i], w_vmem[q], NT).astype(BF16)
+                if tail_refs:
+                    out_vmem[i, q, rows:, :] = tail_refs[0][:, span]
+                store = pltpu.make_async_copy(
+                    out_vmem.at[i, q], out_hbm[i].at[:, span], out_sem.at[i, q]
+                )
+                store.start()
+                stores.append(store)
+        for store in stores:
+            store.wait()
+
+    return pl.pallas_call(
+        body,
+        in_specs=[pl.BlockSpec(memory_space=pl.ANY)] * (n_w + n_out)
+        + [pl.BlockSpec(memory_space=pltpu.VMEM)] * len(tails),
+        out_specs=[pl.BlockSpec(memory_space=pl.ANY)] * n_out,
+        out_shape=[jax.ShapeDtypeStruct((height, width), BF16)] * n_out,
+        scratch_shapes=[
+            pltpu.VMEM((n_w, cols, kv), BF16),
+            pltpu.VMEM((n_out, rows, kv), BF16),
+            pltpu.VMEM((n_out, n_w, height, cols), BF16),
+            pltpu.SemaphoreType.DMA((n_w,)),
+            pltpu.SemaphoreType.DMA((n_out,)),
+            pltpu.SemaphoreType.DMA((n_out, n_w)),
+        ],
         compiler_params=PARAMS,
         cost_estimate=cost(
-            2 * sum(heights) * kv * width, 2 * (sum(heights) * (kv + width) + kv * width)
+            2 * n_out * height * kv * width, 2 * (n_out * height * (kv + width) + kv * width)
         ),
     )(*weights, *stacks, *tails)
 
@@ -211,7 +240,7 @@
 
 def sum_by_tenant(parts, tenants, n_tenants):
     n, groups, rank, cols = parts.shape
-    steps = 4
+    steps = 2
     r = rank // steps
     scale = ADAPTER_SCALE / GROUP_ROWS
 
@@ -232,47 +261,47 @@
             out_specs=pl.BlockSpec((n_tenants, r, cols), lambda i, t: (0, i, 0)),
         ),
         out_shape=jax.ShapeDtypeStruct((n_tenants, rank, cols), F32),
+        compiler_params=PARAMS,
         cost_estimate=cost(
             n * groups * rank * cols, 2 * n * groups * rank * cols + 4 * n_tenants * rank * cols
         ),
     )(tenants, parts)
 
 
-def gradient_columns(out, blocks, frozen, low, down):
+def input_gradient(pieces, blocks, low, down):
     n, groups, rank, cols = down.shape
-    rows = groups * GROUP_ROWS
-    count = frozen.shape[1] // cols
-
-    def body(b_ref, f_ref, low_ref, a_ref, *rest):
-        o_ref = rest[-1]
-        for g in range(groups):
-            span = slice(g * GROUP_ROWS, (g + 1) * GROUP_ROWS)
-            adapter = jnp.dot(low_ref[g], a_ref[0, g], preferred_element_type=F32)
-            o_ref[span, :] = (f_ref[span, :].astype(F32) + ADAPTER_SCALE * adapter).astype(BF16)
-
-    in_specs = [
-        pl.BlockSpec((rows, cols), lambda i, b: (0, i)),
-        pl.BlockSpec((groups, GROUP_ROWS, rank), lambda i, b: (0, 0, 0)),
-        pl.BlockSpec((1, groups, rank, cols), lambda i, b: (b[i], 0, 0, 0)),
-    ]
-    args = [blocks, frozen, low, down]
-    aliases = {}
-    if out is not None:
-        in_specs.append(pl.BlockSpec(memory_space=pl.ANY))
-        aliases = {len(args): 0}
-        args.append(out)
+    per = n // len(pieces)
+    width = n * cols
+
+    def body(b_ref, low_ref, a_ref, *refs):
+        o_ref = refs[-1]
+        for p, f_ref in enumerate(refs[:-1]):
+            for i in range(per):
+                block = b_ref[p * per + i]
+                adapter = jnp.dot(low_ref[0], a_ref[block, 0], preferred_element_type=F32)
+                place = pl.ds(pl.multiple_of(block * cols, cols), cols)
+                frozen = f_ref[:, i * cols : (i + 1) * cols].astype(F32)
+                o_ref[:, place] = (frozen + ADAPTER_SCALE * adapter).astype(BF16)
+
     return pl.pallas_call(
         body,
         grid_spec=pltpu.PrefetchScalarGridSpec(
             num_scalar_prefetch=1,
-            grid=(count,),
-            in_specs=in_specs,
-            out_specs=pl.BlockSpec((rows, cols), lambda i, b: (0, b[i])),
-        ),
-        out_shape=jax.ShapeDtypeStruct((rows, n * cols), BF16),
-        input_output_aliases=aliases,
-        cost_estimate=cost(2 * rows * rank * cols * count, 4 * count * rows * cols),
-    )(*args)
+            grid=(groups,),
+            in_specs=[
+                pl.BlockSpec((1, GROUP_ROWS, rank), lambda g, b: (g, 0, 0)),
+                pl.BlockSpec((n, 1, rank, cols), lambda g, b: (0, g, 0, 0)),
+            ]
+            + [pl.BlockSpec((GROUP_ROWS, per * cols), lambda g, b: (g, 0)) for _ in pieces],
+            out_specs=pl.BlockSpec((GROUP_ROWS, width), lambda g, b: (g, 0)),
+        ),
+        out_shape=jax.ShapeDtypeStruct((groups * GROUP_ROWS, width), BF16),
+        compiler_params=PARAMS,
+        cost_estimate=cost(
+            2 * groups * GROUP_ROWS * rank * width,
+            2 * groups * (2 * GROUP_ROWS + rank) * width,
+        ),
+    )(blocks, low, down, *pieces)
 
 
 def local(
@@ -302,23 +331,22 @@
         up[my_tenants],
         preferred_element_type=F32,
     ).astype(BF16)
+    v_below, v_above, v_far = (move(v_next, "row", step) for step in (1, -1, 2))
+    parts = up_parts(x, down_mine, v)
+    for_above, for_below = frozen_terms((v_above, v_below), weights, parts)
+    from_below, from_above = move(for_above, "row", 1), move(for_below, "row", -1)
+    (for_far,) = frozen_terms((v_far,), weights, parts)
+    down_mine, low, for_above = together(down_mine, low, for_above)
+    down_next = to_previous_section(down_mine)
     low_next = to_previous_section(low)
+    from_far = move(for_far, "row", 2)
+    low, for_far = together(low, for_far)
     sent = group_terms(x, jnp.swapaxes(low, 1, 2))
-    v_below, v_above, v_far = (move(v_next, "row", step) for step in (1, -1, 2))
-    x, sent = together(x, sent)
-
-    parts = up_parts(x, down_mine, v)
-    parts, low_next = together(parts, low_next)
-    down_next = to_previous_section(down_mine)
-    for_above, for_below = frozen_terms((v_above, v_below), weights, parts, 2)
-    from_below, from_above = move(for_above, "row", 1), move(for_below, "row", -1)
-    (for_far,) = frozen_terms((v_far,), weights, parts, 1)
-    from_far = move(for_far, "row", 2)
-    sent, from_below, from_above, from_far, v_next = together(
-        sent, from_below, from_above, from_far, v_next
+    (own,) = frozen_terms((v_next,), weights)
+    sent, from_below, from_above, from_far, own = together(
+        sent, from_below, from_above, from_far, own
     )
     terms = exchange(sent)
-    (own,) = frozen_terms((v_next,), weights)
 
     odd = lax.axis_index("section") % 2 == 1
     mz, mx = me // RING, me % RING
@@ -344,11 +372,10 @@
     mine, to_below, to_above, to_far = by_slot.reshape(RING, per, rank, kv)
     from_up = (move(to_below, "col", -1), move(to_above, "col", 1), move(to_far, "col", 2))
 
-    out = None
-    for piece, step in ((own, 0), (from_below, -1), (from_above, 1), (from_far, 2)):
-        blocks = device_at((row + step) % RING, (col + steps) % RING)
-        out = gradient_columns(out, blocks, piece, low_next, down_next)
-
+    blocks = jnp.concatenate(
+        [device_at((row + step) % RING, (col + steps) % RING) for step in (0, -1, 1, 2)]
+    )
+    out = input_gradient((own, from_below, from_above, from_far), blocks, low_next, down_next)
     out, *from_up = together(out, *from_up)
     up_grad = sum((block.astype(F32) for block in from_up), mine.astype(F32))
     up_grad = up_grad * (ADAPTER_SCALE / GROUP_ROWS)

time: 209 us -> 205 us (0.981)
  waiting for transfers between devices: 80.3 us -> 93.6 us
  Pallas kernels: 55.3 us -> 47.1 us
  local copies, waits for them, and re-layouts: 17.1 us -> 11.6 us
  starting transfers between devices: 47.8 us -> 44.8 us
    pallas_call x7 -> x4, Pallas kernels: 38.3 us -> 27.3 us  [the longest x3 18.7 us: frozen_terms(): pl.pallas_call(body, in_specs=[pl.BlockSpec(memory_space=pl.ANY)] * (n_w...]
    ppermute x13, waiting for transfers between devices: 76.1 us -> 85.9 us  [move(): return lax.ppermute(block, ('section', 'dp'), along(axis, distance, down))]
    unnamed x23 -> x17, local copies, waits for them, and re-layouts: 8.61 us -> 2.83 us
    ppermute x3, waiting for transfers between devices: 4.17 us -> 7.7 us  [to_previous_section(): return lax.ppermute(block, 'section', [(i, i - 1) for i in range(1, n)])]
    ppermute x13, starting transfers between devices: 27.9 us -> 25.5 us  [move(): return lax.ppermute(block, ('section', 'dp'), along(axis, distance, down))]
  transfers between devices with their start and end apart: 18 -> 18, of which waited for: 4 -> 7; matrix products, arithmetic and copies ran while one was open for 6% -> 6% of each run, Pallas kernels for 24% -> 21%
where the time goes in v3:
time: 205 us; the launch traced here: 204 us
  waiting for transfers between devices  93.6 us (46%)
  Pallas kernels  47.1 us (23%)
  starting transfers between devices  44.8 us (22%)
  local copies, waits for them, and re-layouts  11.6 us (6%)
  other arithmetic  5.32 us (3%)
    ppermute x13, waiting for transfers between devices, move(): return lax.ppermute(block, ('section', 'dp'), along(axis, distance, down))  85.9 us
    ppermute x13, starting transfers between devices, move(): return lax.ppermute(block, ('section', 'dp'), along(axis, distance, down))  25.5 us
    pallas_call x3, Pallas kernels, frozen_terms(): pl.pallas_call(body, in_specs=[pl.BlockSpec(memory_space=pl.ANY)] * (n_w...  18.7 us
    all_to_all x2, starting transfers between devices, exchange(): return lax.all_to_all(blocks, 'dp', split_axis=0, concat_axis=0, tiled=True)  12.7 us
    pallas_call x1, Pallas kernels, input_gradient(): pl.pallas_call(body, grid_spec=pltpu.PrefetchScalarGridSpec(num_scalar_pr...  8.66 us
    ppermute x3, waiting for transfers between devices, to_previous_section(): return lax.ppermute(block, 'section', [(i, i - 1) for i in range(1, n)])  7.7 us
    pallas_call x1, Pallas kernels, up_parts(): pl.pallas_call(body, grid=(n // WIDE,), in_specs=[pl.BlockSpec((rows, WID...  6.72 us
    ppermute x3, starting transfers between devices, to_previous_section(): return lax.ppermute(block, 'section', [(i, i - 1) for i in range(1, n)])  6.59 us
  transfers between devices with their start and end apart: 18, of which 7 were waited for; matrix products, arithmetic and copies ran while one was open for 6% of the time, Pallas kernels for 21%

profile of v3, /device:TPU:24, one launch (start us, length us, event | category | flops | bytes accessed | tf_op | source)
XLA Modules:
  0.0 203.8 jit_solution(5584574242536201621)
XLA Ops:
  2.2 2.5 %gather_fusion = bf16[48,64,512]{2,1,0:T(8,128)(2,1)} fusion(bf16[32,64,512]{2,1,0:T(8,128)(2,1)S(1)} %bitcast.27, s32[1024]{0:T(1024)S(1)} %pad_clamp_fusion.3), kind=kCustom, calls=%fused_computation | custom fusion | bytes 6291648 | tf_op jit(solution)/shard_map/gather | solution.py:326
  4.8 8.1 %all-to-all-start = ((bf16[16,3,64,512]{3,2,1,0:T(8,128)(2,1)}), bf16[16,3,64,512]{3,2,1,0:T(8,128)(2,1)}, u32[]{:S(2)}, u32[]{:S(2)}) async-start(bf16[16,3,64,512]{3,2,1,0:T(8,128)(2,1)} %bitcast.30), calls=%async_computation | async-start | bytes 6291456 | tf_op jit(solution)/shard_map/all_to_all | solution.py:52
  12.8 1.9 collective-permute-start
  14.8 2.8 %collective-permute-start.4 = (bf16[384,1024]{1,0:T(8,128)(2,1)S(1)}, bf16[384,1024]{1,0:T(8,128)(2,1)}, u32[]{:S(2)}, u32[]{:S(2)}) collective-permute-start(bf16[384,1024]{1,0:T(8,128)(2,1)S(1)} %bitcast.34), channel_id=1, source_target_pairs={{16,0},{32,16},{48,32},{64,48},{80,64},{96,80},{112,96},{17,1},{33... | collective-permute-start | bytes 2359304 | tf_op jit(solution)/shard_map/ppermute | solution.py:29
  17.5 3.2 %collective-permute-start.1 = (bf16[512,1024]{1,0:T(8,128)(2,1)}, bf16[512,1024]{1,0:T(8,128)(2,1)}, u32[]{:S(2)}, u32[]{:S(2)}) collective-permute-start(bf16[512,1024]{1,0:T(8,128)(2,1)} %bitcast.41), channel_id=1, source_target_pairs={{16,4},{17,5},{18,6},{19,7},{20,8},{21,9},{22,10},{23,11},{24,12},... | collective-permute-start | bytes 3145736 | tf_op jit(solution)/shard_map/ppermute | solution.py:48
  20.8 4.7 %collective-permute-start.2 = (bf16[512,1024]{1,0:T(8,128)(2,1)}, bf16[512,1024]{1,0:T(8,128)(2,1)}, u32[]{:S(2)}, u32[]{:S(2)}) collective-permute-start(bf16[512,1024]{1,0:T(8,128)(2,1)} %bitcast.42), channel_id=1, source_target_pairs={{16,12},{17,13},{18,14},{19,15},{20,0},{21,1},{22,2},{23,3},{24,4}... | collective-permute-start | bytes 3145736 | tf_op jit(solution)/shard_map/ppermute | solution.py:48
  25.5 4.0 %collective-permute-start.3 = (bf16[512,1024]{1,0:T(8,128)(2,1)}, bf16[512,1024]{1,0:T(8,128)(2,1)}, u32[]{:S(2)}, u32[]{:S(2)}) collective-permute-start(bf16[512,1024]{1,0:T(8,128)(2,1)} %bitcast.43), channel_id=1, source_target_pairs={{16,8},{17,9},{18,10},{19,11},{20,12},{21,13},{22,14},{23,15},{24,... | collective-permute-start | bytes 3145736 | tf_op jit(solution)/shard_map/ppermute | solution.py:48
  29.6 6.1 %collective-permute-done.4.refs_4_ = bf16[384,1024]{1,0:T(8,128)(2,1)} collective-permute-done((bf16[384,1024]{1,0:T(8,128)(2,1)S(1)}, bf16[384,1024]{1,0:T(8,128)(2,1)}, u32[]{:S(2)}, u32[]{:S(2)}) %collective-permute-start.4) | collective-permute-done | bytes 786464 | tf_op jit(solution)/shard_map/ppermute | solution.py:29
  35.7 3.1 %collective-permute-start.5 = (bf16[384,1024]{1,0:T(8,128)(2,1)}, bf16[384,1024]{1,0:T(8,128)(2,1)S(1)}, u32[]{:S(2)}, u32[]{:S(2)}) collective-permute-start(bf16[384,1024]{1,0:T(8,128)(2,1)} %collective-permute-done.4.refs_4_), channel_id=1, source_target_pairs={{0,3},{1,0},{2,1},{3,2},{4,7},{5,4},{6,5},{7,6},{8,11},{9,8},{10,9... | collective-permute-start | bytes 2359304 | tf_op jit(solution)/shard_map/ppermute | solution.py:48
  38.8 37.2 %collective-permute-done.1.refs_1_ = bf16[512,1024]{1,0:T(8,128)(2,1)} collective-permute-done((bf16[512,1024]{1,0:T(8,128)(2,1)}, bf16[512,1024]{1,0:T(8,128)(2,1)}, u32[]{:S(2)}, u32[]{:S(2)}) %collective-permute-start.1) | collective-permute-done | bytes 1048608 | tf_op jit(solution)/shard_map/ppermute | solution.py:48
  76.0 6.7 %shard_map.103.refs_6_.refs_5_.refs_0_ = bf16[96,2048]{1,0:T(8,128)(2,1)} custom-call(bf16[384,8192]{1,0:T(8,128)(2,1)} %bitcast.28, bf16[16,3,64,512]{3,2,1,0:T(8,128)(2,1)} %all-to-all-done.a_ref, bf16[384,1024]{1,0:T(8,128)(2,1)} %bitcast.33), custom_call_target="tpu_custom_call" | custom-call | flops 402653184 | bytes 9437184 | tf_op jit(solution)/shard_map/pallas_call | solution.py:125
  82.7 4.5 %collective-permute-done.3.refs_3_ = bf16[512,1024]{1,0:T(8,128)(2,1)} collective-permute-done((bf16[512,1024]{1,0:T(8,128)(2,1)}, bf16[512,1024]{1,0:T(8,128)(2,1)}, u32[]{:S(2)}, u32[]{:S(2)}) %collective-permute-start.3) | collective-permute-done | bytes 1048608 | tf_op jit(solution)/shard_map/ppermute | solution.py:48
  87.3 9.9 %collective-permute-done.5.refs_4_ = bf16[384,1024]{1,0:T(8,128)(2,1)S(1)} collective-permute-done((bf16[384,1024]{1,0:T(8,128)(2,1)}, bf16[384,1024]{1,0:T(8,128)(2,1)S(1)}, u32[]{:S(2)}, u32[]{:S(2)}) %collective-permute-start.5) | collective-permute-done | bytes 786464 | tf_op jit(solution)/shard_map/ppermute | solution.py:48
  98.0 7.7 %shard_map.104 = (bf16[480,2048]{1,0:T(8,128)(2,1)}, bf16[480,2048]{1,0:T(8,128)(2,1)}) custom-call(bf16[512,1024]{1,0:T(8,128)(2,1)} %collective-permute-done.refs_0_, bf16[512,1024]{1,0:T(8,128)(2,1)} %collective-permute-done.1.refs_1_, bf16[512,1024]{1,0:T(8,128)(2,1)} %collective-permute-done.2.refs_2_, ...), custom_call_target="tpu_custom_call" | custom-call | flops 4026531840 | bytes 10092544 | tf_op jit(solution)/shard_map/pallas_call | solution.py:185
  105.9 3.1 %collective-permute-start.11 = (bf16[480,2048]{1,0:T(8,128)(2,1)}, bf16[480,2048]{1,0:T(8,128)(2,1)}, u32[]{:S(2)}, u32[]{:S(2)}) collective-permute-start(bf16[480,2048]{1,0:T(8,128)(2,1)} %get-tuple-element.25), channel_id=1, source_target_pairs={{0,3},{1,0},{2,1},{3,2},{4,7},{5,4},{6,5},{7,6},{8,11},{9,8},{10,9... | collective-permute-start | bytes 5898248 | tf_op jit(solution)/shard_map/ppermute | solution.py:48
  109.0 6.1 %shard_map.105 = bf16[480,2048]{1,0:T(8,128)(2,1)} custom-call(bf16[512,1024]{1,0:T(8,128)(2,1)} %collective-permute-done.refs_0_, bf16[512,1024]{1,0:T(8,128)(2,1)} %collective-permute-done.1.refs_1_, bf16[512,1024]{1,0:T(8,128)(2,1)} %collective-permute-done.2.refs_2_, bf16[512,1024]{1,0:T(8,128)(2,1)} %collective-permute-done.3.refs_3_, ...), custom_call_target="tpu_custom_call" | custom-call | flops 2013265920 | bytes 7143424 | tf_op jit(solution)/shard_map/pallas_call | solution.py:185
  115.3 2.8 %gather_fusion.1 = bf16[3,64,1024]{2,1,0:T(8,128)(2,1)S(1)} fusion(bf16[32,64,1024]{2,1,0:T(8,128)(2,1)} %bitcast.38, s32[1024]{0:T(1024)S(1)} %pad_clamp_fusion.2), kind=kCustom, calls=%fused_computation.1 | custom fusion | bytes 786444 | tf_op jit(solution)/shard_map/gather | solution.py:331
  118.6 1.9 collective-permute-start.8
  120.5 4.9 %shard_map.107.refs_0_ = bf16[384,2048]{1,0:T(8,128)(2,1)} custom-call(bf16[512,1024]{1,0:T(8,128)(2,1)} %collective-permute-done.refs_0_, bf16[512,1024]{1,0:T(8,128)(2,1)} %collective-permute-done.1.refs_1_, bf16[512,1024]{1,0:T(8,128)(2,1)} %collective-permute-done.2.refs_2_, bf16[512,1024]{1,0:T(8,128)(2,1)} %collective-permute-done.3.refs_3_, ...), custom_call_target="tpu_custom_call" | custom-call | flops 1610612736 | bytes 6553600 | tf_op jit(solution)/shard_map/pallas_call | solution.py:185
  126.2 5.6 %shard_map.106 = bf16[16,3,64,512]{3,2,1,0:T(8,128)(2,1)} custom-call(bf16[384,8192]{1,0:T(8,128)(2,1)} %bitcast.29, bf16[3,64,128]{2,1,0:T(8,128)(2,1)} %copy.18.low_ref), custom_call_target="tpu_custom_call" | custom-call | flops 402653184 | bytes 9437184 | tf_op jit(solution)/shard_map/pallas_call | solution.py:74
  131.7 29.4 %collective-permute-done.10.refs_1_ = bf16[480,2048]{1,0:T(8,128)(2,1)} collective-permute-done((bf16[480,2048]{1,0:T(8,128)(2,1)}, bf16[480,2048]{1,0:T(8,128)(2,1)}, u32[]{:S(2)}, u32[]{:S(2)}) %collective-permute-start.10) | collective-permute-done | bytes 1966112 | tf_op jit(solution)/shard_map/ppermute | solution.py:48
  161.2 4.7 %all-to-all-start.1 = ((bf16[16,3,64,512]{3,2,1,0:T(8,128)(2,1)}), bf16[16,3,64,512]{3,2,1,0:T(8,128)(2,1)}, u32[]{:S(2)}, u32[]{:S(2)}) async-start(bf16[16,3,64,512]{3,2,1,0:T(8,128)(2,1)} %shard_map.106), calls=%async_computation.1 | async-start | bytes 6291456 | tf_op jit(solution)/shard_map/all_to_all | solution.py:52
  169.8 2.8 %shard_map.109 = bf16[8,64,1024]{2,1,0:T(8,128)(2,1)} custom-call(s32[12]{0:T(128)} %broadcast_select_fusion.6.place_ref, bf16[96,2048]{1,0:T(8,128)(2,1)} %shard_map.103.refs_6_.refs_5_.refs_0_, bf16[480,2048]{1,0:T(8,128)(2,1)} %collective-permute-done.10.refs_1_, bf16[480,2048]{1,0:T(8,128)(2,1)} %collective-permute-done.11.refs_2_, ...), custom_call_target="tpu_custom_call" | custom-call | flops 393216 | bytes 2621440 | tf_op jit(solution)/shard_map/pallas_call | solution.py:227
  172.7 1.2 fusion.4
  173.9 2.8 %collective-permute-start.13 = (bf16[2,64,1024]{2,1,0:T(8,128)(2,1)S(1)}, bf16[2,64,1024]{2,1,0:T(8,128)(2,1)S(1)}, u32[]{:S(2)}, u32[]{:S(2)}) collective-permute-start(bf16[2,64,1024]{2,1,0:T(8,128)(2,1)S(1)} %get-tuple-element.43), channel_id=1, source_target_pairs={{0,12},{1,13},{2,14},{3,15},{4,0},{5,1},{6,2},{7,3},{8,4},{9,5},{1... | collective-permute-start | bytes 786440 | tf_op jit(solution)/shard_map/ppermute | solution.py:48
  176.7 2.2 %collective-permute-start.15 = (bf16[2,64,1024]{2,1,0:T(8,128)(2,1)S(1)}, bf16[2,64,1024]{2,1,0:T(8,128)(2,1)S(1)}, u32[]{:S(2)}, u32[]{:S(2)}) collective-permute-start(bf16[2,64,1024]{2,1,0:T(8,128)(2,1)S(1)} %get-tuple-element.41), channel_id=1, source_target_pairs={{0,8},{1,9},{2,10},{3,11},{4,12},{5,13},{6,14},{7,15},{8,0},{9,1},... | collective-permute-start | bytes 786440 | tf_op jit(solution)/shard_map/ppermute | solution.py:48
  178.9 1.9 collective-permute-start.7
  181.4 1.6 collective-permute-done.7.low_ref
  183.7 8.7 %shard_map.108 = bf16[384,8192]{1,0:T(8,128)(2,1)} custom-call(s32[16]{0:T(128)} %pad_add_fusion.b_ref, bf16[3,128,64]{2,1,0:T(8,128)(2,1)} %copy-done.3, bf16[16,3,64,512]{3,2,1,0:T(8,128)(2,1)} %collective-permute-done.8.a_ref, bf16[384,2048]{1,0:T(8,128)(2,1)} %shard_map.107.refs_0_, bf16[480,2048]{1,0:T(8,128)(2,1)} %collective-permute-done.10.refs_1_, ...), custom_call_target="tpu_custom_call" | custom-call | flops 402653184 | bytes 15728640 | tf_op jit(solution)/shard_map/pallas_call | solution.py:286
  192.3 4.8 %collective-permute-done.14 = bf16[2,64,1024]{2,1,0:T(8,128)(2,1)S(1)} collective-permute-done((bf16[2,64,1024]{2,1,0:T(8,128)(2,1)S(1)}, bf16[2,64,1024]{2,1,0:T(8,128)(2,1)S(1)}, u32[]{:S(2)}, u32[]{:S(2)}) %collective-permute-start.14) | collective-permute-done | bytes 262176 | tf_op jit(solution)/shard_map/ppermute | solution.py:48
  197.2 1.9 add_multiply_fusion
  199.1 4.7 %shard_map.110 = f32[32,64,512]{2,1,0:T(8,128)} custom-call(s32[48]{0:T(128)} %bitcast.39, bf16[16,3,64,512]{3,2,1,0:T(8,128)(2,1)} %all-to-all-done.1.p_ref), custom_call_target="tpu_custom_call" | custom-call | flops 1572864 | bytes 7340032 | tf_op jit(solution)/shard_map/pallas_call | solution.py:255
  (54 shorter events, 9.3 us)
Async XLA Ops:
  0.6 1.6 copy-start
  4.8 10.0 %copy-start.1 = (bf16[1,384,1024]{2,1,0:T(8,128)(2,1)S(1)}, bf16[1,384,1024]{2,1,0:T(8,128)(2,1)}, u32[]{:S(2)}) copy-start(bf16[1,384,1024]{2,1,0:T(8,128)(2,1)} %param.9) | copy-start | bytes 2359300
  4.8 71.2 %all-to-all-start = ((bf16[16,3,64,512]{3,2,1,0:T(8,128)(2,1)}), bf16[16,3,64,512]{3,2,1,0:T(8,128)(2,1)}, u32[]{:S(2)}, u32[]{:S(2)}) async-start(bf16[16,3,64,512]{3,2,1,0:T(8,128)(2,1)} %bitcast.30), calls=%async_computation | async-start | bytes 6291456 | tf_op jit(solution)/shard_map/all_to_all | solution.py:52
  12.8 25.9 %collective-permute-start = (bf16[512,1024]{1,0:T(8,128)(2,1)}, bf16[512,1024]{1,0:T(8,128)(2,1)}, u32[]{:S(2)}, u32[]{:S(2)}) collective-permute-start(bf16[512,1024]{1,0:T(8,128)(2,1)} %bitcast.40), channel_id=1, source_target_pairs={{16,0},{17,1},{18,2},{19,3},{20,4},{21,5},{22,6},{23,7},{24,8},{25... | collective-permute-start | bytes 3145736 | tf_op jit(solution)/shard_map/ppermute | solution.py:48
  14.8 20.9 %collective-permute-start.4 = (bf16[384,1024]{1,0:T(8,128)(2,1)S(1)}, bf16[384,1024]{1,0:T(8,128)(2,1)}, u32[]{:S(2)}, u32[]{:S(2)}) collective-permute-start(bf16[384,1024]{1,0:T(8,128)(2,1)S(1)} %bitcast.34), channel_id=1, source_target_pairs={{16,0},{32,16},{48,32},{64,48},{80,64},{96,80},{112,96},{17,1},{33... | collective-permute-start | bytes 2359304 | tf_op jit(solution)/shard_map/ppermute | solution.py:29
  17.5 58.4 %collective-permute-start.1 = (bf16[512,1024]{1,0:T(8,128)(2,1)}, bf16[512,1024]{1,0:T(8,128)(2,1)}, u32[]{:S(2)}, u32[]{:S(2)}) collective-permute-start(bf16[512,1024]{1,0:T(8,128)(2,1)} %bitcast.41), channel_id=1, source_target_pairs={{16,4},{17,5},{18,6},{19,7},{20,8},{21,9},{22,10},{23,11},{24,12},... | collective-permute-start | bytes 3145736 | tf_op jit(solution)/shard_map/ppermute | solution.py:48
  20.8 61.9 %collective-permute-start.2 = (bf16[512,1024]{1,0:T(8,128)(2,1)}, bf16[512,1024]{1,0:T(8,128)(2,1)}, u32[]{:S(2)}, u32[]{:S(2)}) collective-permute-start(bf16[512,1024]{1,0:T(8,128)(2,1)} %bitcast.42), channel_id=1, source_target_pairs={{16,12},{17,13},{18,14},{19,15},{20,0},{21,1},{22,2},{23,3},{24,4}... | collective-permute-start | bytes 3145736 | tf_op jit(solution)/shard_map/ppermute | solution.py:48
  25.5 61.7 %collective-permute-start.3 = (bf16[512,1024]{1,0:T(8,128)(2,1)}, bf16[512,1024]{1,0:T(8,128)(2,1)}, u32[]{:S(2)}, u32[]{:S(2)}) collective-permute-start(bf16[512,1024]{1,0:T(8,128)(2,1)} %bitcast.43), channel_id=1, source_target_pairs={{16,8},{17,9},{18,10},{19,11},{20,12},{21,13},{22,14},{23,15},{24,... | collective-permute-start | bytes 3145736 | tf_op jit(solution)/shard_map/ppermute | solution.py:48
  35.7 61.5 %collective-permute-start.5 = (bf16[384,1024]{1,0:T(8,128)(2,1)}, bf16[384,1024]{1,0:T(8,128)(2,1)S(1)}, u32[]{:S(2)}, u32[]{:S(2)}) collective-permute-start(bf16[384,1024]{1,0:T(8,128)(2,1)} %collective-permute-done.4.refs_4_), channel_id=1, source_target_pairs={{0,3},{1,0},{2,1},{3,2},{4,7},{5,4},{6,5},{7,6},{8,11},{9,8},{10,9... | collective-permute-start | bytes 2359304 | tf_op jit(solution)/shard_map/ppermute | solution.py:48
  38.8 58.4 %collective-permute-start.6 = (bf16[384,1024]{1,0:T(8,128)(2,1)}, bf16[384,1024]{1,0:T(8,128)(2,1)}, u32[]{:S(2)}, u32[]{:S(2)}) collective-permute-start(bf16[384,1024]{1,0:T(8,128)(2,1)} %collective-permute-done.4.refs_4_), channel_id=1, source_target_pairs={{0,1},{1,2},{2,3},{3,0},{4,5},{5,6},{6,7},{7,4},{8,9},{9,10},{10,1... | collective-permute-start | bytes 2359304 | tf_op jit(solution)/shard_map/ppermute | solution.py:48
  76.0 33.1 %collective-permute-start.9 = (bf16[384,1024]{1,0:T(8,128)(2,1)}, bf16[384,1024]{1,0:T(8,128)(2,1)}, u32[]{:S(2)}, u32[]{:S(2)}) collective-permute-start(bf16[384,1024]{1,0:T(8,128)(2,1)} %collective-permute-done.4.refs_4_), channel_id=1, source_target_pairs={{0,2},{1,3},{2,0},{3,1},{4,6},{5,7},{6,4},{7,5},{8,10},{9,11},{10,... | collective-permute-start | bytes 2359304 | tf_op jit(solution)/shard_map/ppermute | solution.py:48
  97.2 0.9 copy-start.7
  105.7 55.4 %collective-permute-start.10 = (bf16[480,2048]{1,0:T(8,128)(2,1)}, bf16[480,2048]{1,0:T(8,128)(2,1)}, u32[]{:S(2)}, u32[]{:S(2)}) collective-permute-start(bf16[480,2048]{1,0:T(8,128)(2,1)} %get-tuple-element.21), channel_id=1, source_target_pairs={{0,1},{1,2},{2,3},{3,0},{4,5},{5,6},{6,7},{7,4},{8,9},{9,10},{10,1... | collective-permute-start | bytes 5898248 | tf_op jit(solution)/shard_map/ppermute | solution.py:48
  105.9 9.3 %copy-start.6 = (s32[1,48]{1,0:T(1,128)S(1)}, s32[1,48]{1,0:T(1,128)}, u32[]{:S(2)}) copy-start(s32[1,48]{1,0:T(1,128)} %param.13) | copy-start | bytes 580
  105.9 12.1 %copy-start.2 = (bf16[1,384,1024]{2,1,0:T(8,128)(2,1)S(1)}, bf16[1,384,1024]{2,1,0:T(8,128)(2,1)}, u32[]{:S(2)}) copy-start(bf16[1,384,1024]{2,1,0:T(8,128)(2,1)} %param.9) | copy-start | bytes 2359300
  105.9 55.2 %collective-permute-start.11 = (bf16[480,2048]{1,0:T(8,128)(2,1)}, bf16[480,2048]{1,0:T(8,128)(2,1)}, u32[]{:S(2)}, u32[]{:S(2)}) collective-permute-start(bf16[480,2048]{1,0:T(8,128)(2,1)} %get-tuple-element.25), channel_id=1, source_target_pairs={{0,3},{1,0},{2,1},{3,2},{4,7},{5,4},{6,5},{7,6},{8,11},{9,8},{10,9... | collective-permute-start | bytes 5898248 | tf_op jit(solution)/shard_map/ppermute | solution.py:48
  115.1 46.1 %collective-permute-start.12 = (bf16[480,2048]{1,0:T(8,128)(2,1)}, bf16[480,2048]{1,0:T(8,128)(2,1)}, u32[]{:S(2)}, u32[]{:S(2)}) collective-permute-start(bf16[480,2048]{1,0:T(8,128)(2,1)} %shard_map.105), channel_id=1, source_target_pairs={{0,2},{1,3},{2,0},{3,1},{4,6},{5,7},{6,4},{7,5},{8,10},{9,11},{10,... | collective-permute-start | bytes 5898248 | tf_op jit(solution)/shard_map/ppermute | solution.py:48
  118.6 64.4 %collective-permute-start.8 = (bf16[16,3,64,512]{3,2,1,0:T(8,128)(2,1)}, bf16[16,3,64,512]{3,2,1,0:T(8,128)(2,1)}, u32[]{:S(2)}, u32[]{:S(2)}) collective-permute-start(bf16[16,3,64,512]{3,2,1,0:T(8,128)(2,1)} %all-to-all-done.a_ref), channel_id=1, source_target_pairs={{16,0},{32,16},{48,32},{64,48},{80,64},{96,80},{112,96},{17,1},{33... | collective-permute-start | bytes 9437192 | tf_op jit(solution)/shard_map/ppermute | solution.py:29
  131.7 35.5 %copy-start.5 = (s32[4]{0:T(128)S(1)}, s32[4]{0:T(128)}, u32[]{:S(2)}) copy-start(s32[4]{0:T(128)} %constant.112.clone) | copy-start | bytes 52
  131.7 36.2 %copy-start.4 = (s32[32]{0:T(128)S(1)}, s32[32]{0:T(128)}, u32[]{:S(2)}) copy-start(s32[32]{0:T(128)} %param.14) | copy-start | bytes 388
  161.2 37.9 %all-to-all-start.1 = ((bf16[16,3,64,512]{3,2,1,0:T(8,128)(2,1)}), bf16[16,3,64,512]{3,2,1,0:T(8,128)(2,1)}, u32[]{:S(2)}, u32[]{:S(2)}) async-start(bf16[16,3,64,512]{3,2,1,0:T(8,128)(2,1)} %shard_map.106), calls=%async_computation.1 | async-start | bytes 6291456 | tf_op jit(solution)/shard_map/all_to_all | solution.py:52
  173.9 18.5 %collective-permute-start.13 = (bf16[2,64,1024]{2,1,0:T(8,128)(2,1)S(1)}, bf16[2,64,1024]{2,1,0:T(8,128)(2,1)S(1)}, u32[]{:S(2)}, u32[]{:S(2)}) collective-permute-start(bf16[2,64,1024]{2,1,0:T(8,128)(2,1)S(1)} %get-tuple-element.43), channel_id=1, source_target_pairs={{0,12},{1,13},{2,14},{3,15},{4,0},{5,1},{6,2},{7,3},{8,4},{9,5},{1... | collective-permute-start | bytes 786440 | tf_op jit(solution)/shard_map/ppermute | solution.py:48
  176.7 20.5 %collective-permute-start.14 = (bf16[2,64,1024]{2,1,0:T(8,128)(2,1)S(1)}, bf16[2,64,1024]{2,1,0:T(8,128)(2,1)S(1)}, u32[]{:S(2)}, u32[]{:S(2)}) collective-permute-start(bf16[2,64,1024]{2,1,0:T(8,128)(2,1)S(1)} %get-tuple-element.42), channel_id=1, source_target_pairs={{0,4},{1,5},{2,6},{3,7},{4,8},{5,9},{6,10},{7,11},{8,12},{9,13},{1... | collective-permute-start | bytes 786440 | tf_op jit(solution)/shard_map/ppermute | solution.py:48
  176.7 20.5 %collective-permute-start.15 = (bf16[2,64,1024]{2,1,0:T(8,128)(2,1)S(1)}, bf16[2,64,1024]{2,1,0:T(8,128)(2,1)S(1)}, u32[]{:S(2)}, u32[]{:S(2)}) collective-permute-start(bf16[2,64,1024]{2,1,0:T(8,128)(2,1)S(1)} %get-tuple-element.41), channel_id=1, source_target_pairs={{0,8},{1,9},{2,10},{3,11},{4,12},{5,13},{6,14},{7,15},{8,0},{9,1},... | collective-permute-start | bytes 786440 | tf_op jit(solution)/shard_map/ppermute | solution.py:48
  178.9 4.1 %collective-permute-start.7 = (bf16[3,128,64]{2,1,0:T(8,128)(2,1)S(1)}, bf16[3,128,64]{2,1,0:T(8,128)(2,1)S(1)}, u32[]{:S(2)}, u32[]{:S(2)}) collective-permute-start(bf16[3,128,64]{2,1,0:T(8,128)(2,1)S(1)} %bitcast.37), channel_id=1, source_target_pairs={{16,0},{32,16},{48,32},{64,48},{80,64},{96,80},{112,96},{17,1},{33... | collective-permute-start | bytes 147464 | tf_op jit(solution)/shard_map/ppermute | solution.py:29
  183.0 0.6 copy-start.3

commit v4 on v3

--- a/solution.py
+++ b/solution.py
@@ -320,7 +320,8 @@
     groups = rows // GROUP_ROWS
     my_tenants = lax.dynamic_slice_in_dim(tenants, me * groups, groups)
 
-    weights = tuple(move(w, "col", step, 1) for step in (0, 1, -1, 2))
+    w_own, w_below, w_above = (move(w, "col", step, 1) for step in (0, 1, -1))
+    weights = (w_own, w_below, w_above, move(w_own, "col", 2))
     v_next = to_previous_section(v)
 
     down_mine = exchange(down[tenants].reshape(n, groups, rank, cols))
@@ -336,9 +337,10 @@
     for_above, for_below = frozen_terms((v_above, v_below), weights, parts)
     from_below, from_above = move(for_above, "row", 1), move(for_below, "row", -1)
     (for_far,) = frozen_terms((v_far,), weights, parts)
-    down_mine, low, for_above = together(down_mine, low, for_above)
+    low, for_above = together(low, for_above)
+    low_next = to_previous_section(low)
+    down_mine, low_next = together(down_mine, low_next)
     down_next = to_previous_section(down_mine)
-    low_next = to_previous_section(low)
     from_far = move(for_far, "row", 2)
     low, for_far = together(low, for_far)
     sent = group_terms(x, jnp.swapaxes(low, 1, 2))

time: 205 us -> 203 us (level)
  waiting for transfers between devices: 93.6 us -> 74.1 us
  starting transfers between devices: 44.8 us -> 63 us
    ppermute x13, waiting for transfers between devices: 85.9 us -> 60.9 us  [move(): return lax.ppermute(block, ('section', 'dp'), along(axis, distance, down))]
    ppermute x13, starting transfers between devices: 25.5 us -> 36.5 us  [move(): return lax.ppermute(block, ('section', 'dp'), along(axis, distance, down))]
    all_to_all x2, waiting for transfers between devices: 0.01 us -> 6.14 us  [exchange(): return lax.all_to_all(blocks, 'dp', split_axis=0, concat_axis=0, tiled=True)]
    all_to_all x2, starting transfers between devices: 12.7 us -> 17.7 us  [exchange(): return lax.all_to_all(blocks, 'dp', split_axis=0, concat_axis=0, tiled=True)]
    ppermute x3, starting transfers between devices: 6.59 us -> 8.8 us  [to_previous_section(): return lax.ppermute(block, 'section', [(i, i - 1) for i in range(1, n)])]
  transfers between devices with their start and end apart: 18 -> 18, of which waited for: 7 -> 9; matrix products, arithmetic and copies ran while one was open for 6% -> 6% of each run, Pallas kernels for 21% -> 21%
where the time goes in v4:
time: 203 us; the launch traced here: 202 us
  waiting for transfers between devices  74.1 us (37%)
  starting transfers between devices  63 us (31%)
  Pallas kernels  47.1 us (23%)
  local copies, waits for them, and re-layouts  10.9 us (5%)
  other arithmetic  5.29 us (3%)
    ppermute x13, waiting for transfers between devices, move(): return lax.ppermute(block, ('section', 'dp'), along(axis, distance, down))  60.9 us
    ppermute x13, starting transfers between devices, move(): return lax.ppermute(block, ('section', 'dp'), along(axis, distance, down))  36.5 us
    pallas_call x3, Pallas kernels, frozen_terms(): pl.pallas_call(body, in_specs=[pl.BlockSpec(memory_space=pl.ANY)] * (n_w...  18.7 us
    all_to_all x2, starting transfers between devices, exchange(): return lax.all_to_all(blocks, 'dp', split_axis=0, concat_axis=0, tiled=True)  17.7 us
    ppermute x3, starting transfers between devices, to_previous_section(): return lax.ppermute(block, 'section', [(i, i - 1) for i in range(1, n)])  8.8 us
    pallas_call x1, Pallas kernels, input_gradient(): pl.pallas_call(body, grid_spec=pltpu.PrefetchScalarGridSpec(num_scalar_pr...  8.65 us
    ppermute x3, waiting for transfers between devices, to_previous_section(): return lax.ppermute(block, 'section', [(i, i - 1) for i in range(1, n)])  7.14 us
    pallas_call x1, Pallas kernels, up_parts(): pl.pallas_call(body, grid=(n // WIDE,), in_specs=[pl.BlockSpec((rows, WID...  6.72 us
  transfers between devices with their start and end apart: 18, of which 9 were waited for; matrix products, arithmetic and copies ran while one was open for 6% of the time, Pallas kernels for 21%

profile of v4, /device:TPU:24, one launch (start us, length us, event | category | flops | bytes accessed | tf_op | source)
XLA Modules:
  0.0 201.8 jit_solution(16802181943230018962)
XLA Ops:
  2.2 2.5 %gather_fusion = bf16[48,64,512]{2,1,0:T(8,128)(2,1)} fusion(bf16[32,64,512]{2,1,0:T(8,128)(2,1)S(1)} %bitcast.27, s32[1024]{0:T(1024)S(1)} %pad_clamp_fusion.3), kind=kCustom, calls=%fused_computation | custom fusion | bytes 6291648 | tf_op jit(solution)/shard_map/gather | solution.py:327
  4.8 8.1 %all-to-all-start = ((bf16[16,3,64,512]{3,2,1,0:T(8,128)(2,1)}), bf16[16,3,64,512]{3,2,1,0:T(8,128)(2,1)}, u32[]{:S(2)}, u32[]{:S(2)}) async-start(bf16[16,3,64,512]{3,2,1,0:T(8,128)(2,1)} %bitcast.30), calls=%async_computation | async-start | bytes 6291456 | tf_op jit(solution)/shard_map/all_to_all | solution.py:52
  12.8 1.9 collective-permute-start
  14.8 2.8 %collective-permute-start.4 = (bf16[384,1024]{1,0:T(8,128)(2,1)S(1)}, bf16[384,1024]{1,0:T(8,128)(2,1)}, u32[]{:S(2)}, u32[]{:S(2)}) collective-permute-start(bf16[384,1024]{1,0:T(8,128)(2,1)S(1)} %bitcast.34), channel_id=1, source_target_pairs={{16,0},{32,16},{48,32},{64,48},{80,64},{96,80},{112,96},{17,1},{33... | collective-permute-start | bytes 2359304 | tf_op jit(solution)/shard_map/ppermute | solution.py:29
  17.5 3.2 %collective-permute-start.1 = (bf16[512,1024]{1,0:T(8,128)(2,1)}, bf16[512,1024]{1,0:T(8,128)(2,1)}, u32[]{:S(2)}, u32[]{:S(2)}) collective-permute-start(bf16[512,1024]{1,0:T(8,128)(2,1)} %bitcast.41), channel_id=1, source_target_pairs={{16,4},{17,5},{18,6},{19,7},{20,8},{21,9},{22,10},{23,11},{24,12},... | collective-permute-start | bytes 3145736 | tf_op jit(solution)/shard_map/ppermute | solution.py:48
  20.8 4.7 %collective-permute-start.2 = (bf16[512,1024]{1,0:T(8,128)(2,1)}, bf16[512,1024]{1,0:T(8,128)(2,1)}, u32[]{:S(2)}, u32[]{:S(2)}) collective-permute-start(bf16[512,1024]{1,0:T(8,128)(2,1)} %bitcast.42), channel_id=1, source_target_pairs={{16,12},{17,13},{18,14},{19,15},{20,0},{21,1},{22,2},{23,3},{24,4}... | collective-permute-start | bytes 3145736 | tf_op jit(solution)/shard_map/ppermute | solution.py:48
  27.4 3.4 %collective-permute-start.3 = (bf16[512,1024]{1,0:T(8,128)(2,1)}, bf16[512,1024]{1,0:T(8,128)(2,1)}, u32[]{:S(2)}, u32[]{:S(2)}) collective-permute-start(bf16[512,1024]{1,0:T(8,128)(2,1)} %collective-permute-done.refs_0_), channel_id=1, source_target_pairs={{0,8},{1,9},{2,10},{3,11},{4,12},{5,13},{6,14},{7,15},{8,0},{9,1},... | collective-permute-start | bytes 3145736 | tf_op jit(solution)/shard_map/ppermute | solution.py:48
  30.7 4.9 %collective-permute-done.4.refs_4_ = bf16[384,1024]{1,0:T(8,128)(2,1)} collective-permute-done((bf16[384,1024]{1,0:T(8,128)(2,1)S(1)}, bf16[384,1024]{1,0:T(8,128)(2,1)}, u32[]{:S(2)}, u32[]{:S(2)}) %collective-permute-start.4) | collective-permute-done | bytes 786464 | tf_op jit(solution)/shard_map/ppermute | solution.py:29
  35.7 3.1 %collective-permute-start.5 = (bf16[384,1024]{1,0:T(8,128)(2,1)}, bf16[384,1024]{1,0:T(8,128)(2,1)S(1)}, u32[]{:S(2)}, u32[]{:S(2)}) collective-permute-start(bf16[384,1024]{1,0:T(8,128)(2,1)} %collective-permute-done.4.refs_4_), channel_id=1, source_target_pairs={{0,3},{1,0},{2,1},{3,2},{4,7},{5,4},{6,5},{7,6},{8,11},{9,8},{10,9... | collective-permute-start | bytes 2359304 | tf_op jit(solution)/shard_map/ppermute | solution.py:48
  38.8 38.0 %collective-permute-done.1.refs_1_ = bf16[512,1024]{1,0:T(8,128)(2,1)} collective-permute-done((bf16[512,1024]{1,0:T(8,128)(2,1)}, bf16[512,1024]{1,0:T(8,128)(2,1)}, u32[]{:S(2)}, u32[]{:S(2)}) %collective-permute-start.1) | collective-permute-done | bytes 1048608 | tf_op jit(solution)/shard_map/ppermute | solution.py:48
  76.8 4.3 %collective-permute-start.9 = (bf16[384,1024]{1,0:T(8,128)(2,1)}, bf16[384,1024]{1,0:T(8,128)(2,1)}, u32[]{:S(2)}, u32[]{:S(2)}) collective-permute-start(bf16[384,1024]{1,0:T(8,128)(2,1)} %collective-permute-done.4.refs_4_), channel_id=1, source_target_pairs={{0,2},{1,3},{2,0},{3,1},{4,6},{5,7},{6,4},{7,5},{8,10},{9,11},{10,... | collective-permute-start | bytes 2359304 | tf_op jit(solution)/shard_map/ppermute | solution.py:48
  81.1 6.7 %shard_map.103.refs_6_.refs_5_.refs_0_ = bf16[96,2048]{1,0:T(8,128)(2,1)} custom-call(bf16[384,8192]{1,0:T(8,128)(2,1)} %bitcast.28, bf16[16,3,64,512]{3,2,1,0:T(8,128)(2,1)} %all-to-all-done.a_ref, bf16[384,1024]{1,0:T(8,128)(2,1)} %bitcast.33), custom_call_target="tpu_custom_call" | custom-call | flops 402653184 | bytes 9437184 | tf_op jit(solution)/shard_map/pallas_call | solution.py:125
  90.2 7.7 %shard_map.104 = (bf16[480,2048]{1,0:T(8,128)(2,1)}, bf16[480,2048]{1,0:T(8,128)(2,1)}) custom-call(bf16[512,1024]{1,0:T(8,128)(2,1)} %collective-permute-done.refs_0_, bf16[512,1024]{1,0:T(8,128)(2,1)} %collective-permute-done.1.refs_1_, bf16[512,1024]{1,0:T(8,128)(2,1)} %collective-permute-done.2.refs_2_, ...), custom_call_target="tpu_custom_call" | custom-call | flops 4026531840 | bytes 10092544 | tf_op jit(solution)/shard_map/pallas_call | solution.py:185
  97.8 5.8 %collective-permute-start.10 = (bf16[480,2048]{1,0:T(8,128)(2,1)}, bf16[480,2048]{1,0:T(8,128)(2,1)}, u32[]{:S(2)}, u32[]{:S(2)}) collective-permute-start(bf16[480,2048]{1,0:T(8,128)(2,1)} %get-tuple-element.22), channel_id=1, source_target_pairs={{0,1},{1,2},{2,3},{3,0},{4,5},{5,6},{6,7},{7,4},{8,9},{9,10},{10,1... | collective-permute-start | bytes 5898248 | tf_op jit(solution)/shard_map/ppermute | solution.py:48
  103.7 6.1 %shard_map.105 = bf16[480,2048]{1,0:T(8,128)(2,1)} custom-call(bf16[512,1024]{1,0:T(8,128)(2,1)} %collective-permute-done.refs_0_, bf16[512,1024]{1,0:T(8,128)(2,1)} %collective-permute-done.1.refs_1_, bf16[512,1024]{1,0:T(8,128)(2,1)} %collective-permute-done.2.refs_2_, bf16[512,1024]{1,0:T(8,128)(2,1)} %collective-permute-done.3.refs_3_, ...), custom_call_target="tpu_custom_call" | custom-call | flops 2013265920 | bytes 7143424 | tf_op jit(solution)/shard_map/pallas_call | solution.py:185
  109.8 4.5 %collective-permute-start.12 = (bf16[480,2048]{1,0:T(8,128)(2,1)}, bf16[480,2048]{1,0:T(8,128)(2,1)}, u32[]{:S(2)}, u32[]{:S(2)}) collective-permute-start(bf16[480,2048]{1,0:T(8,128)(2,1)} %shard_map.105), channel_id=1, source_target_pairs={{0,2},{1,3},{2,0},{3,1},{4,6},{5,7},{6,4},{7,5},{8,10},{9,11},{10,... | collective-permute-start | bytes 5898248 | tf_op jit(solution)/shard_map/ppermute | solution.py:48
  114.4 2.8 %gather_fusion.1 = bf16[3,64,1024]{2,1,0:T(8,128)(2,1)S(1)} fusion(bf16[32,64,1024]{2,1,0:T(8,128)(2,1)} %bitcast.38, s32[1024]{0:T(1024)S(1)} %pad_clamp_fusion.2), kind=kCustom, calls=%fused_computation.1 | custom fusion | bytes 786444 | tf_op jit(solution)/shard_map/gather | solution.py:332
  117.7 1.9 collective-permute-start.7
  119.6 2.2 %collective-permute-done.7.low_ref = bf16[3,128,64]{2,1,0:T(8,128)(2,1)S(1)} collective-permute-done((bf16[3,128,64]{2,1,0:T(8,128)(2,1)S(1)}, bf16[3,128,64]{2,1,0:T(8,128)(2,1)S(1)}, u32[]{:S(2)}, u32[]{:S(2)}) %collective-permute-start.7) | collective-permute-done | bytes 49184 | tf_op jit(solution)/shard_map/ppermute | solution.py:29
  121.8 4.1 %collective-permute-start.8 = (bf16[16,3,64,512]{3,2,1,0:T(8,128)(2,1)}, bf16[16,3,64,512]{3,2,1,0:T(8,128)(2,1)}, u32[]{:S(2)}, u32[]{:S(2)}) collective-permute-start(bf16[16,3,64,512]{3,2,1,0:T(8,128)(2,1)} %all-to-all-done.a_ref), channel_id=1, source_target_pairs={{16,0},{32,16},{48,32},{64,48},{80,64},{96,80},{112,96},{17,1},{33... | collective-permute-start | bytes 9437192 | tf_op jit(solution)/shard_map/ppermute | solution.py:29
  126.0 5.0 %shard_map.107.refs_0_ = bf16[384,2048]{1,0:T(8,128)(2,1)} custom-call(bf16[512,1024]{1,0:T(8,128)(2,1)} %collective-permute-done.refs_0_, bf16[512,1024]{1,0:T(8,128)(2,1)} %collective-permute-done.1.refs_1_, bf16[512,1024]{1,0:T(8,128)(2,1)} %collective-permute-done.2.refs_2_, bf16[512,1024]{1,0:T(8,128)(2,1)} %collective-permute-done.3.refs_3_, ...), custom_call_target="tpu_custom_call" | custom-call | flops 1610612736 | bytes 6553600 | tf_op jit(solution)/shard_map/pallas_call | solution.py:185
  131.6 5.6 %shard_map.106 = bf16[16,3,64,512]{3,2,1,0:T(8,128)(2,1)} custom-call(bf16[384,8192]{1,0:T(8,128)(2,1)} %bitcast.29, bf16[3,64,128]{2,1,0:T(8,128)(2,1)} %copy.18.low_ref), custom_call_target="tpu_custom_call" | custom-call | flops 402653184 | bytes 9437184 | tf_op jit(solution)/shard_map/pallas_call | solution.py:74
  137.2 12.9 %collective-permute-done.12.refs_3_ = bf16[480,2048]{1,0:T(8,128)(2,1)} collective-permute-done((bf16[480,2048]{1,0:T(8,128)(2,1)}, bf16[480,2048]{1,0:T(8,128)(2,1)}, u32[]{:S(2)}, u32[]{:S(2)}) %collective-permute-start.12) | collective-permute-done | bytes 1966112 | tf_op jit(solution)/shard_map/ppermute | solution.py:48
  150.2 9.7 %all-to-all-start.1 = ((bf16[16,3,64,512]{3,2,1,0:T(8,128)(2,1)}), bf16[16,3,64,512]{3,2,1,0:T(8,128)(2,1)}, u32[]{:S(2)}, u32[]{:S(2)}) async-start(bf16[16,3,64,512]{3,2,1,0:T(8,128)(2,1)} %shard_map.106), calls=%async_computation.1 | async-start | bytes 6291456 | tf_op jit(solution)/shard_map/all_to_all | solution.py:52
  163.8 2.7 %shard_map.109 = bf16[8,64,1024]{2,1,0:T(8,128)(2,1)} custom-call(s32[12]{0:T(128)} %broadcast_select_fusion.6.place_ref, bf16[96,2048]{1,0:T(8,128)(2,1)} %shard_map.103.refs_6_.refs_5_.refs_0_, bf16[480,2048]{1,0:T(8,128)(2,1)} %collective-permute-done.10.refs_1_, bf16[480,2048]{1,0:T(8,128)(2,1)} %collective-permute-done.11.refs_2_, ...), custom_call_target="tpu_custom_call" | custom-call | flops 393216 | bytes 2621440 | tf_op jit(solution)/shard_map/pallas_call | solution.py:227
  167.8 3.1 %collective-permute-start.13 = (bf16[2,64,1024]{2,1,0:T(8,128)(2,1)S(1)}, bf16[2,64,1024]{2,1,0:T(8,128)(2,1)S(1)}, u32[]{:S(2)}, u32[]{:S(2)}) collective-permute-start(bf16[2,64,1024]{2,1,0:T(8,128)(2,1)S(1)} %get-tuple-element.45), channel_id=1, source_target_pairs={{0,12},{1,13},{2,14},{3,15},{4,0},{5,1},{6,2},{7,3},{8,4},{9,5},{1... | collective-permute-start | bytes 786440 | tf_op jit(solution)/shard_map/ppermute | solution.py:48
  170.9 2.3 %collective-permute-start.15 = (bf16[2,64,1024]{2,1,0:T(8,128)(2,1)S(1)}, bf16[2,64,1024]{2,1,0:T(8,128)(2,1)S(1)}, u32[]{:S(2)}, u32[]{:S(2)}) collective-permute-start(bf16[2,64,1024]{2,1,0:T(8,128)(2,1)S(1)} %get-tuple-element.43), channel_id=1, source_target_pairs={{0,8},{1,9},{2,10},{3,11},{4,12},{5,13},{6,14},{7,15},{8,0},{9,1},... | collective-permute-start | bytes 786440 | tf_op jit(solution)/shard_map/ppermute | solution.py:48
  173.8 8.7 %shard_map.108 = bf16[384,8192]{1,0:T(8,128)(2,1)} custom-call(s32[16]{0:T(128)} %pad_add_fusion.b_ref, bf16[3,128,64]{2,1,0:T(8,128)(2,1)} %copy-done.3, bf16[16,3,64,512]{3,2,1,0:T(8,128)(2,1)} %collective-permute-done.8.a_ref, bf16[384,2048]{1,0:T(8,128)(2,1)} %shard_map.107.refs_0_, bf16[480,2048]{1,0:T(8,128)(2,1)} %collective-permute-done.10.refs_1_, ...), custom_call_target="tpu_custom_call" | custom-call | flops 402653184 | bytes 15728640 | tf_op jit(solution)/shard_map/pallas_call | solution.py:286
  184.2 4.9 %collective-permute-done.15 = bf16[2,64,1024]{2,1,0:T(8,128)(2,1)S(1)} collective-permute-done((bf16[2,64,1024]{2,1,0:T(8,128)(2,1)S(1)}, bf16[2,64,1024]{2,1,0:T(8,128)(2,1)S(1)}, u32[]{:S(2)}, u32[]{:S(2)}) %collective-permute-start.15) | collective-permute-done | bytes 262176 | tf_op jit(solution)/shard_map/ppermute | solution.py:48
  189.0 1.9 add_multiply_fusion
  191.0 6.1 %all-to-all-done.1.p_ref = bf16[16,3,64,512]{3,2,1,0:T(8,128)(2,1)} async-done(((bf16[16,3,64,512]{3,2,1,0:T(8,128)(2,1)}), bf16[16,3,64,512]{3,2,1,0:T(8,128)(2,1)}, u32[]{:S(2)}, u32[]{:S(2)}) %all-to-all-start.1) | async-done | bytes 3145760 | tf_op jit(solution)/shard_map/all_to_all | solution.py:52
  197.1 4.7 %shard_map.110 = f32[32,64,512]{2,1,0:T(8,128)} custom-call(s32[48]{0:T(128)} %bitcast.39, bf16[16,3,64,512]{3,2,1,0:T(8,128)(2,1)} %all-to-all-done.1.p_ref), custom_call_target="tpu_custom_call" | custom-call | flops 1572864 | bytes 7340032 | tf_op jit(solution)/shard_map/pallas_call | solution.py:255
  (54 shorter events, 14.5 us)
Async XLA Ops:
  0.6 1.6 copy-start
  4.8 10.0 %copy-start.1 = (bf16[1,384,1024]{2,1,0:T(8,128)(2,1)S(1)}, bf16[1,384,1024]{2,1,0:T(8,128)(2,1)}, u32[]{:S(2)}) copy-start(bf16[1,384,1024]{2,1,0:T(8,128)(2,1)} %param.9) | copy-start | bytes 2359300
  4.8 76.4 %all-to-all-start = ((bf16[16,3,64,512]{3,2,1,0:T(8,128)(2,1)}), bf16[16,3,64,512]{3,2,1,0:T(8,128)(2,1)}, u32[]{:S(2)}, u32[]{:S(2)}) async-start(bf16[16,3,64,512]{3,2,1,0:T(8,128)(2,1)} %bitcast.30), calls=%async_computation | async-start | bytes 6291456 | tf_op jit(solution)/shard_map/all_to_all | solution.py:52
  12.8 14.5 %collective-permute-start = (bf16[512,1024]{1,0:T(8,128)(2,1)}, bf16[512,1024]{1,0:T(8,128)(2,1)}, u32[]{:S(2)}, u32[]{:S(2)}) collective-permute-start(bf16[512,1024]{1,0:T(8,128)(2,1)} %bitcast.40), channel_id=1, source_target_pairs={{16,0},{17,1},{18,2},{19,3},{20,4},{21,5},{22,6},{23,7},{24,8},{25... | collective-permute-start | bytes 3145736 | tf_op jit(solution)/shard_map/ppermute | solution.py:48
  14.8 20.9 %collective-permute-start.4 = (bf16[384,1024]{1,0:T(8,128)(2,1)S(1)}, bf16[384,1024]{1,0:T(8,128)(2,1)}, u32[]{:S(2)}, u32[]{:S(2)}) collective-permute-start(bf16[384,1024]{1,0:T(8,128)(2,1)S(1)} %bitcast.34), channel_id=1, source_target_pairs={{16,0},{32,16},{48,32},{64,48},{80,64},{96,80},{112,96},{17,1},{33... | collective-permute-start | bytes 2359304 | tf_op jit(solution)/shard_map/ppermute | solution.py:29
  17.5 59.3 %collective-permute-start.1 = (bf16[512,1024]{1,0:T(8,128)(2,1)}, bf16[512,1024]{1,0:T(8,128)(2,1)}, u32[]{:S(2)}, u32[]{:S(2)}) collective-permute-start(bf16[512,1024]{1,0:T(8,128)(2,1)} %bitcast.41), channel_id=1, source_target_pairs={{16,4},{17,5},{18,6},{19,7},{20,8},{21,9},{22,10},{23,11},{24,12},... | collective-permute-start | bytes 3145736 | tf_op jit(solution)/shard_map/ppermute | solution.py:48
  20.8 67.1 %collective-permute-start.2 = (bf16[512,1024]{1,0:T(8,128)(2,1)}, bf16[512,1024]{1,0:T(8,128)(2,1)}, u32[]{:S(2)}, u32[]{:S(2)}) collective-permute-start(bf16[512,1024]{1,0:T(8,128)(2,1)} %bitcast.42), channel_id=1, source_target_pairs={{16,12},{17,13},{18,14},{19,15},{20,0},{21,1},{22,2},{23,3},{24,4}... | collective-permute-start | bytes 3145736 | tf_op jit(solution)/shard_map/ppermute | solution.py:48
  27.4 61.9 %collective-permute-start.3 = (bf16[512,1024]{1,0:T(8,128)(2,1)}, bf16[512,1024]{1,0:T(8,128)(2,1)}, u32[]{:S(2)}, u32[]{:S(2)}) collective-permute-start(bf16[512,1024]{1,0:T(8,128)(2,1)} %collective-permute-done.refs_0_), channel_id=1, source_target_pairs={{0,8},{1,9},{2,10},{3,11},{4,12},{5,13},{6,14},{7,15},{8,0},{9,1},... | collective-permute-start | bytes 3145736 | tf_op jit(solution)/shard_map/ppermute | solution.py:48
  35.7 53.6 %collective-permute-start.5 = (bf16[384,1024]{1,0:T(8,128)(2,1)}, bf16[384,1024]{1,0:T(8,128)(2,1)S(1)}, u32[]{:S(2)}, u32[]{:S(2)}) collective-permute-start(bf16[384,1024]{1,0:T(8,128)(2,1)} %collective-permute-done.4.refs_4_), channel_id=1, source_target_pairs={{0,3},{1,0},{2,1},{3,2},{4,7},{5,4},{6,5},{7,6},{8,11},{9,8},{10,9... | collective-permute-start | bytes 2359304 | tf_op jit(solution)/shard_map/ppermute | solution.py:48
  38.8 50.5 %collective-permute-start.6 = (bf16[384,1024]{1,0:T(8,128)(2,1)}, bf16[384,1024]{1,0:T(8,128)(2,1)}, u32[]{:S(2)}, u32[]{:S(2)}) collective-permute-start(bf16[384,1024]{1,0:T(8,128)(2,1)} %collective-permute-done.4.refs_4_), channel_id=1, source_target_pairs={{0,1},{1,2},{2,3},{3,0},{4,5},{5,6},{6,7},{7,4},{8,9},{9,10},{10,1... | collective-permute-start | bytes 2359304 | tf_op jit(solution)/shard_map/ppermute | solution.py:48
  76.8 26.8 %collective-permute-start.9 = (bf16[384,1024]{1,0:T(8,128)(2,1)}, bf16[384,1024]{1,0:T(8,128)(2,1)}, u32[]{:S(2)}, u32[]{:S(2)}) collective-permute-start(bf16[384,1024]{1,0:T(8,128)(2,1)} %collective-permute-done.4.refs_4_), channel_id=1, source_target_pairs={{0,2},{1,3},{2,0},{3,1},{4,6},{5,7},{6,4},{7,5},{8,10},{9,11},{10,... | collective-permute-start | bytes 2359304 | tf_op jit(solution)/shard_map/ppermute | solution.py:48
  89.3 0.9 copy-start.7
  97.8 39.4 %collective-permute-start.10 = (bf16[480,2048]{1,0:T(8,128)(2,1)}, bf16[480,2048]{1,0:T(8,128)(2,1)}, u32[]{:S(2)}, u32[]{:S(2)}) collective-permute-start(bf16[480,2048]{1,0:T(8,128)(2,1)} %get-tuple-element.22), channel_id=1, source_target_pairs={{0,1},{1,2},{2,3},{3,0},{4,5},{5,6},{6,7},{7,4},{8,9},{9,10},{10,1... | collective-permute-start | bytes 5898248 | tf_op jit(solution)/shard_map/ppermute | solution.py:48
  103.6 10.7 %copy-start.6 = (s32[1,48]{1,0:T(1,128)S(1)}, s32[1,48]{1,0:T(1,128)}, u32[]{:S(2)}) copy-start(s32[1,48]{1,0:T(1,128)} %param.13) | copy-start | bytes 580
  103.6 13.5 %copy-start.2 = (bf16[1,384,1024]{2,1,0:T(8,128)(2,1)S(1)}, bf16[1,384,1024]{2,1,0:T(8,128)(2,1)}, u32[]{:S(2)}) copy-start(bf16[1,384,1024]{2,1,0:T(8,128)(2,1)} %param.9) | copy-start | bytes 2359300
  103.6 33.6 %collective-permute-start.11 = (bf16[480,2048]{1,0:T(8,128)(2,1)}, bf16[480,2048]{1,0:T(8,128)(2,1)}, u32[]{:S(2)}, u32[]{:S(2)}) collective-permute-start(bf16[480,2048]{1,0:T(8,128)(2,1)} %get-tuple-element.27), channel_id=1, source_target_pairs={{0,3},{1,0},{2,1},{3,2},{4,7},{5,4},{6,5},{7,6},{8,11},{9,8},{10,9... | collective-permute-start | bytes 5898248 | tf_op jit(solution)/shard_map/ppermute | solution.py:48
  109.8 40.4 %collective-permute-start.12 = (bf16[480,2048]{1,0:T(8,128)(2,1)}, bf16[480,2048]{1,0:T(8,128)(2,1)}, u32[]{:S(2)}, u32[]{:S(2)}) collective-permute-start(bf16[480,2048]{1,0:T(8,128)(2,1)} %shard_map.105), channel_id=1, source_target_pairs={{0,2},{1,3},{2,0},{3,1},{4,6},{5,7},{6,4},{7,5},{8,10},{9,11},{10,... | collective-permute-start | bytes 5898248 | tf_op jit(solution)/shard_map/ppermute | solution.py:48
  117.7 4.1 %collective-permute-start.7 = (bf16[3,128,64]{2,1,0:T(8,128)(2,1)S(1)}, bf16[3,128,64]{2,1,0:T(8,128)(2,1)S(1)}, u32[]{:S(2)}, u32[]{:S(2)}) collective-permute-start(bf16[3,128,64]{2,1,0:T(8,128)(2,1)S(1)} %bitcast.37), channel_id=1, source_target_pairs={{16,0},{32,16},{48,32},{64,48},{80,64},{96,80},{112,96},{17,1},{33... | collective-permute-start | bytes 147464 | tf_op jit(solution)/shard_map/ppermute | solution.py:29
  121.8 9.1 %copy-start.3 = (bf16[3,128,64]{2,1,0:T(8,128)(2,1)}, bf16[3,128,64]{2,1,0:T(8,128)(2,1)S(1)}, u32[]{:S(2)}) copy-start(bf16[3,128,64]{2,1,0:T(8,128)(2,1)S(1)} %collective-permute-done.7.low_ref) | copy-start | bytes 147460
  121.8 52.0 %collective-permute-start.8 = (bf16[16,3,64,512]{3,2,1,0:T(8,128)(2,1)}, bf16[16,3,64,512]{3,2,1,0:T(8,128)(2,1)}, u32[]{:S(2)}, u32[]{:S(2)}) collective-permute-start(bf16[16,3,64,512]{3,2,1,0:T(8,128)(2,1)} %all-to-all-done.a_ref), channel_id=1, source_target_pairs={{16,0},{32,16},{48,32},{64,48},{80,64},{96,80},{112,96},{17,1},{33... | collective-permute-start | bytes 9437192 | tf_op jit(solution)/shard_map/ppermute | solution.py:29
  137.2 24.0 %copy-start.5 = (s32[4]{0:T(128)S(1)}, s32[4]{0:T(128)}, u32[]{:S(2)}) copy-start(s32[4]{0:T(128)} %constant.112.clone) | copy-start | bytes 52
  137.2 24.7 %copy-start.4 = (s32[32]{0:T(128)S(1)}, s32[32]{0:T(128)}, u32[]{:S(2)}) copy-start(s32[32]{0:T(128)} %param.14) | copy-start | bytes 388
  150.2 46.9 %all-to-all-start.1 = ((bf16[16,3,64,512]{3,2,1,0:T(8,128)(2,1)}), bf16[16,3,64,512]{3,2,1,0:T(8,128)(2,1)}, u32[]{:S(2)}, u32[]{:S(2)}) async-start(bf16[16,3,64,512]{3,2,1,0:T(8,128)(2,1)} %shard_map.106), calls=%async_computation.1 | async-start | bytes 6291456 | tf_op jit(solution)/shard_map/all_to_all | solution.py:52
  167.8 14.7 %collective-permute-start.13 = (bf16[2,64,1024]{2,1,0:T(8,128)(2,1)S(1)}, bf16[2,64,1024]{2,1,0:T(8,128)(2,1)S(1)}, u32[]{:S(2)}, u32[]{:S(2)}) collective-permute-start(bf16[2,64,1024]{2,1,0:T(8,128)(2,1)S(1)} %get-tuple-element.45), channel_id=1, source_target_pairs={{0,12},{1,13},{2,14},{3,15},{4,0},{5,1},{6,2},{7,3},{8,4},{9,5},{1... | collective-permute-start | bytes 786440 | tf_op jit(solution)/shard_map/ppermute | solution.py:48
  170.9 13.3 %collective-permute-start.14 = (bf16[2,64,1024]{2,1,0:T(8,128)(2,1)S(1)}, bf16[2,64,1024]{2,1,0:T(8,128)(2,1)S(1)}, u32[]{:S(2)}, u32[]{:S(2)}) collective-permute-start(bf16[2,64,1024]{2,1,0:T(8,128)(2,1)S(1)} %get-tuple-element.44), channel_id=1, source_target_pairs={{0,4},{1,5},{2,6},{3,7},{4,8},{5,9},{6,10},{7,11},{8,12},{9,13},{1... | collective-permute-start | bytes 786440 | tf_op jit(solution)/shard_map/ppermute | solution.py:48
  170.9 18.1 %collective-permute-start.15 = (bf16[2,64,1024]{2,1,0:T(8,128)(2,1)S(1)}, bf16[2,64,1024]{2,1,0:T(8,128)(2,1)S(1)}, u32[]{:S(2)}, u32[]{:S(2)}) collective-permute-start(bf16[2,64,1024]{2,1,0:T(8,128)(2,1)S(1)} %get-tuple-element.43), channel_id=1, source_target_pairs={{0,8},{1,9},{2,10},{3,11},{4,12},{5,13},{6,14},{7,15},{8,0},{9,1},... | collective-permute-start | bytes 786440 | tf_op jit(solution)/shard_map/ppermute | solution.py:48

commit v5 on v4

--- a/solution.py
+++ b/solution.py
@@ -238,34 +238,41 @@
     )(places, *pieces)
 
 
-def sum_by_tenant(parts, tenants, n_tenants):
+def owners_sums(parts, tenants, n_tenants, by_slot, from_up):
     n, groups, rank, cols = parts.shape
-    steps = 2
-    r = rank // steps
+    per, _, kv = from_up[0].shape
+    r = rank // per
     scale = ADAPTER_SCALE / GROUP_ROWS
 
-    def body(t_ref, p_ref, o_ref):
-        o_ref[...] = jnp.zeros_like(o_ref)
+    def body(t_ref, p_ref, *refs):
+        down_ref, up_ref = refs[-2:]
+        up_ref[...] = sum(block[...].astype(F32) for block in refs[:-2]) * scale
+        down_ref[...] = jnp.zeros_like(down_ref)
 
         @pl.loop(0, n)
         def _(d):
             for g in range(groups):
-                o_ref[t_ref[d * groups + g]] += p_ref[d, g].astype(F32) * scale
-
+                down_ref[t_ref[d * groups + g]] += p_ref[d, g].astype(F32) * scale
+
+    slot = pl.BlockSpec((1, rank, kv), lambda i, t: (i, 0, 0))
     return pl.pallas_call(
         body,
         grid_spec=pltpu.PrefetchScalarGridSpec(
             num_scalar_prefetch=1,
-            grid=(steps,),
-            in_specs=[pl.BlockSpec((n, groups, r, cols), lambda i, t: (0, 0, i, 0))],
-            out_specs=pl.BlockSpec((n_tenants, r, cols), lambda i, t: (0, i, 0)),
-        ),
-        out_shape=jax.ShapeDtypeStruct((n_tenants, rank, cols), F32),
+            grid=(per,),
+            in_specs=[pl.BlockSpec((n, groups, r, cols), lambda i, t: (0, 0, i, 0))]
+            + [slot] * (1 + len(from_up)),
+            out_specs=[pl.BlockSpec((n_tenants, r, cols), lambda i, t: (0, i, 0)), slot],
+        ),
+        out_shape=[
+            jax.ShapeDtypeStruct((n_tenants, rank, cols), F32),
+            jax.ShapeDtypeStruct((per, rank, kv), F32),
+        ],
         compiler_params=PARAMS,
         cost_estimate=cost(
             n * groups * rank * cols, 2 * n * groups * rank * cols + 4 * n_tenants * rank * cols
         ),
-    )(tenants, parts)
+    )(tenants, parts, by_slot, *from_up)
 
 
 def input_gradient(pieces, blocks, low, down):
@@ -371,18 +378,15 @@
         RING * per,
         rank,
     )
-    mine, to_below, to_above, to_far = by_slot.reshape(RING, per, rank, kv)
+    _, to_below, to_above, to_far = by_slot.reshape(RING, per, rank, kv)
     from_up = (move(to_below, "col", -1), move(to_above, "col", 1), move(to_far, "col", 2))
 
     blocks = jnp.concatenate(
         [device_at((row + step) % RING, (col + steps) % RING) for step in (0, -1, 1, 2)]
     )
     out = input_gradient((own, from_below, from_above, from_far), blocks, low_next, down_next)
-    out, *from_up = together(out, *from_up)
-    up_grad = sum((block.astype(F32) for block in from_up), mine.astype(F32))
-    up_grad = up_grad * (ADAPTER_SCALE / GROUP_ROWS)
-    out, up_grad, terms = together(out, up_grad, terms)
-    down_grad = sum_by_tenant(terms, tenants, n_tenants)
+    out, terms, *from_up = together(out, terms, *from_up)
+    down_grad, up_grad = owners_sums(terms, tenants, n_tenants, by_slot, from_up)
     return (out[None], jnp.swapaxes(down_grad, 1, 2)[None], up_grad[None])
 
 

time: 203 us -> 203 us (level)
  transfers between devices with their start and end apart: 18 -> 18, of which waited for: 9 -> 9; matrix products, arithmetic and copies ran while one was open for 6% -> 5% of each run, Pallas kernels for 21% -> 21%
where the time goes in v5:
time: 203 us; the launch traced here: 202 us
  waiting for transfers between devices  76 us (37%)
  starting transfers between devices  63 us (31%)
  Pallas kernels  47.4 us (23%)
  local copies, waits for them, and re-layouts  11 us (5%)
  other arithmetic  3.38 us (2%)
    ppermute x13, waiting for transfers between devices, move(): return lax.ppermute(block, ('section', 'dp'), along(axis, distance, down))  60.9 us
    ppermute x13, starting transfers between devices, move(): return lax.ppermute(block, ('section', 'dp'), along(axis, distance, down))  36.5 us
    pallas_call x3, Pallas kernels, frozen_terms(): pl.pallas_call(body, in_specs=[pl.BlockSpec(memory_space=pl.ANY)] * (n_w...  18.8 us
    all_to_all x2, starting transfers between devices, exchange(): return lax.all_to_all(blocks, 'dp', split_axis=0, concat_axis=0, tiled=True)  17.7 us
    ppermute x3, starting transfers between devices, to_previous_section(): return lax.ppermute(block, 'section', [(i, i - 1) for i in range(1, n)])  8.8 us
    pallas_call x1, Pallas kernels, input_gradient(): pl.pallas_call(body, grid_spec=pltpu.PrefetchScalarGridSpec(num_scalar_pr...  8.65 us
    all_to_all x2, waiting for transfers between devices, exchange(): return lax.all_to_all(blocks, 'dp', split_axis=0, concat_axis=0, tiled=True)  8.04 us
    ppermute x3, waiting for transfers between devices, to_previous_section(): return lax.ppermute(block, 'section', [(i, i - 1) for i in range(1, n)])  7.14 us
  transfers between devices with their start and end apart: 18, of which 9 were waited for; matrix products, arithmetic and copies ran while one was open for 5% of the time, Pallas kernels for 21%

profile of v5, /device:TPU:24, one launch (start us, length us, event | category | flops | bytes accessed | tf_op | source)
XLA Modules:
  0.0 202.1 jit_solution(6081406940417332525)
XLA Ops:
  2.2 2.5 %gather_fusion = bf16[48,64,512]{2,1,0:T(8,128)(2,1)} fusion(bf16[32,64,512]{2,1,0:T(8,128)(2,1)S(1)} %bitcast.27, s32[1024]{0:T(1024)S(1)} %pad_clamp_fusion.3), kind=kCustom, calls=%fused_computation | custom fusion | bytes 6291648 | tf_op jit(solution)/shard_map/gather | solution.py:334
  4.8 8.1 %all-to-all-start = ((bf16[16,3,64,512]{3,2,1,0:T(8,128)(2,1)}), bf16[16,3,64,512]{3,2,1,0:T(8,128)(2,1)}, u32[]{:S(2)}, u32[]{:S(2)}) async-start(bf16[16,3,64,512]{3,2,1,0:T(8,128)(2,1)} %bitcast.30), calls=%async_computation | async-start | bytes 6291456 | tf_op jit(solution)/shard_map/all_to_all | solution.py:52
  12.8 1.9 collective-permute-start
  14.8 2.8 %collective-permute-start.4 = (bf16[384,1024]{1,0:T(8,128)(2,1)S(1)}, bf16[384,1024]{1,0:T(8,128)(2,1)}, u32[]{:S(2)}, u32[]{:S(2)}) collective-permute-start(bf16[384,1024]{1,0:T(8,128)(2,1)S(1)} %bitcast.33), channel_id=1, source_target_pairs={{16,0},{32,16},{48,32},{64,48},{80,64},{96,80},{112,96},{17,1},{33... | collective-permute-start | bytes 2359304 | tf_op jit(solution)/shard_map/ppermute | solution.py:29
  17.5 3.2 %collective-permute-start.1 = (bf16[512,1024]{1,0:T(8,128)(2,1)}, bf16[512,1024]{1,0:T(8,128)(2,1)}, u32[]{:S(2)}, u32[]{:S(2)}) collective-permute-start(bf16[512,1024]{1,0:T(8,128)(2,1)} %bitcast.40), channel_id=1, source_target_pairs={{16,4},{17,5},{18,6},{19,7},{20,8},{21,9},{22,10},{23,11},{24,12},... | collective-permute-start | bytes 3145736 | tf_op jit(solution)/shard_map/ppermute | solution.py:48
  20.8 4.7 %collective-permute-start.2 = (bf16[512,1024]{1,0:T(8,128)(2,1)}, bf16[512,1024]{1,0:T(8,128)(2,1)}, u32[]{:S(2)}, u32[]{:S(2)}) collective-permute-start(bf16[512,1024]{1,0:T(8,128)(2,1)} %bitcast.41), channel_id=1, source_target_pairs={{16,12},{17,13},{18,14},{19,15},{20,0},{21,1},{22,2},{23,3},{24,4}... | collective-permute-start | bytes 3145736 | tf_op jit(solution)/shard_map/ppermute | solution.py:48
  25.5 1.8 collective-permute-done.refs_0_
  27.4 3.4 %collective-permute-start.3 = (bf16[512,1024]{1,0:T(8,128)(2,1)}, bf16[512,1024]{1,0:T(8,128)(2,1)}, u32[]{:S(2)}, u32[]{:S(2)}) collective-permute-start(bf16[512,1024]{1,0:T(8,128)(2,1)} %collective-permute-done.refs_0_), channel_id=1, source_target_pairs={{0,8},{1,9},{2,10},{3,11},{4,12},{5,13},{6,14},{7,15},{8,0},{9,1},... | collective-permute-start | bytes 3145736 | tf_op jit(solution)/shard_map/ppermute | solution.py:48
  30.7 4.9 %collective-permute-done.4.refs_4_ = bf16[384,1024]{1,0:T(8,128)(2,1)} collective-permute-done((bf16[384,1024]{1,0:T(8,128)(2,1)S(1)}, bf16[384,1024]{1,0:T(8,128)(2,1)}, u32[]{:S(2)}, u32[]{:S(2)}) %collective-permute-start.4) | collective-permute-done | bytes 786464 | tf_op jit(solution)/shard_map/ppermute | solution.py:29
  35.7 3.1 %collective-permute-start.5 = (bf16[384,1024]{1,0:T(8,128)(2,1)}, bf16[384,1024]{1,0:T(8,128)(2,1)S(1)}, u32[]{:S(2)}, u32[]{:S(2)}) collective-permute-start(bf16[384,1024]{1,0:T(8,128)(2,1)} %collective-permute-done.4.refs_4_), channel_id=1, source_target_pairs={{0,3},{1,0},{2,1},{3,2},{4,7},{5,4},{6,5},{7,6},{8,11},{9,8},{10,9... | collective-permute-start | bytes 2359304 | tf_op jit(solution)/shard_map/ppermute | solution.py:48
  38.8 38.0 %collective-permute-done.1.refs_1_ = bf16[512,1024]{1,0:T(8,128)(2,1)} collective-permute-done((bf16[512,1024]{1,0:T(8,128)(2,1)}, bf16[512,1024]{1,0:T(8,128)(2,1)}, u32[]{:S(2)}, u32[]{:S(2)}) %collective-permute-start.1) | collective-permute-done | bytes 1048608 | tf_op jit(solution)/shard_map/ppermute | solution.py:48
  76.8 4.3 %collective-permute-start.9 = (bf16[384,1024]{1,0:T(8,128)(2,1)}, bf16[384,1024]{1,0:T(8,128)(2,1)}, u32[]{:S(2)}, u32[]{:S(2)}) collective-permute-start(bf16[384,1024]{1,0:T(8,128)(2,1)} %collective-permute-done.4.refs_4_), channel_id=1, source_target_pairs={{0,2},{1,3},{2,0},{3,1},{4,6},{5,7},{6,4},{7,5},{8,10},{9,11},{10,... | collective-permute-start | bytes 2359304 | tf_op jit(solution)/shard_map/ppermute | solution.py:48
  81.1 6.7 %shard_map.103.refs_6_.refs_5_.refs_0_ = bf16[96,2048]{1,0:T(8,128)(2,1)} custom-call(bf16[384,8192]{1,0:T(8,128)(2,1)} %bitcast.28, bf16[16,3,64,512]{3,2,1,0:T(8,128)(2,1)} %all-to-all-done.a_ref, bf16[384,1024]{1,0:T(8,128)(2,1)} %bitcast.32), custom_call_target="tpu_custom_call" | custom-call | flops 402653184 | bytes 9437184 | tf_op jit(solution)/shard_map/pallas_call | solution.py:125
  90.2 7.7 %shard_map.104 = (bf16[480,2048]{1,0:T(8,128)(2,1)}, bf16[480,2048]{1,0:T(8,128)(2,1)}) custom-call(bf16[512,1024]{1,0:T(8,128)(2,1)} %collective-permute-done.refs_0_, bf16[512,1024]{1,0:T(8,128)(2,1)} %collective-permute-done.1.refs_1_, bf16[512,1024]{1,0:T(8,128)(2,1)} %collective-permute-done.2.refs_2_, ...), custom_call_target="tpu_custom_call" | custom-call | flops 4026531840 | bytes 10092544 | tf_op jit(solution)/shard_map/pallas_call | solution.py:185
  97.9 5.8 %collective-permute-start.10 = (bf16[480,2048]{1,0:T(8,128)(2,1)}, bf16[480,2048]{1,0:T(8,128)(2,1)}, u32[]{:S(2)}, u32[]{:S(2)}) collective-permute-start(bf16[480,2048]{1,0:T(8,128)(2,1)} %get-tuple-element.22), channel_id=1, source_target_pairs={{0,1},{1,2},{2,3},{3,0},{4,5},{5,6},{6,7},{7,4},{8,9},{9,10},{10,1... | collective-permute-start | bytes 5898248 | tf_op jit(solution)/shard_map/ppermute | solution.py:48
  103.7 6.1 %shard_map.105 = bf16[480,2048]{1,0:T(8,128)(2,1)} custom-call(bf16[512,1024]{1,0:T(8,128)(2,1)} %collective-permute-done.refs_0_, bf16[512,1024]{1,0:T(8,128)(2,1)} %collective-permute-done.1.refs_1_, bf16[512,1024]{1,0:T(8,128)(2,1)} %collective-permute-done.2.refs_2_, bf16[512,1024]{1,0:T(8,128)(2,1)} %collective-permute-done.3.refs_3_, ...), custom_call_target="tpu_custom_call" | custom-call | flops 2013265920 | bytes 7143424 | tf_op jit(solution)/shard_map/pallas_call | solution.py:185
  109.8 4.5 %collective-permute-start.12 = (bf16[480,2048]{1,0:T(8,128)(2,1)}, bf16[480,2048]{1,0:T(8,128)(2,1)}, u32[]{:S(2)}, u32[]{:S(2)}) collective-permute-start(bf16[480,2048]{1,0:T(8,128)(2,1)} %shard_map.105), channel_id=1, source_target_pairs={{0,2},{1,3},{2,0},{3,1},{4,6},{5,7},{6,4},{7,5},{8,10},{9,11},{10,... | collective-permute-start | bytes 5898248 | tf_op jit(solution)/shard_map/ppermute | solution.py:48
  114.4 2.8 %gather_fusion.1 = bf16[3,64,1024]{2,1,0:T(8,128)(2,1)S(1)} fusion(bf16[32,64,1024]{2,1,0:T(8,128)(2,1)} %bitcast.36, s32[1024]{0:T(1024)S(1)} %pad_clamp_fusion.2), kind=kCustom, calls=%fused_computation.1 | custom fusion | bytes 786444 | tf_op jit(solution)/shard_map/gather | solution.py:339
  117.7 1.9 collective-permute-start.7
  119.6 2.2 %collective-permute-done.7.low_ref = bf16[3,128,64]{2,1,0:T(8,128)(2,1)S(1)} collective-permute-done((bf16[3,128,64]{2,1,0:T(8,128)(2,1)S(1)}, bf16[3,128,64]{2,1,0:T(8,128)(2,1)S(1)}, u32[]{:S(2)}, u32[]{:S(2)}) %collective-permute-start.7) | collective-permute-done | bytes 49184 | tf_op jit(solution)/shard_map/ppermute | solution.py:29
  121.8 4.1 %collective-permute-start.8 = (bf16[16,3,64,512]{3,2,1,0:T(8,128)(2,1)}, bf16[16,3,64,512]{3,2,1,0:T(8,128)(2,1)}, u32[]{:S(2)}, u32[]{:S(2)}) collective-permute-start(bf16[16,3,64,512]{3,2,1,0:T(8,128)(2,1)} %all-to-all-done.a_ref), channel_id=1, source_target_pairs={{16,0},{32,16},{48,32},{64,48},{80,64},{96,80},{112,96},{17,1},{33... | collective-permute-start | bytes 9437192 | tf_op jit(solution)/shard_map/ppermute | solution.py:29
  126.0 5.0 %shard_map.107.refs_0_ = bf16[384,2048]{1,0:T(8,128)(2,1)} custom-call(bf16[512,1024]{1,0:T(8,128)(2,1)} %collective-permute-done.refs_0_, bf16[512,1024]{1,0:T(8,128)(2,1)} %collective-permute-done.1.refs_1_, bf16[512,1024]{1,0:T(8,128)(2,1)} %collective-permute-done.2.refs_2_, bf16[512,1024]{1,0:T(8,128)(2,1)} %collective-permute-done.3.refs_3_, ...), custom_call_target="tpu_custom_call" | custom-call | flops 1610612736 | bytes 6553600 | tf_op jit(solution)/shard_map/pallas_call | solution.py:185
  131.7 5.6 %shard_map.106 = bf16[16,3,64,512]{3,2,1,0:T(8,128)(2,1)} custom-call(bf16[384,8192]{1,0:T(8,128)(2,1)} %bitcast.29, bf16[3,64,128]{2,1,0:T(8,128)(2,1)} %copy.18.low_ref), custom_call_target="tpu_custom_call" | custom-call | flops 402653184 | bytes 9437184 | tf_op jit(solution)/shard_map/pallas_call | solution.py:74
  137.2 12.9 %collective-permute-done.12.refs_3_ = bf16[480,2048]{1,0:T(8,128)(2,1)} collective-permute-done((bf16[480,2048]{1,0:T(8,128)(2,1)}, bf16[480,2048]{1,0:T(8,128)(2,1)}, u32[]{:S(2)}, u32[]{:S(2)}) %collective-permute-start.12) | collective-permute-done | bytes 1966112 | tf_op jit(solution)/shard_map/ppermute | solution.py:48
  150.2 9.7 %all-to-all-start.1 = ((bf16[16,3,64,512]{3,2,1,0:T(8,128)(2,1)}), bf16[16,3,64,512]{3,2,1,0:T(8,128)(2,1)}, u32[]{:S(2)}, u32[]{:S(2)}) async-start(bf16[16,3,64,512]{3,2,1,0:T(8,128)(2,1)} %shard_map.106), calls=%async_computation.1 | async-start | bytes 6291456 | tf_op jit(solution)/shard_map/all_to_all | solution.py:52
  163.9 2.7 %shard_map.109.refs_0_ = bf16[8,64,1024]{2,1,0:T(8,128)(2,1)} custom-call(s32[12]{0:T(128)} %broadcast_select_fusion.6.place_ref, bf16[96,2048]{1,0:T(8,128)(2,1)} %shard_map.103.refs_6_.refs_5_.refs_0_, bf16[480,2048]{1,0:T(8,128)(2,1)} %collective-permute-done.10.refs_1_, bf16[480,2048]{1,0:T(8,128)(2,1)} %collective-permute-done.11.refs_2_, ...), custom_call_target="tpu_custom_call" | custom-call | flops 393216 | bytes 2621440 | tf_op jit(solution)/shard_map/pallas_call | solution.py:227
  167.8 3.1 %collective-permute-start.13 = (bf16[2,64,1024]{2,1,0:T(8,128)(2,1)S(1)}, bf16[2,64,1024]{2,1,0:T(8,128)(2,1)S(1)}, u32[]{:S(2)}, u32[]{:S(2)}) collective-permute-start(bf16[2,64,1024]{2,1,0:T(8,128)(2,1)S(1)} %get-tuple-element.45), channel_id=1, source_target_pairs={{0,12},{1,13},{2,14},{3,15},{4,0},{5,1},{6,2},{7,3},{8,4},{9,5},{1... | collective-permute-start | bytes 786440 | tf_op jit(solution)/shard_map/ppermute | solution.py:48
  170.9 2.3 %collective-permute-start.15 = (bf16[2,64,1024]{2,1,0:T(8,128)(2,1)S(1)}, bf16[2,64,1024]{2,1,0:T(8,128)(2,1)S(1)}, u32[]{:S(2)}, u32[]{:S(2)}) collective-permute-start(bf16[2,64,1024]{2,1,0:T(8,128)(2,1)S(1)} %get-tuple-element.43), channel_id=1, source_target_pairs={{0,8},{1,9},{2,10},{3,11},{4,12},{5,13},{6,14},{7,15},{8,0},{9,1},... | collective-permute-start | bytes 786440 | tf_op jit(solution)/shard_map/ppermute | solution.py:48
  173.8 8.7 %shard_map.108 = bf16[384,8192]{1,0:T(8,128)(2,1)} custom-call(s32[16]{0:T(128)} %pad_add_fusion.b_ref, bf16[3,128,64]{2,1,0:T(8,128)(2,1)} %copy-done.6, bf16[16,3,64,512]{3,2,1,0:T(8,128)(2,1)} %collective-permute-done.8.a_ref, bf16[384,2048]{1,0:T(8,128)(2,1)} %shard_map.107.refs_0_, bf16[480,2048]{1,0:T(8,128)(2,1)} %collective-permute-done.10.refs_1_, ...), custom_call_target="tpu_custom_call" | custom-call | flops 402653184 | bytes 15728640 | tf_op jit(solution)/shard_map/pallas_call | solution.py:293
  184.2 4.9 %collective-permute-done.15.refs_3_ = bf16[2,64,1024]{2,1,0:T(8,128)(2,1)S(1)} collective-permute-done((bf16[2,64,1024]{2,1,0:T(8,128)(2,1)S(1)}, bf16[2,64,1024]{2,1,0:T(8,128)(2,1)S(1)}, u32[]{:S(2)}, u32[]{:S(2)}) %collective-permute-start.15) | collective-permute-done | bytes 262176 | tf_op jit(solution)/shard_map/ppermute | solution.py:48
  189.1 8.0 %all-to-all-done.1.p_ref = bf16[16,3,64,512]{3,2,1,0:T(8,128)(2,1)} async-done(((bf16[16,3,64,512]{3,2,1,0:T(8,128)(2,1)}), bf16[16,3,64,512]{3,2,1,0:T(8,128)(2,1)}, u32[]{:S(2)}, u32[]{:S(2)}) %all-to-all-start.1) | async-done | bytes 3145760 | tf_op jit(solution)/shard_map/all_to_all | solution.py:52
  197.1 5.0 %shard_map.110 = (f32[32,64,512]{2,1,0:T(8,128)}, f32[2,64,1024]{2,1,0:T(8,128)}) custom-call(s32[48]{0:T(128)} %bitcast.37, bf16[16,3,64,512]{3,2,1,0:T(8,128)(2,1)} %all-to-all-done.1.p_ref, bf16[8,64,1024]{2,1,0:T(8,128)(2,1)} %shard_map.109.refs_0_, bf16[2,64,1024]{2,1,0:T(8,128)(2,1)} %copy-done.3, bf16[2,64,1024]{2,1,0:T(8,128)(2,1)} %copy-done.4, ...), custom_call_target="tpu_custom_call" | custom-call | flops 1572864 | bytes 7340032 | tf_op jit(solution)/shard_map/pallas_call | solution.py:258
  (59 shorter events, 12.7 us)
Async XLA Ops:
  0.6 1.6 copy-start
  4.8 10.0 %copy-start.1 = (bf16[1,384,1024]{2,1,0:T(8,128)(2,1)S(1)}, bf16[1,384,1024]{2,1,0:T(8,128)(2,1)}, u32[]{:S(2)}) copy-start(bf16[1,384,1024]{2,1,0:T(8,128)(2,1)} %param.9) | copy-start | bytes 2359300
  4.8 76.4 %all-to-all-start = ((bf16[16,3,64,512]{3,2,1,0:T(8,128)(2,1)}), bf16[16,3,64,512]{3,2,1,0:T(8,128)(2,1)}, u32[]{:S(2)}, u32[]{:S(2)}) async-start(bf16[16,3,64,512]{3,2,1,0:T(8,128)(2,1)} %bitcast.30), calls=%async_computation | async-start | bytes 6291456 | tf_op jit(solution)/shard_map/all_to_all | solution.py:52
  12.8 14.5 %collective-permute-start = (bf16[512,1024]{1,0:T(8,128)(2,1)}, bf16[512,1024]{1,0:T(8,128)(2,1)}, u32[]{:S(2)}, u32[]{:S(2)}) collective-permute-start(bf16[512,1024]{1,0:T(8,128)(2,1)} %bitcast.39), channel_id=1, source_target_pairs={{16,0},{17,1},{18,2},{19,3},{20,4},{21,5},{22,6},{23,7},{24,8},{25... | collective-permute-start | bytes 3145736 | tf_op jit(solution)/shard_map/ppermute | solution.py:48
  14.8 20.9 %collective-permute-start.4 = (bf16[384,1024]{1,0:T(8,128)(2,1)S(1)}, bf16[384,1024]{1,0:T(8,128)(2,1)}, u32[]{:S(2)}, u32[]{:S(2)}) collective-permute-start(bf16[384,1024]{1,0:T(8,128)(2,1)S(1)} %bitcast.33), channel_id=1, source_target_pairs={{16,0},{32,16},{48,32},{64,48},{80,64},{96,80},{112,96},{17,1},{33... | collective-permute-start | bytes 2359304 | tf_op jit(solution)/shard_map/ppermute | solution.py:29
  17.5 59.3 %collective-permute-start.1 = (bf16[512,1024]{1,0:T(8,128)(2,1)}, bf16[512,1024]{1,0:T(8,128)(2,1)}, u32[]{:S(2)}, u32[]{:S(2)}) collective-permute-start(bf16[512,1024]{1,0:T(8,128)(2,1)} %bitcast.40), channel_id=1, source_target_pairs={{16,4},{17,5},{18,6},{19,7},{20,8},{21,9},{22,10},{23,11},{24,12},... | collective-permute-start | bytes 3145736 | tf_op jit(solution)/shard_map/ppermute | solution.py:48
  20.8 67.1 %collective-permute-start.2 = (bf16[512,1024]{1,0:T(8,128)(2,1)}, bf16[512,1024]{1,0:T(8,128)(2,1)}, u32[]{:S(2)}, u32[]{:S(2)}) collective-permute-start(bf16[512,1024]{1,0:T(8,128)(2,1)} %bitcast.41), channel_id=1, source_target_pairs={{16,12},{17,13},{18,14},{19,15},{20,0},{21,1},{22,2},{23,3},{24,4}... | collective-permute-start | bytes 3145736 | tf_op jit(solution)/shard_map/ppermute | solution.py:48
  27.4 61.9 %collective-permute-start.3 = (bf16[512,1024]{1,0:T(8,128)(2,1)}, bf16[512,1024]{1,0:T(8,128)(2,1)}, u32[]{:S(2)}, u32[]{:S(2)}) collective-permute-start(bf16[512,1024]{1,0:T(8,128)(2,1)} %collective-permute-done.refs_0_), channel_id=1, source_target_pairs={{0,8},{1,9},{2,10},{3,11},{4,12},{5,13},{6,14},{7,15},{8,0},{9,1},... | collective-permute-start | bytes 3145736 | tf_op jit(solution)/shard_map/ppermute | solution.py:48
  35.7 53.6 %collective-permute-start.5 = (bf16[384,1024]{1,0:T(8,128)(2,1)}, bf16[384,1024]{1,0:T(8,128)(2,1)S(1)}, u32[]{:S(2)}, u32[]{:S(2)}) collective-permute-start(bf16[384,1024]{1,0:T(8,128)(2,1)} %collective-permute-done.4.refs_4_), channel_id=1, source_target_pairs={{0,3},{1,0},{2,1},{3,2},{4,7},{5,4},{6,5},{7,6},{8,11},{9,8},{10,9... | collective-permute-start | bytes 2359304 | tf_op jit(solution)/shard_map/ppermute | solution.py:48
  38.8 50.5 %collective-permute-start.6 = (bf16[384,1024]{1,0:T(8,128)(2,1)}, bf16[384,1024]{1,0:T(8,128)(2,1)}, u32[]{:S(2)}, u32[]{:S(2)}) collective-permute-start(bf16[384,1024]{1,0:T(8,128)(2,1)} %collective-permute-done.4.refs_4_), channel_id=1, source_target_pairs={{0,1},{1,2},{2,3},{3,0},{4,5},{5,6},{6,7},{7,4},{8,9},{9,10},{10,1... | collective-permute-start | bytes 2359304 | tf_op jit(solution)/shard_map/ppermute | solution.py:48
  76.8 26.8 %collective-permute-start.9 = (bf16[384,1024]{1,0:T(8,128)(2,1)}, bf16[384,1024]{1,0:T(8,128)(2,1)}, u32[]{:S(2)}, u32[]{:S(2)}) collective-permute-start(bf16[384,1024]{1,0:T(8,128)(2,1)} %collective-permute-done.4.refs_4_), channel_id=1, source_target_pairs={{0,2},{1,3},{2,0},{3,1},{4,6},{5,7},{6,4},{7,5},{8,10},{9,11},{10,... | collective-permute-start | bytes 2359304 | tf_op jit(solution)/shard_map/ppermute | solution.py:48
  89.3 0.9 copy-start.10
  97.9 39.4 %collective-permute-start.10 = (bf16[480,2048]{1,0:T(8,128)(2,1)}, bf16[480,2048]{1,0:T(8,128)(2,1)}, u32[]{:S(2)}, u32[]{:S(2)}) collective-permute-start(bf16[480,2048]{1,0:T(8,128)(2,1)} %get-tuple-element.22), channel_id=1, source_target_pairs={{0,1},{1,2},{2,3},{3,0},{4,5},{5,6},{6,7},{7,4},{8,9},{9,10},{10,1... | collective-permute-start | bytes 5898248 | tf_op jit(solution)/shard_map/ppermute | solution.py:48
  103.7 10.7 %copy-start.7 = (s32[1,48]{1,0:T(1,128)S(1)}, s32[1,48]{1,0:T(1,128)}, u32[]{:S(2)}) copy-start(s32[1,48]{1,0:T(1,128)} %param.13) | copy-start | bytes 580
  103.7 13.5 %copy-start.2 = (bf16[1,384,1024]{2,1,0:T(8,128)(2,1)S(1)}, bf16[1,384,1024]{2,1,0:T(8,128)(2,1)}, u32[]{:S(2)}) copy-start(bf16[1,384,1024]{2,1,0:T(8,128)(2,1)} %param.9) | copy-start | bytes 2359300
  103.7 33.6 %collective-permute-start.11 = (bf16[480,2048]{1,0:T(8,128)(2,1)}, bf16[480,2048]{1,0:T(8,128)(2,1)}, u32[]{:S(2)}, u32[]{:S(2)}) collective-permute-start(bf16[480,2048]{1,0:T(8,128)(2,1)} %get-tuple-element.27), channel_id=1, source_target_pairs={{0,3},{1,0},{2,1},{3,2},{4,7},{5,4},{6,5},{7,6},{8,11},{9,8},{10,9... | collective-permute-start | bytes 5898248 | tf_op jit(solution)/shard_map/ppermute | solution.py:48
  109.8 40.4 %collective-permute-start.12 = (bf16[480,2048]{1,0:T(8,128)(2,1)}, bf16[480,2048]{1,0:T(8,128)(2,1)}, u32[]{:S(2)}, u32[]{:S(2)}) collective-permute-start(bf16[480,2048]{1,0:T(8,128)(2,1)} %shard_map.105), channel_id=1, source_target_pairs={{0,2},{1,3},{2,0},{3,1},{4,6},{5,7},{6,4},{7,5},{8,10},{9,11},{10,... | collective-permute-start | bytes 5898248 | tf_op jit(solution)/shard_map/ppermute | solution.py:48
  117.7 4.1 %collective-permute-start.7 = (bf16[3,128,64]{2,1,0:T(8,128)(2,1)S(1)}, bf16[3,128,64]{2,1,0:T(8,128)(2,1)S(1)}, u32[]{:S(2)}, u32[]{:S(2)}) collective-permute-start(bf16[3,128,64]{2,1,0:T(8,128)(2,1)S(1)} %bitcast.35), channel_id=1, source_target_pairs={{16,0},{32,16},{48,32},{64,48},{80,64},{96,80},{112,96},{17,1},{33... | collective-permute-start | bytes 147464 | tf_op jit(solution)/shard_map/ppermute | solution.py:29
  121.8 9.1 %copy-start.6 = (bf16[3,128,64]{2,1,0:T(8,128)(2,1)}, bf16[3,128,64]{2,1,0:T(8,128)(2,1)S(1)}, u32[]{:S(2)}) copy-start(bf16[3,128,64]{2,1,0:T(8,128)(2,1)S(1)} %collective-permute-done.7.low_ref) | copy-start | bytes 147460
  121.8 51.9 %collective-permute-start.8 = (bf16[16,3,64,512]{3,2,1,0:T(8,128)(2,1)}, bf16[16,3,64,512]{3,2,1,0:T(8,128)(2,1)}, u32[]{:S(2)}, u32[]{:S(2)}) collective-permute-start(bf16[16,3,64,512]{3,2,1,0:T(8,128)(2,1)} %all-to-all-done.a_ref), channel_id=1, source_target_pairs={{16,0},{32,16},{48,32},{64,48},{80,64},{96,80},{112,96},{17,1},{33... | collective-permute-start | bytes 9437192 | tf_op jit(solution)/shard_map/ppermute | solution.py:29
  137.2 24.0 %copy-start.9 = (s32[4]{0:T(128)S(1)}, s32[4]{0:T(128)}, u32[]{:S(2)}) copy-start(s32[4]{0:T(128)} %constant.110.clone) | copy-start | bytes 52
  137.2 24.7 %copy-start.8 = (s32[32]{0:T(128)S(1)}, s32[32]{0:T(128)}, u32[]{:S(2)}) copy-start(s32[32]{0:T(128)} %param.14) | copy-start | bytes 388
  150.2 46.9 %all-to-all-start.1 = ((bf16[16,3,64,512]{3,2,1,0:T(8,128)(2,1)}), bf16[16,3,64,512]{3,2,1,0:T(8,128)(2,1)}, u32[]{:S(2)}, u32[]{:S(2)}) async-start(bf16[16,3,64,512]{3,2,1,0:T(8,128)(2,1)} %shard_map.106), calls=%async_computation.1 | async-start | bytes 6291456 | tf_op jit(solution)/shard_map/all_to_all | solution.py:52
  167.8 14.7 %collective-permute-start.13 = (bf16[2,64,1024]{2,1,0:T(8,128)(2,1)S(1)}, bf16[2,64,1024]{2,1,0:T(8,128)(2,1)S(1)}, u32[]{:S(2)}, u32[]{:S(2)}) collective-permute-start(bf16[2,64,1024]{2,1,0:T(8,128)(2,1)S(1)} %get-tuple-element.45), channel_id=1, source_target_pairs={{0,12},{1,13},{2,14},{3,15},{4,0},{5,1},{6,2},{7,3},{8,4},{9,5},{1... | collective-permute-start | bytes 786440 | tf_op jit(solution)/shard_map/ppermute | solution.py:48
  170.9 13.3 %collective-permute-start.14 = (bf16[2,64,1024]{2,1,0:T(8,128)(2,1)S(1)}, bf16[2,64,1024]{2,1,0:T(8,128)(2,1)S(1)}, u32[]{:S(2)}, u32[]{:S(2)}) collective-permute-start(bf16[2,64,1024]{2,1,0:T(8,128)(2,1)S(1)} %get-tuple-element.44), channel_id=1, source_target_pairs={{0,4},{1,5},{2,6},{3,7},{4,8},{5,9},{6,10},{7,11},{8,12},{9,13},{1... | collective-permute-start | bytes 786440 | tf_op jit(solution)/shard_map/ppermute | solution.py:48
  170.9 18.2 %collective-permute-start.15 = (bf16[2,64,1024]{2,1,0:T(8,128)(2,1)S(1)}, bf16[2,64,1024]{2,1,0:T(8,128)(2,1)S(1)}, u32[]{:S(2)}, u32[]{:S(2)}) collective-permute-start(bf16[2,64,1024]{2,1,0:T(8,128)(2,1)S(1)} %get-tuple-element.43), channel_id=1, source_target_pairs={{0,8},{1,9},{2,10},{3,11},{4,12},{5,13},{6,14},{7,15},{8,0},{9,1},... | collective-permute-start | bytes 786440 | tf_op jit(solution)/shard_map/ppermute | solution.py:48
  182.4 14.7 %copy-start.3 = (bf16[2,64,1024]{2,1,0:T(8,128)(2,1)}, bf16[2,64,1024]{2,1,0:T(8,128)(2,1)S(1)}, u32[]{:S(2)}) copy-start(bf16[2,64,1024]{2,1,0:T(8,128)(2,1)S(1)} %collective-permute-done.13.refs_1_) | copy-start | bytes 786436
  184.2 12.9 %copy-start.4 = (bf16[2,64,1024]{2,1,0:T(8,128)(2,1)}, bf16[2,64,1024]{2,1,0:T(8,128)(2,1)S(1)}, u32[]{:S(2)}) copy-start(bf16[2,64,1024]{2,1,0:T(8,128)(2,1)S(1)} %collective-permute-done.14.refs_2_) | copy-start | bytes 786436
  189.1 8.1 %copy-start.5 = (bf16[2,64,1024]{2,1,0:T(8,128)(2,1)}, bf16[2,64,1024]{2,1,0:T(8,128)(2,1)S(1)}, u32[]{:S(2)}) copy-start(bf16[2,64,1024]{2,1,0:T(8,128)(2,1)S(1)} %collective-permute-done.15.refs_3_) | copy-start | bytes 786436

commit v6 on v5

--- a/solution.py
+++ b/solution.py
@@ -344,10 +344,9 @@
     for_above, for_below = frozen_terms((v_above, v_below), weights, parts)
     from_below, from_above = move(for_above, "row", 1), move(for_below, "row", -1)
     (for_far,) = frozen_terms((v_far,), weights, parts)
-    low, for_above = together(low, for_above)
+    down_mine, low, for_above = together(down_mine, low, for_above)
+    down_next = to_previous_section(down_mine)
     low_next = to_previous_section(low)
-    down_mine, low_next = together(down_mine, low_next)
-    down_next = to_previous_section(down_mine)
     from_far = move(for_far, "row", 2)
     low, for_far = together(low, for_far)
     sent = group_terms(x, jnp.swapaxes(low, 1, 2))

time: 203 us -> 203 us (level)
  starting transfers between devices: 63 us -> 60.7 us
    ppermute x3, starting transfers between devices: 8.8 us -> 6.59 us  [to_previous_section(): return lax.ppermute(block, 'section', [(i, i - 1) for i in range(1, n)])]
    ppermute x13, waiting for transfers between devices: 60.9 us -> 63 us  [move(): return lax.ppermute(block, ('section', 'dp'), along(axis, distance, down))]
  transfers between devices with their start and end apart: 18 -> 18, of which waited for: 9 -> 8; matrix products, arithmetic and copies ran while one was open for 5% -> 5% of each run, Pallas kernels for 21% -> 21%
where the time goes in v6:
time: 203 us; the launch traced here: 202 us
  waiting for transfers between devices  77.5 us (38%)
  starting transfers between devices  60.7 us (30%)
  Pallas kernels  47.4 us (23%)
  local copies, waits for them, and re-layouts  11.6 us (6%)
  other arithmetic  3.45 us (2%)
    ppermute x13, waiting for transfers between devices, move(): return lax.ppermute(block, ('section', 'dp'), along(axis, distance, down))  63 us
    ppermute x13, starting transfers between devices, move(): return lax.ppermute(block, ('section', 'dp'), along(axis, distance, down))  36.4 us
    pallas_call x3, Pallas kernels, frozen_terms(): pl.pallas_call(body, in_specs=[pl.BlockSpec(memory_space=pl.ANY)] * (n_w...  18.8 us
    all_to_all x2, starting transfers between devices, exchange(): return lax.all_to_all(blocks, 'dp', split_axis=0, concat_axis=0, tiled=True)  17.8 us
    pallas_call x1, Pallas kernels, input_gradient(): pl.pallas_call(body, grid_spec=pltpu.PrefetchScalarGridSpec(num_scalar_pr...  8.65 us
    all_to_all x2, waiting for transfers between devices, exchange(): return lax.all_to_all(blocks, 'dp', split_axis=0, concat_axis=0, tiled=True)  8.04 us
    pallas_call x1, Pallas kernels, up_parts(): pl.pallas_call(body, grid=(n // WIDE,), in_specs=[pl.BlockSpec((rows, WID...  6.72 us
    ppermute x3, starting transfers between devices, to_previous_section(): return lax.ppermute(block, 'section', [(i, i - 1) for i in range(1, n)])  6.59 us
  transfers between devices with their start and end apart: 18, of which 8 were waited for; matrix products, arithmetic and copies ran while one was open for 5% of the time, Pallas kernels for 21%

profile of v6, /device:TPU:24, one launch (start us, length us, event | category | flops | bytes accessed | tf_op | source)
XLA Modules:
  0.0 202.1 jit_solution(5708625139831971913)
XLA Ops:
  2.2 2.5 %gather_fusion = bf16[48,64,512]{2,1,0:T(8,128)(2,1)} fusion(bf16[32,64,512]{2,1,0:T(8,128)(2,1)S(1)} %bitcast.27, s32[1024]{0:T(1024)S(1)} %pad_clamp_fusion.3), kind=kCustom, calls=%fused_computation | custom fusion | bytes 6291648 | tf_op jit(solution)/shard_map/gather | solution.py:334
  4.8 8.1 %all-to-all-start = ((bf16[16,3,64,512]{3,2,1,0:T(8,128)(2,1)}), bf16[16,3,64,512]{3,2,1,0:T(8,128)(2,1)}, u32[]{:S(2)}, u32[]{:S(2)}) async-start(bf16[16,3,64,512]{3,2,1,0:T(8,128)(2,1)} %bitcast.30), calls=%async_computation | async-start | bytes 6291456 | tf_op jit(solution)/shard_map/all_to_all | solution.py:52
  12.8 1.9 collective-permute-start
  14.8 2.8 %collective-permute-start.4 = (bf16[384,1024]{1,0:T(8,128)(2,1)S(1)}, bf16[384,1024]{1,0:T(8,128)(2,1)}, u32[]{:S(2)}, u32[]{:S(2)}) collective-permute-start(bf16[384,1024]{1,0:T(8,128)(2,1)S(1)} %bitcast.33), channel_id=1, source_target_pairs={{16,0},{32,16},{48,32},{64,48},{80,64},{96,80},{112,96},{17,1},{33... | collective-permute-start | bytes 2359304 | tf_op jit(solution)/shard_map/ppermute | solution.py:29
  17.5 3.2 %collective-permute-start.1 = (bf16[512,1024]{1,0:T(8,128)(2,1)}, bf16[512,1024]{1,0:T(8,128)(2,1)}, u32[]{:S(2)}, u32[]{:S(2)}) collective-permute-start(bf16[512,1024]{1,0:T(8,128)(2,1)} %bitcast.40), channel_id=1, source_target_pairs={{16,4},{17,5},{18,6},{19,7},{20,8},{21,9},{22,10},{23,11},{24,12},... | collective-permute-start | bytes 3145736 | tf_op jit(solution)/shard_map/ppermute | solution.py:48
  20.8 4.7 %collective-permute-start.2 = (bf16[512,1024]{1,0:T(8,128)(2,1)}, bf16[512,1024]{1,0:T(8,128)(2,1)}, u32[]{:S(2)}, u32[]{:S(2)}) collective-permute-start(bf16[512,1024]{1,0:T(8,128)(2,1)} %bitcast.41), channel_id=1, source_target_pairs={{16,12},{17,13},{18,14},{19,15},{20,0},{21,1},{22,2},{23,3},{24,4}... | collective-permute-start | bytes 3145736 | tf_op jit(solution)/shard_map/ppermute | solution.py:48
  25.5 1.8 collective-permute-done.refs_0_
  27.4 3.4 %collective-permute-start.3 = (bf16[512,1024]{1,0:T(8,128)(2,1)}, bf16[512,1024]{1,0:T(8,128)(2,1)}, u32[]{:S(2)}, u32[]{:S(2)}) collective-permute-start(bf16[512,1024]{1,0:T(8,128)(2,1)} %collective-permute-done.refs_0_), channel_id=1, source_target_pairs={{0,8},{1,9},{2,10},{3,11},{4,12},{5,13},{6,14},{7,15},{8,0},{9,1},... | collective-permute-start | bytes 3145736 | tf_op jit(solution)/shard_map/ppermute | solution.py:48
  30.7 4.9 %collective-permute-done.4.refs_4_ = bf16[384,1024]{1,0:T(8,128)(2,1)} collective-permute-done((bf16[384,1024]{1,0:T(8,128)(2,1)S(1)}, bf16[384,1024]{1,0:T(8,128)(2,1)}, u32[]{:S(2)}, u32[]{:S(2)}) %collective-permute-start.4) | collective-permute-done | bytes 786464 | tf_op jit(solution)/shard_map/ppermute | solution.py:29
  35.7 3.1 %collective-permute-start.5 = (bf16[384,1024]{1,0:T(8,128)(2,1)}, bf16[384,1024]{1,0:T(8,128)(2,1)S(1)}, u32[]{:S(2)}, u32[]{:S(2)}) collective-permute-start(bf16[384,1024]{1,0:T(8,128)(2,1)} %collective-permute-done.4.refs_4_), channel_id=1, source_target_pairs={{0,3},{1,0},{2,1},{3,2},{4,7},{5,4},{6,5},{7,6},{8,11},{9,8},{10,9... | collective-permute-start | bytes 2359304 | tf_op jit(solution)/shard_map/ppermute | solution.py:48
  38.8 38.0 %collective-permute-done.1.refs_1_ = bf16[512,1024]{1,0:T(8,128)(2,1)} collective-permute-done((bf16[512,1024]{1,0:T(8,128)(2,1)}, bf16[512,1024]{1,0:T(8,128)(2,1)}, u32[]{:S(2)}, u32[]{:S(2)}) %collective-permute-start.1) | collective-permute-done | bytes 1048608 | tf_op jit(solution)/shard_map/ppermute | solution.py:48
  76.8 4.3 %collective-permute-start.9 = (bf16[384,1024]{1,0:T(8,128)(2,1)}, bf16[384,1024]{1,0:T(8,128)(2,1)}, u32[]{:S(2)}, u32[]{:S(2)}) collective-permute-start(bf16[384,1024]{1,0:T(8,128)(2,1)} %collective-permute-done.4.refs_4_), channel_id=1, source_target_pairs={{0,2},{1,3},{2,0},{3,1},{4,6},{5,7},{6,4},{7,5},{8,10},{9,11},{10,... | collective-permute-start | bytes 2359304 | tf_op jit(solution)/shard_map/ppermute | solution.py:48
  81.1 6.7 %shard_map.103.refs_6_.refs_5_.refs_0_ = bf16[96,2048]{1,0:T(8,128)(2,1)} custom-call(bf16[384,8192]{1,0:T(8,128)(2,1)} %bitcast.28, bf16[16,3,64,512]{3,2,1,0:T(8,128)(2,1)} %all-to-all-done.a_ref, bf16[384,1024]{1,0:T(8,128)(2,1)} %bitcast.32), custom_call_target="tpu_custom_call" | custom-call | flops 402653184 | bytes 9437184 | tf_op jit(solution)/shard_map/pallas_call | solution.py:125
  90.2 7.7 %shard_map.104 = (bf16[480,2048]{1,0:T(8,128)(2,1)}, bf16[480,2048]{1,0:T(8,128)(2,1)}) custom-call(bf16[512,1024]{1,0:T(8,128)(2,1)} %collective-permute-done.refs_0_, bf16[512,1024]{1,0:T(8,128)(2,1)} %collective-permute-done.1.refs_1_, bf16[512,1024]{1,0:T(8,128)(2,1)} %collective-permute-done.2.refs_2_, ...), custom_call_target="tpu_custom_call" | custom-call | flops 4026531840 | bytes 10092544 | tf_op jit(solution)/shard_map/pallas_call | solution.py:185
  97.8 5.8 %collective-permute-start.10 = (bf16[480,2048]{1,0:T(8,128)(2,1)}, bf16[480,2048]{1,0:T(8,128)(2,1)}, u32[]{:S(2)}, u32[]{:S(2)}) collective-permute-start(bf16[480,2048]{1,0:T(8,128)(2,1)} %get-tuple-element.21), channel_id=1, source_target_pairs={{0,1},{1,2},{2,3},{3,0},{4,5},{5,6},{6,7},{7,4},{8,9},{9,10},{10,1... | collective-permute-start | bytes 5898248 | tf_op jit(solution)/shard_map/ppermute | solution.py:48
  103.7 6.1 %shard_map.105 = bf16[480,2048]{1,0:T(8,128)(2,1)} custom-call(bf16[512,1024]{1,0:T(8,128)(2,1)} %collective-permute-done.refs_0_, bf16[512,1024]{1,0:T(8,128)(2,1)} %collective-permute-done.1.refs_1_, bf16[512,1024]{1,0:T(8,128)(2,1)} %collective-permute-done.2.refs_2_, bf16[512,1024]{1,0:T(8,128)(2,1)} %collective-permute-done.3.refs_3_, ...), custom_call_target="tpu_custom_call" | custom-call | flops 2013265920 | bytes 7143424 | tf_op jit(solution)/shard_map/pallas_call | solution.py:185
  109.8 4.5 %collective-permute-start.12 = (bf16[480,2048]{1,0:T(8,128)(2,1)}, bf16[480,2048]{1,0:T(8,128)(2,1)}, u32[]{:S(2)}, u32[]{:S(2)}) collective-permute-start(bf16[480,2048]{1,0:T(8,128)(2,1)} %shard_map.105), channel_id=1, source_target_pairs={{0,2},{1,3},{2,0},{3,1},{4,6},{5,7},{6,4},{7,5},{8,10},{9,11},{10,... | collective-permute-start | bytes 5898248 | tf_op jit(solution)/shard_map/ppermute | solution.py:48
  114.4 2.8 %gather_fusion.1 = bf16[3,64,1024]{2,1,0:T(8,128)(2,1)S(1)} fusion(bf16[32,64,1024]{2,1,0:T(8,128)(2,1)} %bitcast.36, s32[1024]{0:T(1024)S(1)} %pad_clamp_fusion.2), kind=kCustom, calls=%fused_computation.1 | custom fusion | bytes 786444 | tf_op jit(solution)/shard_map/gather | solution.py:339
  117.7 1.9 collective-permute-start.8
  119.6 5.0 %shard_map.107.refs_0_ = bf16[384,2048]{1,0:T(8,128)(2,1)} custom-call(bf16[512,1024]{1,0:T(8,128)(2,1)} %collective-permute-done.refs_0_, bf16[512,1024]{1,0:T(8,128)(2,1)} %collective-permute-done.1.refs_1_, bf16[512,1024]{1,0:T(8,128)(2,1)} %collective-permute-done.2.refs_2_, bf16[512,1024]{1,0:T(8,128)(2,1)} %collective-permute-done.3.refs_3_, ...), custom_call_target="tpu_custom_call" | custom-call | flops 1610612736 | bytes 6553600 | tf_op jit(solution)/shard_map/pallas_call | solution.py:185
  125.3 5.5 %shard_map.106 = bf16[16,3,64,512]{3,2,1,0:T(8,128)(2,1)} custom-call(bf16[384,8192]{1,0:T(8,128)(2,1)} %bitcast.29, bf16[3,64,128]{2,1,0:T(8,128)(2,1)} %copy.18.low_ref), custom_call_target="tpu_custom_call" | custom-call | flops 402653184 | bytes 9437184 | tf_op jit(solution)/shard_map/pallas_call | solution.py:74
  130.9 19.3 %collective-permute-done.12.refs_3_ = bf16[480,2048]{1,0:T(8,128)(2,1)} collective-permute-done((bf16[480,2048]{1,0:T(8,128)(2,1)}, bf16[480,2048]{1,0:T(8,128)(2,1)}, u32[]{:S(2)}, u32[]{:S(2)}) %collective-permute-start.12) | collective-permute-done | bytes 1966112 | tf_op jit(solution)/shard_map/ppermute | solution.py:48
  150.2 9.7 %all-to-all-start.1 = ((bf16[16,3,64,512]{3,2,1,0:T(8,128)(2,1)}), bf16[16,3,64,512]{3,2,1,0:T(8,128)(2,1)}, u32[]{:S(2)}, u32[]{:S(2)}) async-start(bf16[16,3,64,512]{3,2,1,0:T(8,128)(2,1)} %shard_map.106), calls=%async_computation.1 | async-start | bytes 6291456 | tf_op jit(solution)/shard_map/all_to_all | solution.py:52
  163.9 2.7 %shard_map.109.refs_0_ = bf16[8,64,1024]{2,1,0:T(8,128)(2,1)} custom-call(s32[12]{0:T(128)} %broadcast_select_fusion.6.place_ref, bf16[96,2048]{1,0:T(8,128)(2,1)} %shard_map.103.refs_6_.refs_5_.refs_0_, bf16[480,2048]{1,0:T(8,128)(2,1)} %collective-permute-done.10.refs_1_, bf16[480,2048]{1,0:T(8,128)(2,1)} %collective-permute-done.11.refs_2_, ...), custom_call_target="tpu_custom_call" | custom-call | flops 393216 | bytes 2621440 | tf_op jit(solution)/shard_map/pallas_call | solution.py:227
  167.8 3.1 %collective-permute-start.13 = (bf16[2,64,1024]{2,1,0:T(8,128)(2,1)S(1)}, bf16[2,64,1024]{2,1,0:T(8,128)(2,1)S(1)}, u32[]{:S(2)}, u32[]{:S(2)}) collective-permute-start(bf16[2,64,1024]{2,1,0:T(8,128)(2,1)S(1)} %get-tuple-element.43), channel_id=1, source_target_pairs={{0,12},{1,13},{2,14},{3,15},{4,0},{5,1},{6,2},{7,3},{8,4},{9,5},{1... | collective-permute-start | bytes 786440 | tf_op jit(solution)/shard_map/ppermute | solution.py:48
  170.9 2.3 %collective-permute-start.15 = (bf16[2,64,1024]{2,1,0:T(8,128)(2,1)S(1)}, bf16[2,64,1024]{2,1,0:T(8,128)(2,1)S(1)}, u32[]{:S(2)}, u32[]{:S(2)}) collective-permute-start(bf16[2,64,1024]{2,1,0:T(8,128)(2,1)S(1)} %get-tuple-element.41), channel_id=1, source_target_pairs={{0,8},{1,9},{2,10},{3,11},{4,12},{5,13},{6,14},{7,15},{8,0},{9,1},... | collective-permute-start | bytes 786440 | tf_op jit(solution)/shard_map/ppermute | solution.py:48
  173.2 1.9 collective-permute-start.7
  175.8 1.5 collective-permute-done.7.low_ref
  177.9 8.7 %shard_map.108 = bf16[384,8192]{1,0:T(8,128)(2,1)} custom-call(s32[16]{0:T(128)} %pad_add_fusion.b_ref, bf16[3,128,64]{2,1,0:T(8,128)(2,1)} %copy-done.6, bf16[16,3,64,512]{3,2,1,0:T(8,128)(2,1)} %collective-permute-done.8.a_ref, bf16[384,2048]{1,0:T(8,128)(2,1)} %shard_map.107.refs_0_, bf16[480,2048]{1,0:T(8,128)(2,1)} %collective-permute-done.10.refs_1_, ...), custom_call_target="tpu_custom_call" | custom-call | flops 402653184 | bytes 15728640 | tf_op jit(solution)/shard_map/pallas_call | solution.py:293
  186.6 2.4 %collective-permute-done.15.refs_3_ = bf16[2,64,1024]{2,1,0:T(8,128)(2,1)S(1)} collective-permute-done((bf16[2,64,1024]{2,1,0:T(8,128)(2,1)S(1)}, bf16[2,64,1024]{2,1,0:T(8,128)(2,1)S(1)}, u32[]{:S(2)}, u32[]{:S(2)}) %collective-permute-start.15) | collective-permute-done | bytes 262176 | tf_op jit(solution)/shard_map/ppermute | solution.py:48
  189.1 8.0 %all-to-all-done.1.p_ref = bf16[16,3,64,512]{3,2,1,0:T(8,128)(2,1)} async-done(((bf16[16,3,64,512]{3,2,1,0:T(8,128)(2,1)}), bf16[16,3,64,512]{3,2,1,0:T(8,128)(2,1)}, u32[]{:S(2)}, u32[]{:S(2)}) %all-to-all-start.1) | async-done | bytes 3145760 | tf_op jit(solution)/shard_map/all_to_all | solution.py:52
  197.1 5.0 %shard_map.110 = (f32[32,64,512]{2,1,0:T(8,128)}, f32[2,64,1024]{2,1,0:T(8,128)}) custom-call(s32[48]{0:T(128)} %bitcast.37, bf16[16,3,64,512]{3,2,1,0:T(8,128)(2,1)} %all-to-all-done.1.p_ref, bf16[8,64,1024]{2,1,0:T(8,128)(2,1)} %shard_map.109.refs_0_, bf16[2,64,1024]{2,1,0:T(8,128)(2,1)} %copy-done.3, bf16[2,64,1024]{2,1,0:T(8,128)(2,1)} %copy-done.4, ...), custom_call_target="tpu_custom_call" | custom-call | flops 1572864 | bytes 7340032 | tf_op jit(solution)/shard_map/pallas_call | solution.py:258
  (59 shorter events, 11.6 us)
Async XLA Ops:
  0.6 1.6 copy-start
  4.8 10.0 %copy-start.1 = (bf16[1,384,1024]{2,1,0:T(8,128)(2,1)S(1)}, bf16[1,384,1024]{2,1,0:T(8,128)(2,1)}, u32[]{:S(2)}) copy-start(bf16[1,384,1024]{2,1,0:T(8,128)(2,1)} %param.9) | copy-start | bytes 2359300
  4.8 76.4 %all-to-all-start = ((bf16[16,3,64,512]{3,2,1,0:T(8,128)(2,1)}), bf16[16,3,64,512]{3,2,1,0:T(8,128)(2,1)}, u32[]{:S(2)}, u32[]{:S(2)}) async-start(bf16[16,3,64,512]{3,2,1,0:T(8,128)(2,1)} %bitcast.30), calls=%async_computation | async-start | bytes 6291456 | tf_op jit(solution)/shard_map/all_to_all | solution.py:52
  12.8 14.5 %collective-permute-start = (bf16[512,1024]{1,0:T(8,128)(2,1)}, bf16[512,1024]{1,0:T(8,128)(2,1)}, u32[]{:S(2)}, u32[]{:S(2)}) collective-permute-start(bf16[512,1024]{1,0:T(8,128)(2,1)} %bitcast.39), channel_id=1, source_target_pairs={{16,0},{17,1},{18,2},{19,3},{20,4},{21,5},{22,6},{23,7},{24,8},{25... | collective-permute-start | bytes 3145736 | tf_op jit(solution)/shard_map/ppermute | solution.py:48
  14.8 20.9 %collective-permute-start.4 = (bf16[384,1024]{1,0:T(8,128)(2,1)S(1)}, bf16[384,1024]{1,0:T(8,128)(2,1)}, u32[]{:S(2)}, u32[]{:S(2)}) collective-permute-start(bf16[384,1024]{1,0:T(8,128)(2,1)S(1)} %bitcast.33), channel_id=1, source_target_pairs={{16,0},{32,16},{48,32},{64,48},{80,64},{96,80},{112,96},{17,1},{33... | collective-permute-start | bytes 2359304 | tf_op jit(solution)/shard_map/ppermute | solution.py:29
  17.5 59.3 %collective-permute-start.1 = (bf16[512,1024]{1,0:T(8,128)(2,1)}, bf16[512,1024]{1,0:T(8,128)(2,1)}, u32[]{:S(2)}, u32[]{:S(2)}) collective-permute-start(bf16[512,1024]{1,0:T(8,128)(2,1)} %bitcast.40), channel_id=1, source_target_pairs={{16,4},{17,5},{18,6},{19,7},{20,8},{21,9},{22,10},{23,11},{24,12},... | collective-permute-start | bytes 3145736 | tf_op jit(solution)/shard_map/ppermute | solution.py:48
  20.8 67.1 %collective-permute-start.2 = (bf16[512,1024]{1,0:T(8,128)(2,1)}, bf16[512,1024]{1,0:T(8,128)(2,1)}, u32[]{:S(2)}, u32[]{:S(2)}) collective-permute-start(bf16[512,1024]{1,0:T(8,128)(2,1)} %bitcast.41), channel_id=1, source_target_pairs={{16,12},{17,13},{18,14},{19,15},{20,0},{21,1},{22,2},{23,3},{24,4}... | collective-permute-start | bytes 3145736 | tf_op jit(solution)/shard_map/ppermute | solution.py:48
  27.4 61.9 %collective-permute-start.3 = (bf16[512,1024]{1,0:T(8,128)(2,1)}, bf16[512,1024]{1,0:T(8,128)(2,1)}, u32[]{:S(2)}, u32[]{:S(2)}) collective-permute-start(bf16[512,1024]{1,0:T(8,128)(2,1)} %collective-permute-done.refs_0_), channel_id=1, source_target_pairs={{0,8},{1,9},{2,10},{3,11},{4,12},{5,13},{6,14},{7,15},{8,0},{9,1},... | collective-permute-start | bytes 3145736 | tf_op jit(solution)/shard_map/ppermute | solution.py:48
  35.7 53.6 %collective-permute-start.5 = (bf16[384,1024]{1,0:T(8,128)(2,1)}, bf16[384,1024]{1,0:T(8,128)(2,1)S(1)}, u32[]{:S(2)}, u32[]{:S(2)}) collective-permute-start(bf16[384,1024]{1,0:T(8,128)(2,1)} %collective-permute-done.4.refs_4_), channel_id=1, source_target_pairs={{0,3},{1,0},{2,1},{3,2},{4,7},{5,4},{6,5},{7,6},{8,11},{9,8},{10,9... | collective-permute-start | bytes 2359304 | tf_op jit(solution)/shard_map/ppermute | solution.py:48
  38.8 50.5 %collective-permute-start.6 = (bf16[384,1024]{1,0:T(8,128)(2,1)}, bf16[384,1024]{1,0:T(8,128)(2,1)}, u32[]{:S(2)}, u32[]{:S(2)}) collective-permute-start(bf16[384,1024]{1,0:T(8,128)(2,1)} %collective-permute-done.4.refs_4_), channel_id=1, source_target_pairs={{0,1},{1,2},{2,3},{3,0},{4,5},{5,6},{6,7},{7,4},{8,9},{9,10},{10,1... | collective-permute-start | bytes 2359304 | tf_op jit(solution)/shard_map/ppermute | solution.py:48
  76.8 26.8 %collective-permute-start.9 = (bf16[384,1024]{1,0:T(8,128)(2,1)}, bf16[384,1024]{1,0:T(8,128)(2,1)}, u32[]{:S(2)}, u32[]{:S(2)}) collective-permute-start(bf16[384,1024]{1,0:T(8,128)(2,1)} %collective-permute-done.4.refs_4_), channel_id=1, source_target_pairs={{0,2},{1,3},{2,0},{3,1},{4,6},{5,7},{6,4},{7,5},{8,10},{9,11},{10,... | collective-permute-start | bytes 2359304 | tf_op jit(solution)/shard_map/ppermute | solution.py:48
  89.3 0.9 copy-start.10
  97.8 33.0 %collective-permute-start.10 = (bf16[480,2048]{1,0:T(8,128)(2,1)}, bf16[480,2048]{1,0:T(8,128)(2,1)}, u32[]{:S(2)}, u32[]{:S(2)}) collective-permute-start(bf16[480,2048]{1,0:T(8,128)(2,1)} %get-tuple-element.21), channel_id=1, source_target_pairs={{0,1},{1,2},{2,3},{3,0},{4,5},{5,6},{6,7},{7,4},{8,9},{9,10},{10,1... | collective-permute-start | bytes 5898248 | tf_op jit(solution)/shard_map/ppermute | solution.py:48
  103.6 10.7 %copy-start.7 = (s32[1,48]{1,0:T(1,128)S(1)}, s32[1,48]{1,0:T(1,128)}, u32[]{:S(2)}) copy-start(s32[1,48]{1,0:T(1,128)} %param.13) | copy-start | bytes 580
  103.6 13.5 %copy-start.2 = (bf16[1,384,1024]{2,1,0:T(8,128)(2,1)S(1)}, bf16[1,384,1024]{2,1,0:T(8,128)(2,1)}, u32[]{:S(2)}) copy-start(bf16[1,384,1024]{2,1,0:T(8,128)(2,1)} %param.9) | copy-start | bytes 2359300
  103.6 27.2 %collective-permute-start.11 = (bf16[480,2048]{1,0:T(8,128)(2,1)}, bf16[480,2048]{1,0:T(8,128)(2,1)}, u32[]{:S(2)}, u32[]{:S(2)}) collective-permute-start(bf16[480,2048]{1,0:T(8,128)(2,1)} %get-tuple-element.25), channel_id=1, source_target_pairs={{0,3},{1,0},{2,1},{3,2},{4,7},{5,4},{6,5},{7,6},{8,11},{9,8},{10,9... | collective-permute-start | bytes 5898248 | tf_op jit(solution)/shard_map/ppermute | solution.py:48
  109.8 40.4 %collective-permute-start.12 = (bf16[480,2048]{1,0:T(8,128)(2,1)}, bf16[480,2048]{1,0:T(8,128)(2,1)}, u32[]{:S(2)}, u32[]{:S(2)}) collective-permute-start(bf16[480,2048]{1,0:T(8,128)(2,1)} %shard_map.105), channel_id=1, source_target_pairs={{0,2},{1,3},{2,0},{3,1},{4,6},{5,7},{6,4},{7,5},{8,10},{9,11},{10,... | collective-permute-start | bytes 5898248 | tf_op jit(solution)/shard_map/ppermute | solution.py:48
  117.7 59.6 %collective-permute-start.8 = (bf16[16,3,64,512]{3,2,1,0:T(8,128)(2,1)}, bf16[16,3,64,512]{3,2,1,0:T(8,128)(2,1)}, u32[]{:S(2)}, u32[]{:S(2)}) collective-permute-start(bf16[16,3,64,512]{3,2,1,0:T(8,128)(2,1)} %all-to-all-done.a_ref), channel_id=1, source_target_pairs={{16,0},{32,16},{48,32},{64,48},{80,64},{96,80},{112,96},{17,1},{33... | collective-permute-start | bytes 9437192 | tf_op jit(solution)/shard_map/ppermute | solution.py:29
  130.9 30.4 %copy-start.9 = (s32[4]{0:T(128)S(1)}, s32[4]{0:T(128)}, u32[]{:S(2)}) copy-start(s32[4]{0:T(128)} %constant.110.clone) | copy-start | bytes 52
  130.9 31.0 %copy-start.8 = (s32[32]{0:T(128)S(1)}, s32[32]{0:T(128)}, u32[]{:S(2)}) copy-start(s32[32]{0:T(128)} %param.14) | copy-start | bytes 388
  150.2 46.9 %all-to-all-start.1 = ((bf16[16,3,64,512]{3,2,1,0:T(8,128)(2,1)}), bf16[16,3,64,512]{3,2,1,0:T(8,128)(2,1)}, u32[]{:S(2)}, u32[]{:S(2)}) async-start(bf16[16,3,64,512]{3,2,1,0:T(8,128)(2,1)} %shard_map.106), calls=%async_computation.1 | async-start | bytes 6291456 | tf_op jit(solution)/shard_map/all_to_all | solution.py:52
  167.8 18.8 %collective-permute-start.13 = (bf16[2,64,1024]{2,1,0:T(8,128)(2,1)S(1)}, bf16[2,64,1024]{2,1,0:T(8,128)(2,1)S(1)}, u32[]{:S(2)}, u32[]{:S(2)}) collective-permute-start(bf16[2,64,1024]{2,1,0:T(8,128)(2,1)S(1)} %get-tuple-element.43), channel_id=1, source_target_pairs={{0,12},{1,13},{2,14},{3,15},{4,0},{5,1},{6,2},{7,3},{8,4},{9,5},{1... | collective-permute-start | bytes 786440 | tf_op jit(solution)/shard_map/ppermute | solution.py:48
  170.9 15.7 %collective-permute-start.14 = (bf16[2,64,1024]{2,1,0:T(8,128)(2,1)S(1)}, bf16[2,64,1024]{2,1,0:T(8,128)(2,1)S(1)}, u32[]{:S(2)}, u32[]{:S(2)}) collective-permute-start(bf16[2,64,1024]{2,1,0:T(8,128)(2,1)S(1)} %get-tuple-element.42), channel_id=1, source_target_pairs={{0,4},{1,5},{2,6},{3,7},{4,8},{5,9},{6,10},{7,11},{8,12},{9,13},{1... | collective-permute-start | bytes 786440 | tf_op jit(solution)/shard_map/ppermute | solution.py:48
  170.9 18.2 %collective-permute-start.15 = (bf16[2,64,1024]{2,1,0:T(8,128)(2,1)S(1)}, bf16[2,64,1024]{2,1,0:T(8,128)(2,1)S(1)}, u32[]{:S(2)}, u32[]{:S(2)}) collective-permute-start(bf16[2,64,1024]{2,1,0:T(8,128)(2,1)S(1)} %get-tuple-element.41), channel_id=1, source_target_pairs={{0,8},{1,9},{2,10},{3,11},{4,12},{5,13},{6,14},{7,15},{8,0},{9,1},... | collective-permute-start | bytes 786440 | tf_op jit(solution)/shard_map/ppermute | solution.py:48
  173.2 4.1 %collective-permute-start.7 = (bf16[3,128,64]{2,1,0:T(8,128)(2,1)S(1)}, bf16[3,128,64]{2,1,0:T(8,128)(2,1)S(1)}, u32[]{:S(2)}, u32[]{:S(2)}) collective-permute-start(bf16[3,128,64]{2,1,0:T(8,128)(2,1)S(1)} %bitcast.35), channel_id=1, source_target_pairs={{16,0},{32,16},{48,32},{64,48},{80,64},{96,80},{112,96},{17,1},{33... | collective-permute-start | bytes 147464 | tf_op jit(solution)/shard_map/ppermute | solution.py:29
  177.3 0.6 copy-start.6
  186.6 10.5 %copy-start.3 = (bf16[2,64,1024]{2,1,0:T(8,128)(2,1)}, bf16[2,64,1024]{2,1,0:T(8,128)(2,1)S(1)}, u32[]{:S(2)}) copy-start(bf16[2,64,1024]{2,1,0:T(8,128)(2,1)S(1)} %collective-permute-done.13.refs_1_) | copy-start | bytes 786436
  186.6 10.5 %copy-start.4 = (bf16[2,64,1024]{2,1,0:T(8,128)(2,1)}, bf16[2,64,1024]{2,1,0:T(8,128)(2,1)S(1)}, u32[]{:S(2)}) copy-start(bf16[2,64,1024]{2,1,0:T(8,128)(2,1)S(1)} %collective-permute-done.14.refs_2_) | copy-start | bytes 786436
  189.0 8.0 %copy-start.5 = (bf16[2,64,1024]{2,1,0:T(8,128)(2,1)}, bf16[2,64,1024]{2,1,0:T(8,128)(2,1)S(1)}, u32[]{:S(2)}) copy-start(bf16[2,64,1024]{2,1,0:T(8,128)(2,1)S(1)} %collective-permute-done.15.refs_3_) | copy-start | bytes 786436
